TPU v7x, 32 devices: a whole 2x2x4 slice. The times are simulated.
32 devices in a mesh: batch: 4 (over y, x), tensor: 8 (over z, core).
Axes of the slice: x: 2, y: 2, z: 4, core: 2. Of those that a mesh axis runs over, the one named last changes fastest.
Arguments:
- tokens: bfloat16 [8, 1024, 2048], P('batch', 'tensor'), may hold values from -6 to 6
- cotangent: bfloat16 [8, 1024, 2048], P('batch', 'tensor'), may hold values from -6 to 6
- segment_ids: int32 [8, 1024], P('batch'), may hold values from 0 to 3, as said below
- prefix_lengths: int32 [8, 4], P('batch'), may hold values from 1 to 1021, as said below
- rotary_positions: int32 [8, 1024], P('batch'), may hold values from 0 to 1023, as said below
- residual_scale: float32 [1], replicated, may hold values from 1.2 to 2
- qkv_weight: bfloat16 [2048, 3, 2048], P(None, None, 'tensor'), may hold values from -0.125 to 0.125
- qkv_bias: float32 [3, 2048], P(None, 'tensor'), may hold values from -0.625 to 0.625
- out_weight: bfloat16 [2048, 2048], P('tensor'), may hold values from -1 to 1
- out_bias: float32 [2048], replicated, may hold values from -1.25 to 1.25
- norm_gain: float32 [2048], replicated, may hold values from 0.5 to 1.5
- norm_shift: float32 [2048], replicated, may hold values from -1.25 to 1.25
- gate_weight: bfloat16 [2048, 5504], P(None, 'tensor'), may hold values from -0.125 to 0.125
- gate_bias: float32 [5504], P('tensor'), may hold values from -1.75 to 1.75
- up_weight: bfloat16 [2048, 5504], P(None, 'tensor'), may hold values from -0.125 to 0.125
- up_bias: float32 [5504], P('tensor'), may hold values from -1.75 to 1.75
- down_weight: bfloat16 [5504, 2048], P('tensor'), may hold values from -0.078125 to 0.078125
- down_bias: float32 [2048], replicated, may hold values from -1.25 to 1.25
- final_gain: float32 [2048], replicated, may hold values from 0.5 to 1.5
- final_shift: float32 [2048], replicated, may hold values from -1.25 to 1.25
Outputs:
- block_output: bfloat16 [8, 1024, 2048], P('batch', 'tensor')
- tokens_grad: float32 [8, 1024, 2048], P('batch', 'tensor')
- qkv_weight_grad: float32 [2048, 3, 2048], P(None, None, 'tensor')
- qkv_bias_grad: float32 [3, 2048], P(None, 'tensor')
- out_weight_grad: float32 [2048, 2048], P('tensor')
- out_bias_grad: float32 [2048], replicated
- norm_gain_grad: float32 [2048], replicated
- norm_shift_grad: float32 [2048], replicated
- gate_weight_grad: float32 [2048, 5504], P(None, 'tensor')
- gate_bias_grad: float32 [5504], P('tensor')
- up_weight_grad: float32 [2048, 5504], P(None, 'tensor')
- up_bias_grad: float32 [5504], P('tensor')
- down_weight_grad: float32 [5504, 2048], P('tensor')
- down_bias_grad: float32 [2048], replicated
- final_gain_grad: float32 [2048], replicated
- final_shift_grad: float32 [2048], replicated
Inputs may be any that keep to these rules, and one draw needn't show every extreme that they name: `segment_ids`: along each pack the ids never fall, and each of 0 to 3 appears. prefix_lengths[p, s] lies between 1 and the number of positions of segment s in pack p. `rotary_positions`: within a segment the positions rise by one from each position to the next.
All inputs are finite; a program needn't handle non-finite values.
Results may differ from a plain program's by a relative error of at most 0.019.
Values may be sent and summed in bfloat16 or wider, within the bound.
No kernel may reach another device: no remote copies, remote signals or barrier semaphores. Data moves between devices by JAX's collectives and lax.ppermute only.
A program may use at most 256 MiB of HBM per device.

v0:
```python
import math

import jax
import jax.numpy as jnp
from jax import lax
from jax.sharding import PartitionSpec as P

FF_LIVE = 5461
SEGS = 4
HEAD_DIM = 128


EPSILON = 1e-05
NEG_FILL = -1e30
ROPE_BASE = 10000.0
GELU_ROOT = math.sqrt(2.0 / math.pi)
GELU_CUBIC = 0.044715


def gelu_value(values):
    return (
        0.5
        * values
        * (1.0 + jnp.tanh(GELU_ROOT * (values + GELU_CUBIC * values * values * values)))
    )


def gelu_slope(values):
    squared = values * values
    tangent = jnp.tanh(GELU_ROOT * values * (1.0 + GELU_CUBIC * squared))
    return 0.5 * (1.0 + tangent) + 0.5 * values * (1.0 - tangent * tangent) * GELU_ROOT * (
        1.0 + 3.0 * GELU_CUBIC * squared
    )


def norm_forward(values, gain_vector, shift_vector):
    average = jnp.mean(values, axis=-1, keepdims=True)
    centred = values - average
    spread = jnp.mean(centred * centred, axis=-1, keepdims=True)
    inverse = lax.rsqrt(spread + EPSILON)
    normal = centred * inverse
    return (normal * gain_vector + shift_vector, normal, inverse)


def norm_backward(grad_rows, gain_vector, normal, inverse):
    scaled = grad_rows * gain_vector
    return inverse * (
        scaled
        - jnp.mean(scaled, axis=-1, keepdims=True)
        - normal * jnp.mean(scaled * normal, axis=-1, keepdims=True)
    )


def rotary_tables(positions):
    half_dim = HEAD_DIM // 2
    frequency = jnp.exp(
        jnp.arange(half_dim, dtype=jnp.float32) * (-2.0 * math.log(ROPE_BASE) / HEAD_DIM)
    )
    angles = positions.astype(jnp.float32)[:, None] * frequency[None, :]
    angles = jnp.concatenate([angles, angles], axis=-1)
    return (jnp.cos(angles), jnp.sin(angles))


def rotate_heads(values, cosine, sine_table):
    half_dim = values.shape[-1] // 2
    turned = jnp.concatenate([-values[..., half_dim:], values[..., :half_dim]], axis=-1)
    return values * cosine + turned * sine_table


def rotate_back(grads, cosine, sine_table):
    half_dim = grads.shape[-1] // 2
    moved = grads * sine_table
    return grads * cosine + jnp.concatenate(
        [moved[..., half_dim:], -moved[..., :half_dim]], axis=-1
    )


def attend_mask(segment, prefix):
    seg_slots = jnp.arange(SEGS, dtype=jnp.int32)
    member = (segment[:, None] == seg_slots[None, :]).astype(jnp.int32)
    counts = jnp.sum(member, axis=0)
    starts = jnp.cumsum(counts) - counts
    ordinal = jnp.arange(segment.shape[0], dtype=jnp.int32)
    offset = ordinal - jnp.sum(member * starts[None, :], axis=1)
    in_prefix = offset < jnp.sum(member * prefix[None, :], axis=1)
    same_doc = segment[:, None] == segment[None, :]
    return same_doc & (in_prefix[None, :] | (ordinal[None, :] <= ordinal[:, None]))


def add_trees(running, addend):
    return jax.tree.map(lambda left_part, right_part: left_part + right_part, running, addend)


def per_device(
    tokens,
    cotangent,
    segment_ids,
    prefix_lengths,
    rotary_positions,
    residual_scale,
    qkv_weight,
    qkv_bias,
    out_weight,
    out_bias,
    norm_gain,
    norm_shift,
    gate_weight,
    gate_bias,
    up_weight,
    up_bias,
    down_weight,
    down_bias,
    final_gain,
    final_shift,
):
    pack_count, local_rows, model_width = tokens.shape
    seq_len = segment_ids.shape[1]
    head_width = qkv_weight.shape[2]
    local_heads = head_width // HEAD_DIM
    ff_local = gate_weight.shape[1]
    tensor_rank = lax.axis_index("tensor")
    live_cols = (tensor_rank * ff_local + jnp.arange(ff_local, dtype=jnp.int32) < FF_LIVE).astype(
        jnp.float32
    )
    live_low = live_cols.astype(jnp.bfloat16)
    gate_live = gate_weight * live_low[None, :]
    up_live = up_weight * live_low[None, :]
    down_live = down_weight * live_low[:, None]
    gate_shift = gate_bias * live_cols
    up_shift = up_bias * live_cols
    qkv_flat = qkv_weight.reshape(model_width, 3 * head_width)
    scale_value = residual_scale[0]
    block_rows = 512
    block_count = seq_len // block_rows
    factor = 1.0 / math.sqrt(HEAD_DIM)
    whole_out = lax.all_gather(out_weight, "tensor", axis=0, tiled=True)
    outputs = []
    input_grads = []
    column_total = None
    shared_total = None
    out_total = None
    for pack_index in range(pack_count):
        local_tokens = tokens[pack_index]
        whole_tokens = lax.all_gather(local_tokens, "tensor", axis=0, tiled=True)
        allowed = attend_mask(segment_ids[pack_index], prefix_lengths[pack_index])
        cosine, sine_table = rotary_tables(rotary_positions[pack_index])
        cos_heads = cosine[:, None, :]
        sin_heads = sine_table[:, None, :]
        projected = jnp.dot(whole_tokens, qkv_flat, preferred_element_type=jnp.float32).reshape(
            seq_len, 3, local_heads, HEAD_DIM
        )
        projected = projected + qkv_bias.reshape(1, 3, local_heads, HEAD_DIM)
        queries = rotate_heads(projected[:, 0], cos_heads, sin_heads).astype(jnp.bfloat16)
        keys_all = rotate_heads(projected[:, 1], cos_heads, sin_heads).astype(jnp.bfloat16)
        values_all = projected[:, 2].astype(jnp.bfloat16)

        def forward_block(block_index):
            first_row = block_index * block_rows
            query_block = lax.dynamic_slice_in_dim(queries, first_row, block_rows, 0)
            mask_block = lax.dynamic_slice_in_dim(allowed, first_row, block_rows, 0)
            scores = (
                jnp.einsum(
                    "qhd,khd->hqk", query_block, keys_all, preferred_element_type=jnp.float32
                )
                * factor
            )
            scores = jnp.where(mask_block[None], scores, NEG_FILL)
            row_top = jnp.max(scores, axis=-1, keepdims=True)
            shifted = jnp.exp(scores - row_top)
            row_total = jnp.sum(shifted, axis=-1, keepdims=True)
            probs_low = (shifted / row_total).astype(jnp.bfloat16)
            block_context = jnp.einsum(
                "hqk,khd->qhd", probs_low, values_all, preferred_element_type=jnp.float32
            )
            return (block_context, (row_top + jnp.log(row_total))[..., 0])

        contexts, log_sums = lax.map(forward_block, jnp.arange(block_count))
        context = contexts.reshape(seq_len, head_width).astype(jnp.bfloat16)
        context_rows = lax.all_to_all(context, "tensor", split_axis=0, concat_axis=1, tiled=True)
        attended = jnp.dot(context_rows, whole_out, preferred_element_type=jnp.float32) + out_bias
        normed, normal_one, inverse_one = norm_forward(
            scale_value * local_tokens.astype(jnp.float32) + attended, norm_gain, norm_shift
        )
        hidden_local = normed.astype(jnp.bfloat16)
        whole_hidden = lax.all_gather(hidden_local, "tensor", axis=0, tiled=True)
        gate_pre = jnp.dot(whole_hidden, gate_live, preferred_element_type=jnp.float32) + gate_shift
        up_pre = jnp.dot(whole_hidden, up_live, preferred_element_type=jnp.float32) + up_shift
        gelu_gate = gelu_value(gate_pre)
        activated = (gelu_gate * up_pre).astype(jnp.bfloat16)
        branch = (
            lax.psum_scatter(
                jnp.dot(activated, down_live, preferred_element_type=jnp.float32).astype(
                    jnp.bfloat16
                ),
                "tensor",
                scatter_dimension=0,
                tiled=True,
            ).astype(jnp.float32)
            + down_bias
        )
        final_rows, normal_two, inverse_two = norm_forward(
            scale_value * normed + branch, final_gain, final_shift
        )
        outputs.append(final_rows.astype(jnp.bfloat16))
        grad_final = cotangent[pack_index].astype(jnp.float32)
        final_gain_part = jnp.sum(grad_final * normal_two, axis=0)
        final_shift_part = jnp.sum(grad_final, axis=0)
        grad_two = norm_backward(grad_final, final_gain, normal_two, inverse_two)
        down_bias_part = jnp.sum(grad_two, axis=0)
        branch_grad = lax.all_gather(grad_two.astype(jnp.bfloat16), "tensor", axis=0, tiled=True)
        down_weight_part = (
            jnp.einsum("nf,nd->fd", activated, branch_grad, preferred_element_type=jnp.float32)
            * live_cols[:, None]
        )
        activated_grad = jnp.einsum(
            "nd,fd->nf", branch_grad, down_live, preferred_element_type=jnp.float32
        )
        up_grad = activated_grad * gelu_gate
        gate_grad = activated_grad * up_pre * gelu_slope(gate_pre)
        gate_bias_part = jnp.sum(gate_grad, axis=0) * live_cols
        up_bias_part = jnp.sum(up_grad, axis=0) * live_cols
        gate_low = gate_grad.astype(jnp.bfloat16)
        up_low = up_grad.astype(jnp.bfloat16)
        gate_weight_part = (
            jnp.einsum("nd,nf->df", whole_hidden, gate_low, preferred_element_type=jnp.float32)
            * live_cols[None, :]
        )
        up_weight_part = (
            jnp.einsum("nd,nf->df", whole_hidden, up_low, preferred_element_type=jnp.float32)
            * live_cols[None, :]
        )
        normed_grad = (
            lax.psum_scatter(
                jnp.einsum("nf,df->nd", gate_low, gate_live, preferred_element_type=jnp.float32)
                + jnp.einsum("nf,df->nd", up_low, up_live, preferred_element_type=jnp.float32),
                "tensor",
                scatter_dimension=0,
                tiled=True,
            )
            + scale_value * grad_two
        )
        norm_gain_part = jnp.sum(normed_grad * normal_one, axis=0)
        norm_shift_part = jnp.sum(normed_grad, axis=0)
        grad_one = norm_backward(normed_grad, norm_gain, normal_one, inverse_one)
        out_bias_part = jnp.sum(grad_one, axis=0)
        attended_low = grad_one.astype(jnp.bfloat16)
        out_weight_part = jnp.einsum(
            "nc,nd->cd", context_rows, attended_low, preferred_element_type=jnp.float32
        )
        row_context_grad = jnp.einsum(
            "nd,cd->nc", attended_low, whole_out, preferred_element_type=jnp.float32
        ).astype(jnp.bfloat16)
        context_grad = lax.all_to_all(
            row_context_grad, "tensor", split_axis=1, concat_axis=0, tiled=True
        )
        context_grad = context_grad.reshape(seq_len, local_heads, HEAD_DIM)

        def backward_block(totals_in, block_index):
            key_total, value_total = totals_in
            first_row = block_index * block_rows
            query_block = lax.dynamic_slice_in_dim(queries, first_row, block_rows, 0)
            mask_block = lax.dynamic_slice_in_dim(allowed, first_row, block_rows, 0)
            grad_block = lax.dynamic_slice_in_dim(context_grad, first_row, block_rows, 0)
            log_block = log_sums[block_index]
            scores = (
                jnp.einsum(
                    "qhd,khd->hqk", query_block, keys_all, preferred_element_type=jnp.float32
                )
                * factor
            )
            scores = jnp.where(mask_block[None], scores, NEG_FILL)
            attention_probs = jnp.exp(scores - log_block[..., None])
            probs_low = attention_probs.astype(jnp.bfloat16)
            probs_grad = jnp.einsum(
                "qhd,khd->hqk", grad_block, values_all, preferred_element_type=jnp.float32
            )
            row_delta = jnp.sum(attention_probs * probs_grad, axis=-1, keepdims=True)
            score_grad = (attention_probs * (probs_grad - row_delta)).astype(jnp.bfloat16)
            query_grad = (
                jnp.einsum("hqk,khd->qhd", score_grad, keys_all, preferred_element_type=jnp.float32)
                * factor
            )
            key_total = (
                key_total
                + jnp.einsum(
                    "hqk,qhd->khd", score_grad, query_block, preferred_element_type=jnp.float32
                )
                * factor
            )
            value_total = value_total + jnp.einsum(
                "hqk,qhd->khd", probs_low, grad_block, preferred_element_type=jnp.float32
            )
            return ((key_total, value_total), query_grad)

        empty_heads = jnp.zeros((seq_len, local_heads, HEAD_DIM), jnp.float32)
        (key_grad, value_grad), query_grads = lax.scan(
            backward_block, (empty_heads, empty_heads), jnp.arange(block_count)
        )
        query_grad = query_grads.reshape(seq_len, local_heads, HEAD_DIM)
        projected_grad = jnp.stack(
            [
                rotate_back(query_grad, cos_heads, sin_heads),
                rotate_back(key_grad, cos_heads, sin_heads),
                value_grad,
            ],
            axis=1,
        )
        projected_grad = projected_grad.reshape(seq_len, 3 * head_width)
        qkv_bias_part = jnp.sum(projected_grad, axis=0)
        projected_low = projected_grad.astype(jnp.bfloat16)
        qkv_weight_part = jnp.einsum(
            "nd,nc->dc", whole_tokens, projected_low, preferred_element_type=jnp.float32
        )
        input_grad = (
            lax.psum_scatter(
                jnp.einsum(
                    "nc,dc->nd", projected_low, qkv_flat, preferred_element_type=jnp.float32
                ).astype(jnp.bfloat16),
                "tensor",
                scatter_dimension=0,
                tiled=True,
            ).astype(jnp.float32)
            + scale_value * grad_one
        )
        input_grads.append(input_grad)
        column_parts = (
            qkv_weight_part,
            qkv_bias_part,
            gate_weight_part,
            gate_bias_part,
            up_weight_part,
            up_bias_part,
            down_weight_part,
        )
        shared_parts = (
            out_bias_part,
            norm_gain_part,
            norm_shift_part,
            down_bias_part,
            final_gain_part,
            final_shift_part,
        )
        column_total = (
            column_parts if column_total is None else add_trees(column_total, column_parts)
        )
        shared_total = (
            shared_parts if shared_total is None else add_trees(shared_total, shared_parts)
        )
        out_total = out_weight_part if out_total is None else out_total + out_weight_part
    out_total = lax.psum_scatter(
        out_total.astype(jnp.bfloat16), "tensor", scatter_dimension=0, tiled=True
    ).astype(jnp.float32)
    summed = (
        lax.psum(column_total[0].astype(jnp.bfloat16), "batch").astype(jnp.float32),
        lax.psum(column_total[1].astype(jnp.bfloat16), "batch").astype(jnp.float32),
        lax.psum(out_total.astype(jnp.bfloat16), "batch").astype(jnp.float32),
        lax.psum(column_total[2].astype(jnp.bfloat16), "batch").astype(jnp.float32),
        lax.psum(column_total[3].astype(jnp.bfloat16), "batch").astype(jnp.float32),
        lax.psum(column_total[4].astype(jnp.bfloat16), "batch").astype(jnp.float32),
        lax.psum(column_total[5].astype(jnp.bfloat16), "batch").astype(jnp.float32),
        lax.psum(column_total[6].astype(jnp.bfloat16), "batch").astype(jnp.float32),
    )
    shared_total = lax.psum(
        (
            shared_total[0],
            shared_total[1],
            shared_total[2],
            shared_total[3],
            shared_total[4],
            shared_total[5],
        ),
        ("batch", "tensor"),
    )
    return (
        jnp.stack(outputs),
        jnp.stack(input_grads),
        summed[0].reshape(model_width, 3, head_width),
        summed[1].reshape(3, head_width),
        summed[2],
        shared_total[0],
        shared_total[1],
        shared_total[2],
        summed[3],
        summed[4],
        summed[5],
        summed[6],
        summed[7],
        shared_total[3],
        shared_total[4],
        shared_total[5],
    )


def solution(mesh):
    return jax.shard_map(
        per_device,
        mesh=mesh,
        in_specs=(
            P("batch", "tensor", None),
            P("batch", "tensor", None),
            P("batch", None),
            P("batch", None),
            P("batch", None),
            P(),
            P(None, None, "tensor"),
            P(None, "tensor"),
            P("tensor", None),
            P(),
            P(),
            P(),
            P(None, "tensor"),
            P("tensor"),
            P(None, "tensor"),
            P("tensor"),
            P("tensor", None),
            P(),
            P(),
            P(),
        ),
        out_specs=(
            P("batch", "tensor", None),
            P("batch", "tensor", None),
            P(None, None, "tensor"),
            P(None, "tensor"),
            P("tensor", None),
            P(),
            P(),
            P(),
            P(None, "tensor"),
            P("tensor"),
            P(None, "tensor"),
            P("tensor"),
            P("tensor", None),
            P(),
            P(),
            P(),
        ),
        check_vma=False,
    )
```

profile of v0, /device:TPU:0, one launch (start us, length us, event | category | flops | bytes accessed | tf_op | source)
XLA Modules:
  0.0 1297.2 jit_solution(6874520605455802822)
XLA Ops:
  21.5 38.6 %all-gather.22.cloned.1.call-done = bf16[1,1024,2048]{2,1,0:T(8,128)(2,1)} async-done(((bf16[1,128,2048]{2,1,0:T(8,128)(2,1)}), bf16[1,1024,2048]{2,1,0:T(8,128)(2,1)}) %all-gather.22.cloned.1.call-update) | async-done | bytes 4194320 | tf_op jit(solution)/shard_map/all_gather | solution.py:144
  60.1 6.2 fusion.107
  77.3 13.7 %while.55 = (s32[]{:T(128)}, bf16[2,512,2,128]{3,1,2,0:T(8,128)(2,1)}, f32[2,2,512]{2,1,0:T(2,128)S(1)}, s32[2]{0:T(128)S(1)}, pred[1024,1024]{1,0:T(8,128)(4,1)...) while((s32[]{:T(128)}, ...), condition=%wide.region_20.21_spmd, body=%wide.region_17.20_spmd.sunk | while | flops 549452800 | bytes 17072828 | solution.py:177
  100.3 10.5 all-gather.20.cloned.1.call-done
  110.8 6.2 fusion.104
  123.1 12.6 while.54
  144.3 27.8 %all-to-all-done = bf16[8,128,256]{2,1,0:T(8,128)(2,1)S(1)} async-done(((bf16[8,128,256]{2,1,0:T(8,128)(2,1)}), bf16[8,128,256]{2,1,0:T(8,128)(2,1)S(1)}, u32[]{:S(2)}, u32[]{:S(2)}) %all-to-all-start) | async-done | bytes 524320 | tf_op jit(solution)/shard_map/all_to_all | solution.py:179
  174.2 32.9 %all-gather.10.cloned.1.call-done = bf16[2048,2048]{1,0:T(8,128)(2,1)} async-done(((bf16[256,2048]{1,0:T(8,128)(2,1)}), bf16[2048,2048]{1,0:T(8,128)(2,1)}) %all-gather.10.cloned.1.call-update) | async-done | bytes 8388624 | tf_op jit(solution)/shard_map/all_gather | solution.py:136
  207.1 4.9 fusion.212
  217.4 11.2 reduce-scatter.10.cloned.1.call-start
  228.6 33.9 %all-gather.14.cloned.1.call-done = bf16[1024,2048]{1,0:T(8,128)(2,1)} async-done(((bf16[128,2048]{1,0:T(8,128)(2,1)}), bf16[1024,2048]{1,0:T(8,128)(2,1)}) %all-gather.14.cloned.1.call-update) | async-done | bytes 4194320 | tf_op jit(solution)/shard_map/all_gather | solution.py:185
  262.5 7.9 fusion.118
  275.1 35.4 %all-gather.12.cloned.1.call-done = bf16[1024,2048]{1,0:T(8,128)(2,1)} async-done(((bf16[128,2048]{1,0:T(8,128)(2,1)}), bf16[1024,2048]{1,0:T(8,128)(2,1)}) %all-gather.12.cloned.1.call-update) | async-done | bytes 4194320 | tf_op jit(solution)/shard_map/all_gather | solution.py:185
  310.5 5.9 fusion.128
  317.2 7.2 multiply_convert_fusion.6
  325.6 5.1 convolution_convert_fusion
  330.7 7.8 convolution_convert_fusion.1
  338.6 40.9 %reduce-scatter.10.cloned.1.call-done = bf16[128,2048]{1,0:T(8,128)(2,1)} async-done(((bf16[1024,2048]{1,0:T(8,128)(2,1)}), bf16[128,2048]{1,0:T(8,128)(2,1)}) %reduce-scatter.10.cloned.1.call-update) | async-done | bytes 524304 | tf_op jit(solution)/shard_map/reduce_scatter | solution.py:191
  379.5 51.1 %reduce-scatter.8.cloned.1.call-done = bf16[128,2048]{1,0:T(8,128)(2,1)} async-done(((bf16[1024,2048]{1,0:T(8,128)(2,1)}), bf16[128,2048]{1,0:T(8,128)(2,1)}) %reduce-scatter.8.cloned.1.call-update) | async-done | bytes 524304 | tf_op jit(solution)/shard_map/reduce_scatter | solution.py:191
  440.5 44.1 %all-gather.18.cloned.1.call-done = bf16[1024,2048]{1,0:T(8,128)(2,1)} async-done(((bf16[128,2048]{1,0:T(8,128)(2,1)}), bf16[1024,2048]{1,0:T(8,128)(2,1)}) %all-gather.18.cloned.1.call-update) | async-done | bytes 4194320 | tf_op jit(solution)/shard_map/all_gather | solution.py:210
  484.6 7.7 fusion.110
  492.4 40.3 %all-gather.16.cloned.1.call-done = bf16[1024,2048]{1,0:T(8,128)(2,1)} async-done(((bf16[128,2048]{1,0:T(8,128)(2,1)}), bf16[1024,2048]{1,0:T(8,128)(2,1)}) %all-gather.16.cloned.1.call-update) | async-done | bytes 4194320 | tf_op jit(solution)/shard_map/all_gather | solution.py:210
  532.7 16.1 %multiply_reduce_fusion.3 = (f32[688]{0:T(1024)}, f32[688]{0:T(1024)}, bf16[1024,688]{0,1:T(8,128)(2,1)}, f32[688]{0:T(1024)}, bf16[1024,688]{0,1:T(8,128)(2,1)}...) fusion(f32[1024,688]{0,1:T(8,128)} %copy-done.117, f32[688]{0:T(1024)S(1)} %fusion.193, ...), kind=kOutput, calls=%fused_computation.191 | convolution fusion | flops 2932175872 | bytes 26756576 | tf_op jit(solution)/shard_map/nd,fd->nf/dot_general | solution.py:215
  552.4 6.1 convolution_add_fusion.1
  558.7 5.9 fusion.122
  564.7 6.0 convolution_add_fusion
  570.8 76.2 %reduce-scatter.12.cloned.1.call-done = f32[128,2048]{1,0:T(8,128)} async-done(((f32[1024,2048]{1,0:T(8,128)}), f32[128,2048]{1,0:T(8,128)}) %reduce-scatter.12.cloned.1.call-update) | async-done | bytes 1048592 | tf_op jit(solution)/shard_map/reduce_scatter | solution.py:233
  650.2 87.1 %reduce-scatter.16.cloned.1.call-done = f32[128,2048]{1,0:T(8,128)} async-done(((f32[1024,2048]{1,0:T(8,128)}), f32[128,2048]{1,0:T(8,128)}) %reduce-scatter.16.cloned.1.call-update) | async-done | bytes 1048592 | tf_op jit(solution)/shard_map/reduce_scatter | solution.py:233
  740.7 8.1 fusion.189
  749.8 11.7 add_convert_fusion
  761.6 6.3 convolution_convert_fusion.5
  772.4 6.3 convolution_convert_fusion.4
  779.8 16.5 %all-to-all-done.2 = bf16[128,8,256]{0,2,1:T(8,128)(2,1)S(1)} async-done(((bf16[128,8,256]{0,2,1:T(8,128)(2,1)}), bf16[128,8,256]{0,2,1:T(8,128)(2,1)S(1)}, u32[]{:S(2)}, u32[]{:S(2)}) %all-to-all-start.2) | async-done | bytes 524320 | tf_op jit(solution)/shard_map/all_to_all | solution.py:253
  802.7 67.7 %while.56 = (s32[]{:T(128)}, f32[1024,2,128]{0,2,1:T(8,128)}, f32[1024,2,128]{0,2,1:T(8,128)}, f32[2,512,2,128]{1,0,3,2:T(2,128)}, s32[2]{0:T(128)S(1)}, /*index...) while((s32[]{:T(128)}, f32[1024,2,128]{0,2,1:T(8,128)}, ...), condition=%wide.region_33.34_spmd.clone, body=%wide.region_31.33_spmd.clone.sunk | while | flops 1359346688 | bytes 83390888 | solution.py:296
  819.7 10.4 dynamic_update_slice.36
  853.2 10.4 dynamic_update_slice.36
  881.9 5.0 convolution_convert_fusion.3
  890.1 68.0 %while.57 = (s32[]{:T(128)}, f32[1024,2,128]{0,2,1:T(8,128)}, f32[1024,2,128]{0,2,1:T(8,128)}, f32[2,512,2,128]{1,0,3,2:T(2,128)}, s32[2]{0:T(128)S(1)}, /*index...) while((s32[]{:T(128)}, f32[1024,2,128]{0,2,1:T(8,128)}, ...), condition=%wide.region_42.43_spmd.clone, body=%wide.region_40.42_spmd.clone.sunk | while | flops 1359346688 | bytes 83390888 | solution.py:296
  907.3 10.4 dynamic_update_slice.37
  940.9 10.4 dynamic_update_slice.37
  969.0 5.0 convolution_convert_fusion.2
  975.4 5.0 fusion.213
  995.7 4.7 multiply_convert_fusion.4
  1003.9 4.8 add_convert_fusion.1
  1017.4 42.5 %all-reduce = (f32[2048]{0:T(1024)}, f32[2048]{0:T(1024)}, f32[2048]{0:T(1024)}, f32[2048]{0:T(1024)}, f32[2048]{0:T(1024)}, /*index=5*/f32[2048]{0:T(1024)}) all-reduce(f32[2048]{0:T(1024)S(1)} %add.481, f32[2048]{0:T(1024)S(1)} %add.482, f32[2048]{0:T(1024)S(1)} %add.483, ...), channel_id=1, replica_groups=mesh['batch'=4,'tensor'=8] {'batch','tensor'}, use_global_device_ids=true, to_apply=%region_52.53 | all-reduce | flops 12288 | bytes 98304 | tf_op jit(solution)/shard_map/psum | solution.py:363
  1063.8 10.3 all-reduce.1
  1079.8 193.8 %all-reduce.5.cloned.1.call-done = (bf16[2048,3,256]{2,0,1:T(8,128)(2,1)}, bf16[256,2048]{1,0:T(8,128)(2,1)}, bf16[2048,688]{0,1:T(8,128)(2,1)}, bf16[2048,688]{0,1:T(8,128)(2,1)}, bf16[688,2048]{1,0:T(8,128)(2,1)}) async-done(((bf16[2048,3,256]{2,0,1:T(8,128)(2,1)}, bf16[256,2048]{1,0:T(8,128)(2,1)}, bf16[2048,688]{0,1:T(8,128)(2,1)}, bf16[2048,688]{0,1:T(8,128)(2,1)}, bf16[688,2048]{1,0:T(8,128)(2,1)}), ...) | async-done | bytes 12648464 | tf_op jit(solution)/shard_map/psum | solution.py:354
  1273.6 5.3 reshape.565
  (508 shorter events, 277.7 us)
Async XLA Ops:
  7.2 52.9 %all-gather.22.cloned.1.call-start = ((), (), s32[]{:S(2)}) async-start(), calls=%async_computation.24 | async-start | bytes 4718592 | tf_op jit(solution)/shard_map/all_gather | solution.py:144
  9.7 101.1 %all-gather.20.cloned.1.call-start = ((), (), s32[]{:S(2)}) async-start(), calls=%async_computation.23 | async-start | bytes 4718592 | tf_op jit(solution)/shard_map/all_gather | solution.py:144
  10.4 196.7 %all-gather.10.cloned.1.call-start = ((), (), s32[]{:S(2)}) async-start(), calls=%async_computation.11 | async-start | bytes 9437184 | tf_op jit(solution)/shard_map/all_gather | solution.py:136
  16.3 50.5 %copy-start.32 = (f32[1024,128]{0,1:T(8,128)}, f32[1024,128]{0,1:T(8,128)S(1)}, u32[]{:S(2)}) copy-start(f32[1024,128]{0,1:T(8,128)S(1)} %get-tuple-element.637) | copy-start | bytes 1572868
  16.3 50.5 %copy-start.46 = (f32[1024,128]{0,1:T(8,128)}, f32[1024,128]{0,1:T(8,128)S(1)}, u32[]{:S(2)}) copy-start(f32[1024,128]{0,1:T(8,128)S(1)} %get-tuple-element.638) | copy-start | bytes 1572868
  90.9 26.1 %copy-start.5 = (bf16[1024,2,128]{2,0,1:T(8,128)(2,1)}, bf16[1024,2,128]{2,0,1:T(8,128)(2,1)S(1)}, u32[]{:S(2)}) copy-start(bf16[1024,2,128]{2,0,1:T(8,128)(2,1)S(1)} %get-tuple-element.1116) | copy-start | bytes 1572868
  91.0 26.1 %copy-start.11 = (pred[1024,1024]{1,0:T(8,128)(4,1)}, pred[1024,1024]{1,0:T(8,128)(4,1)S(1)}, u32[]{:S(2)}) copy-start(pred[1024,1024]{1,0:T(8,128)(4,1)S(1)} %get-tuple-element.1118) | copy-start | bytes 3145732
  91.0 26.1 %copy-start.15 = (bf16[1024,2,128]{2,0,1:T(8,128)(2,1)}, bf16[1024,2,128]{2,0,1:T(8,128)(2,1)S(1)}, u32[]{:S(2)}) copy-start(bf16[1024,2,128]{2,0,1:T(8,128)(2,1)S(1)} %get-tuple-element.1122) | copy-start | bytes 1572868
  91.0 26.1 %copy-start.66 = (f32[2,2,512]{2,1,0:T(2,128)}, f32[2,2,512]{2,1,0:T(2,128)S(1)}, u32[]{:S(2)}) copy-start(f32[2,2,512]{2,1,0:T(2,128)S(1)} %get-tuple-element.1003) | copy-start | bytes 24580
  95.9 42.1 %all-to-all-start.1 = ((bf16[8,128,256]{2,1,0:T(8,128)(2,1)}), bf16[8,128,256]{2,1,0:T(8,128)(2,1)}, u32[]{:S(2)}, u32[]{:S(2)}) async-start(bf16[8,128,256]{2,1,0:T(8,128)(2,1)} %convert_element_type.298), calls=%async_computation.2 | async-start | bytes 1048576 | tf_op jit(solution)/shard_map/all_to_all | solution.py:179
  136.3 75.8 %copy-start.7 = (bf16[1024,2,128]{2,0,1:T(8,128)(2,1)}, bf16[1024,2,128]{2,0,1:T(8,128)(2,1)S(1)}, u32[]{:S(2)}) copy-start(bf16[1024,2,128]{2,0,1:T(8,128)(2,1)S(1)} %get-tuple-element.1117) | copy-start | bytes 1572868
  136.3 75.8 %copy-start.12 = (pred[1024,1024]{1,0:T(8,128)(4,1)}, pred[1024,1024]{1,0:T(8,128)(4,1)S(1)}, u32[]{:S(2)}) copy-start(pred[1024,1024]{1,0:T(8,128)(4,1)S(1)} %get-tuple-element.1119) | copy-start | bytes 3145732
  136.3 75.8 %copy-start.18 = (bf16[1024,2,128]{2,0,1:T(8,128)(2,1)}, bf16[1024,2,128]{2,0,1:T(8,128)(2,1)S(1)}, u32[]{:S(2)}) copy-start(bf16[1024,2,128]{2,0,1:T(8,128)(2,1)S(1)} %get-tuple-element.1140) | copy-start | bytes 1572868
  136.3 70.8 %copy-start.70 = (f32[2048]{0:T(1024)S(1)}, f32[2048]{0:T(1024)}, u32[]{:S(2)}) copy-start(f32[2048]{0:T(1024)} %param.37) | copy-start | bytes 24580
  138.0 34.1 %all-to-all-start = ((bf16[8,128,256]{2,1,0:T(8,128)(2,1)}), bf16[8,128,256]{2,1,0:T(8,128)(2,1)S(1)}, u32[]{:S(2)}, u32[]{:S(2)}) async-start(bf16[8,128,256]{2,1,0:T(8,128)(2,1)} %convert_element_type.282), calls=%async_computation | async-start | bytes 1048576 | tf_op jit(solution)/shard_map/all_to_all | solution.py:179
  142.3 120.3 %all-gather.14.cloned.1.call-start = ((), (), s32[]{:S(2)}) async-start(), calls=%async_computation.14 | async-start | bytes 4718592 | tf_op jit(solution)/shard_map/all_gather | solution.py:185
  144.3 67.8 %copy-start.38 = (bf16[128,8,256]{0,2,1:T(8,128)(2,1)}, bf16[128,8,256]{0,2,1:T(8,128)(2,1)S(1)}, u32[]{:S(2)}) copy-start(bf16[128,8,256]{0,2,1:T(8,128)(2,1)S(1)} %copy.133) | copy-start | bytes 1572868
  174.2 38.2 %copy-start.36 = (bf16[128,8,256]{0,2,1:T(8,128)(2,1)}, bf16[128,8,256]{0,2,1:T(8,128)(2,1)S(1)}, u32[]{:S(2)}) copy-start(bf16[128,8,256]{0,2,1:T(8,128)(2,1)S(1)} %copy.128) | copy-start | bytes 1572868
  215.0 13.5 %copy-start.88 = (f32[688]{0:T(1024)S(1)}, f32[688]{0:T(1024)}, u32[]{:S(2)}) copy-start(f32[688]{0:T(1024)} %param.43) | copy-start | bytes 8260
  215.1 13.6 %copy-start.89 = (f32[688]{0:T(1024)S(1)}, f32[688]{0:T(1024)}, u32[]{:S(2)}) copy-start(f32[688]{0:T(1024)} %param.41) | copy-start | bytes 8260
  216.8 93.6 %all-gather.12.cloned.1.call-start = ((), (), s32[]{:S(2)}) async-start(), calls=%async_computation.12 | async-start | bytes 4718592 | tf_op jit(solution)/shard_map/all_gather | solution.py:185
  217.4 162.1 %reduce-scatter.10.cloned.1.call-start = ((), (), s32[]{:S(2)}) async-start(), calls=%async_computation.15 | async-start | bytes 4718592 | tf_op jit(solution)/shard_map/reduce_scatter | solution.py:191
  330.7 99.9 %reduce-scatter.8.cloned.1.call-start = ((), (), s32[]{:S(2)}) async-start(), calls=%async_computation.13 | async-start | bytes 4718592 | tf_op jit(solution)/shard_map/reduce_scatter | solution.py:191
  338.5 92.0 %copy-start.14 = (f32[128,2048]{1,0:T(8,128)S(1)}, f32[128,2048]{1,0:T(8,128)}, u32[]{:S(2)}) copy-start(f32[128,2048]{1,0:T(8,128)} %copy-done.13) | copy-start | bytes 3145732
  338.5 92.0 %copy-start.83 = (f32[2048]{0:T(1024)S(1)}, f32[2048]{0:T(1024)}, u32[]{:S(2)}) copy-start(f32[2048]{0:T(1024)} %param.45) | copy-start | bytes 24580
  338.5 146.1 %all-gather.18.cloned.1.call-start = ((), (), s32[]{:S(2)}) async-start(), calls=%async_computation.19 | async-start | bytes 4718592 | tf_op jit(solution)/shard_map/all_gather | solution.py:210
  439.2 93.5 %all-gather.16.cloned.1.call-start = ((), (), s32[]{:S(2)}) async-start(), calls=%async_computation.16 | async-start | bytes 4718592 | tf_op jit(solution)/shard_map/all_gather | solution.py:210
  440.1 206.9 %reduce-scatter.12.cloned.1.call-start = ((), (), s32[]{:S(2)}) async-start(), calls=%async_computation.17 | async-start | bytes 9437184 | tf_op jit(solution)/shard_map/reduce_scatter | solution.py:233
  532.7 16.1 %copy-start.104 = (bf16[2048,688]{0,1:T(8,128)(2,1)S(1)}, bf16[2048,688]{0,1:T(8,128)(2,1)}, u32[]{:S(2)}) copy-start(bf16[2048,688]{0,1:T(8,128)(2,1)} %param.40) | copy-start | bytes 8454148
  558.5 178.8 %reduce-scatter.16.cloned.1.call-start = ((), (), s32[]{:S(2)}) async-start(), calls=%async_computation.20 | async-start | bytes 9437184 | tf_op jit(solution)/shard_map/reduce_scatter | solution.py:233
  570.7 442.6 %reduce-scatter.20.cloned.1.call-start = ((), (), s32[]{:S(2)}) async-start(), calls=%async_computation.22 | async-start | bytes 9437184 | tf_op jit(solution)/shard_map/reduce_scatter | solution.py:350
  740.6 20.9 %copy-start.21 = (f32[128,2048]{1,0:T(8,128)}, f32[128,2048]{1,0:T(8,128)S(1)}, u32[]{:S(2)}) copy-start(f32[128,2048]{1,0:T(8,128)S(1)} %get-tuple-element.575) | copy-start | bytes 3145732
  749.8 22.6 %copy-start.23 = (f32[128,2048]{1,0:T(8,128)}, f32[128,2048]{1,0:T(8,128)S(1)}, u32[]{:S(2)}) copy-start(f32[128,2048]{1,0:T(8,128)S(1)} %get-tuple-element.573) | copy-start | bytes 3145732
  768.8 27.4 %all-to-all-start.2 = ((bf16[128,8,256]{0,2,1:T(8,128)(2,1)}), bf16[128,8,256]{0,2,1:T(8,128)(2,1)S(1)}, u32[]{:S(2)}, u32[]{:S(2)}) async-start(bf16[128,8,256]{0,2,1:T(8,128)(2,1)} %bitcast.45), calls=%async_computation.5 | async-start | bytes 1048576 | tf_op jit(solution)/shard_map/all_to_all | solution.py:253
  778.7 24.0 %copy-start.8 = (bf16[1024,2,128]{2,0,1:T(8,128)(2,1)S(1)}, bf16[1024,2,128]{2,0,1:T(8,128)(2,1)}, u32[]{:S(2)}) copy-start(bf16[1024,2,128]{2,0,1:T(8,128)(2,1)} %copy-done.7) | copy-start | bytes 1572868
  778.7 24.0 %copy-start.19 = (bf16[1024,2,128]{2,0,1:T(8,128)(2,1)S(1)}, bf16[1024,2,128]{2,0,1:T(8,128)(2,1)}, u32[]{:S(2)}) copy-start(bf16[1024,2,128]{2,0,1:T(8,128)(2,1)} %copy-done.18) | copy-start | bytes 1572868
  778.7 24.0 %copy-start.69 = (f32[2,2,512]{2,1,0:T(2,128)S(1)}, f32[2,2,512]{2,1,0:T(2,128)}, u32[]{:S(2)}) copy-start(f32[2,2,512]{2,1,0:T(2,128)} %copy-done.68) | copy-start | bytes 24580
  796.3 90.9 %all-to-all-start.3 = ((bf16[128,8,256]{0,2,1:T(8,128)(2,1)}), bf16[128,8,256]{0,2,1:T(8,128)(2,1)}, u32[]{:S(2)}, u32[]{:S(2)}) async-start(bf16[128,8,256]{0,2,1:T(8,128)(2,1)} %bitcast.54), calls=%async_computation.8 | async-start | bytes 1048576 | tf_op jit(solution)/shard_map/all_to_all | solution.py:253
  800.4 275.5 %reduce-scatter.14.cloned.1.call-start = ((), (), s32[]{:S(2)}) async-start(), calls=%async_computation.18 | async-start | bytes 4718592 | tf_op jit(solution)/shard_map/reduce_scatter | solution.py:315
  802.7 12.2 copy-start.44
  836.2 12.2 copy-start.44
  887.0 190.1 %reduce-scatter.18.cloned.1.call-start = ((), (), s32[]{:S(2)}) async-start(), calls=%async_computation.21 | async-start | bytes 4718592 | tf_op jit(solution)/shard_map/reduce_scatter | solution.py:315
  890.2 12.3 copy-start.42
  923.8 12.2 copy-start.42
  974.0 299.6 %all-reduce.5.cloned.1.call-start = ((), (), s32[]{:S(2)}) async-start(), calls=%async_computation.25 | async-start | bytes 25296896 | tf_op jit(solution)/shard_map/psum | solution.py:354
  1014.6 47.3 %copy-start.26 = (f32[1024,1,2,128]{0,3,2,1:T(8,128)S(1)}, f32[1024,1,2,128]{0,3,2,1:T(8,128)}, u32[]{:S(2)}) copy-start(f32[1024,1,2,128]{0,3,2,1:T(8,128)} %copy-done.25) | copy-start | bytes 3145732
  1059.9 16.0 %copy-start.22 = (f32[128,2048]{1,0:T(8,128)S(1)}, f32[128,2048]{1,0:T(8,128)}, u32[]{:S(2)}) copy-start(f32[128,2048]{1,0:T(8,128)} %copy-done.21) | copy-start | bytes 3145732
  1061.9 15.2 %copy-start.24 = (f32[128,2048]{1,0:T(8,128)S(1)}, f32[128,2048]{1,0:T(8,128)}, u32[]{:S(2)}) copy-start(f32[128,2048]{1,0:T(8,128)} %copy-done.23) | copy-start | bytes 3145732
  (102 other events, 345.9 us)
Sparse Core Ops, SparseCore 0:
  10.2 49.8 all-gather.21
  62.3 48.5 all-gather.19
  112.4 94.6 all-gather.9
  216.9 45.5 all-gather.13
  264.5 45.8 all-gather.11
  330.8 48.6 reduce-scatter.9
  382.3 48.1 reduce-scatter.7
  439.3 45.2 all-gather.17
  486.8 45.8 all-gather.15
  558.6 88.3 reduce-scatter.11
  649.3 87.9 reduce-scatter.15
  761.7 104.7 reduce-scatter.19
  887.1 51.3 reduce-scatter.13
  974.2 51.4 reduce-scatter.17
  1030.5 243.0 all-reduce.4
where the time goes:
time: 1310 us; the launch traced here: 1300 us
  waiting for transfers between devices  731 us (56%)
  matrix products  258 us (20%)
  local copies, waits for them, and re-layouts  125 us (10%)
  other arithmetic  71.7 us (5%)
  blocking collectives  52.8 us (4%)
  starting transfers between devices  29.4 us (2%)
  between operations  16.6 us (1%)
    psum x1, waiting for transfers between devices, per_device(): lax.psum(column_total[0].astype(jnp.bfloat16), 'batch').astype(jnp.float32)  194 us
    reduce_scatter x2, waiting for transfers between devices, per_device(): lax.psum_scatter(jnp.einsum('nf,df->nd', gate_low, gate_live, preferred_e...  163 us
    reduce_scatter x2, waiting for transfers between devices, per_device(): lax.psum_scatter(jnp.dot(activated, down_live, preferred_element_type=jnp...  92 us
    all_gather x2, waiting for transfers between devices, per_device(): lax.all_gather(grad_two.astype(jnp.bfloat16), 'tensor', axis=0, tiled=True)  84.4 us
    all_gather x2, waiting for transfers between devices, per_device(): whole_hidden = lax.all_gather(hidden_local, 'tensor', axis=0, tiled=True)  69.3 us
    dynamic_update_slice x8, local copies, waits for them, and re-layouts, per_device(): contexts, log_sums = lax.map(forward_block, jnp.arange(block_count))  49.4 us
    all_gather x2, waiting for transfers between devices, per_device(): whole_tokens = lax.all_gather(local_tokens, 'tensor', axis=0, tiled=True)  49.1 us
    psum x1, blocking collectives, per_device(): lax.psum((shared_total[0], shared_total[1], shared_total[2], shared_total...  42.5 us
  transfers between devices with their start and end apart: 19, of which 14 were waited for; matrix products, arithmetic and copies ran while one was open for 26% of the time, Pallas kernels for 0%

commit v1 on v0

v1 whole, which is shorter than its diff:
```python
import functools
import math

import jax
import jax.numpy as jnp
from jax import lax
from jax.experimental import pallas as pl
from jax.experimental.pallas import tpu as pltpu
from jax.sharding import PartitionSpec as P

FF_LIVE = 5461
SEGS = 4
HEAD_DIM = 128

EPSILON = 1e-05
NEG_FILL = -1e30
ROPE_BASE = 10000.0
GELU_ROOT = math.sqrt(2.0 / math.pi)
GELU_CUBIC = 0.044715
FACTOR = 1.0 / math.sqrt(HEAD_DIM)
QUERY_TILE = 256
ROW_TILE = 256
VMEM_LIMIT = 56 * 1024 * 1024
BF16 = jnp.bfloat16
F32 = jnp.float32


def dot_nn(a, b):
    return lax.dot_general(a, b, (((1,), (0,)), ((), ())), preferred_element_type=F32)


def dot_nt(a, b):
    return lax.dot_general(a, b, (((1,), (1,)), ((), ())), preferred_element_type=F32)


def dot_tn(a, b):
    return lax.dot_general(a, b, (((0,), (0,)), ((), ())), preferred_element_type=F32)


def attend_forward_kernel(
    x_ref, w_ref, b_ref, cos_ref, sin_ref, lo_ref, hi_ref, qkv_ref, ctx_ref, lse_ref
):
    step = pl.program_id(0)
    heads = ctx_ref.shape[1] // HEAD_DIM
    tile = x_ref.shape[0]
    rows = pl.ds(pl.multiple_of(step * tile, tile), tile)
    x = x_ref[...]
    cosine = cos_ref[rows, :]
    sine = sin_ref[rows, :]
    for part in range(3):
        projected = dot_nn(x, w_ref[part]) + b_ref[part]
        for head in range(heads):
            value = projected[:, head * HEAD_DIM : (head + 1) * HEAD_DIM]
            if part < 2:
                value = value * cosine + pltpu.roll(value, HEAD_DIM // 2, 1) * sine
            qkv_ref[part * heads + head, rows, :] = value.astype(BF16)

    @pl.when(step == pl.num_programs(0) - 1)
    def _():
        length = qkv_ref.shape[1]
        for head in range(heads):
            keys = qkv_ref[heads + head]
            values_t = qkv_ref[2 * heads + head].T

            def one_tile(index, carry):
                first = pl.multiple_of(index * QUERY_TILE, QUERY_TILE)
                queries = qkv_ref[head, pl.ds(first, QUERY_TILE), :]
                scores = dot_nt(keys, queries)
                place = lax.broadcasted_iota(jnp.int32, (length, QUERY_TILE), 0)
                seen = (place >= lo_ref[index]) & (place <= hi_ref[index])
                scores = jnp.where(seen, scores, NEG_FILL)
                top = jnp.max(scores, axis=0, keepdims=True)
                shifted = jnp.exp((scores - top) * FACTOR)
                total = jnp.sum(shifted, axis=0, keepdims=True)
                probs = (shifted * (1.0 / total)).astype(BF16)
                context_t = dot_nn(values_t, probs)
                ctx_ref[pl.ds(first, QUERY_TILE), head * HEAD_DIM : (head + 1) * HEAD_DIM] = (
                    context_t.T.astype(BF16)
                )
                lse_ref[head, index] = top * FACTOR + jnp.log(total)
                return carry

            lax.fori_loop(0, length // QUERY_TILE, one_tile, 0)


def attend_forward(x, w, b, cosine, sine, lo, hi):
    length, width = x.shape
    head_width = w.shape[2]
    heads = head_width // HEAD_DIM
    tiles = length // QUERY_TILE
    whole = lambda *shape: pl.BlockSpec(shape, lambda i: (0,) * len(shape))
    return pl.pallas_call(
        attend_forward_kernel,
        grid=(length // ROW_TILE,),
        in_specs=[
            pl.BlockSpec((ROW_TILE, width), lambda i: (i, 0)),
            whole(3, width, head_width),
            whole(3, 1, head_width),
            whole(length, HEAD_DIM),
            whole(length, HEAD_DIM),
            whole(tiles, 1, QUERY_TILE),
            whole(tiles, 1, QUERY_TILE),
        ],
        out_specs=[
            whole(3 * heads, length, HEAD_DIM),
            whole(length, head_width),
            whole(heads, tiles, 1, QUERY_TILE),
        ],
        out_shape=[
            jax.ShapeDtypeStruct((3 * heads, length, HEAD_DIM), BF16),
            jax.ShapeDtypeStruct((length, head_width), BF16),
            jax.ShapeDtypeStruct((heads, tiles, 1, QUERY_TILE), F32),
        ],
        compiler_params=pltpu.CompilerParams(vmem_limit_bytes=VMEM_LIMIT),
        cost_estimate=pl.CostEstimate(
            flops=2 * length * width * 3 * head_width + 8 * heads * length * length * HEAD_DIM,
            bytes_accessed=2 * (length * width + 3 * width * head_width),
            transcendentals=heads * length * length,
        ),
        name="attend_forward",
    )(x, w, b, cosine, sine, lo, hi)


def attend_backward_kernel(
    qkv_ref,
    grad_ref,
    lse_ref,
    lo_ref,
    hi_ref,
    cos_ref,
    sin_ref,
    w_ref,
    low_ref,
    bias_ref,
    x_grad_ref,
    key_total,
    value_total,
):
    step = pl.program_id(0)
    length = qkv_ref.shape[1]
    heads = qkv_ref.shape[0] // 3
    tile = x_grad_ref.shape[0]

    def rope_back(grad, cosine, sine):
        return grad * cosine - pltpu.roll(grad, HEAD_DIM // 2, 1) * sine

    @pl.when(step == 0)
    def _():
        for head in range(heads):
            lanes = slice(head * HEAD_DIM, (head + 1) * HEAD_DIM)
            keys = qkv_ref[heads + head]
            keys_t = keys.T
            values = qkv_ref[2 * heads + head]
            key_total[...] = jnp.zeros_like(key_total)
            value_total[...] = jnp.zeros_like(value_total)

            def one_tile(index, query_bias):
                first = pl.multiple_of(index * QUERY_TILE, QUERY_TILE)
                rows = pl.ds(first, QUERY_TILE)
                queries = qkv_ref[head, rows, :]
                grads = grad_ref[rows, lanes]
                scores = dot_nt(keys, queries)
                place = lax.broadcasted_iota(jnp.int32, (length, QUERY_TILE), 0)
                seen = (place >= lo_ref[index]) & (place <= hi_ref[index])
                scores = jnp.where(seen, scores * FACTOR, NEG_FILL)
                probs = jnp.exp(scores - lse_ref[head, index])
                probs_grad = dot_nt(values, grads)
                delta = jnp.sum(probs * probs_grad, axis=0, keepdims=True)
                score_grad = (probs * (probs_grad - delta)).astype(BF16)
                query_grad = dot_nn(keys_t, score_grad).T * FACTOR
                key_total[...] += dot_nn(score_grad, queries)
                value_total[...] += dot_nn(probs.astype(BF16), grads)
                query_grad = rope_back(query_grad, cos_ref[rows, :], sin_ref[rows, :])
                low_ref[0, rows, lanes] = query_grad.astype(BF16)
                return query_bias + jnp.sum(query_grad, axis=0, keepdims=True)

            query_bias = lax.fori_loop(
                0, length // QUERY_TILE, one_tile, jnp.zeros((1, HEAD_DIM), F32)
            )
            key_grad = rope_back(key_total[...] * FACTOR, cos_ref[...], sin_ref[...])
            value_grad = value_total[...]
            low_ref[1, :, lanes] = key_grad.astype(BF16)
            low_ref[2, :, lanes] = value_grad.astype(BF16)
            bias_ref[0, :, lanes] = query_bias
            bias_ref[1, :, lanes] = jnp.sum(key_grad, axis=0, keepdims=True)
            bias_ref[2, :, lanes] = jnp.sum(value_grad, axis=0, keepdims=True)

    rows = pl.ds(pl.multiple_of(step * tile, tile), tile)
    total = dot_nt(low_ref[0, rows, :], w_ref[0])
    total += dot_nt(low_ref[1, rows, :], w_ref[1])
    total += dot_nt(low_ref[2, rows, :], w_ref[2])
    x_grad_ref[...] = total.astype(BF16)


def attend_backward(qkv, grad, lse, lo, hi, cosine, sine, w):
    width, head_width = w.shape[1:]
    length = grad.shape[0]
    heads = head_width // HEAD_DIM
    tiles = length // QUERY_TILE
    whole = lambda *shape: pl.BlockSpec(shape, lambda i: (0,) * len(shape))
    return pl.pallas_call(
        attend_backward_kernel,
        grid=(length // ROW_TILE,),
        in_specs=[
            whole(3 * heads, length, HEAD_DIM),
            whole(length, head_width),
            whole(heads, tiles, 1, QUERY_TILE),
            whole(tiles, 1, QUERY_TILE),
            whole(tiles, 1, QUERY_TILE),
            whole(length, HEAD_DIM),
            whole(length, HEAD_DIM),
            whole(3, width, head_width),
        ],
        out_specs=[
            whole(3, length, head_width),
            whole(3, 1, head_width),
            pl.BlockSpec((ROW_TILE, width), lambda i: (i, 0)),
        ],
        out_shape=[
            jax.ShapeDtypeStruct((3, length, head_width), BF16),
            jax.ShapeDtypeStruct((3, 1, head_width), F32),
            jax.ShapeDtypeStruct((length, width), BF16),
        ],
        scratch_shapes=[
            pltpu.VMEM((length, HEAD_DIM), F32),
            pltpu.VMEM((length, HEAD_DIM), F32),
        ],
        compiler_params=pltpu.CompilerParams(vmem_limit_bytes=VMEM_LIMIT),
        cost_estimate=pl.CostEstimate(
            flops=2 * length * width * 3 * head_width + 20 * heads * length * length * HEAD_DIM,
            bytes_accessed=2 * (length * width + 3 * width * head_width),
            transcendentals=heads * length * length,
        ),
        name="attend_backward",
    )(qkv, grad, lse, lo, hi, cosine, sine, w)


def glu_forward_kernel(
    live_ref, h_ref, wg_ref, wu_ref, wd_ref, bg_ref, bu_ref, act_ref, gelu_ref, slope_ref, out_ref
):
    hidden = h_ref[...]
    gate = dot_nt(wg_ref[...], hidden) + bg_ref[...]
    up = dot_nt(wu_ref[...], hidden) + bu_ref[...]
    squared = gate * gate
    tangent = jnp.tanh(GELU_ROOT * gate * (1.0 + GELU_CUBIC * squared))
    half = 0.5 * (1.0 + tangent)
    gelu = gate * half
    slope = half + 0.5 * gate * (1.0 - tangent * tangent) * GELU_ROOT * (
        1.0 + 3.0 * GELU_CUBIC * squared
    )
    column = lax.broadcasted_iota(jnp.int32, gate.shape, 0)
    activated = jnp.where(column < live_ref[0], gelu * up, 0.0).astype(BF16)
    act_ref[...] = activated
    gelu_ref[...] = gelu.astype(BF16)
    slope_ref[...] = (up * slope).astype(BF16)
    out_ref[...] = dot_tn(activated, wd_ref[...]).astype(BF16)


def glu_forward(live, hidden, wg, wu, wd, bg, bu):
    length, width = hidden.shape
    columns = wg.shape[0]
    whole = lambda *shape: pl.BlockSpec(shape, lambda i: (0,) * len(shape))
    tall = pl.BlockSpec((columns, ROW_TILE), lambda i: (0, i))
    wide = pl.BlockSpec((ROW_TILE, width), lambda i: (i, 0))
    return pl.pallas_call(
        glu_forward_kernel,
        grid=(length // ROW_TILE,),
        in_specs=[pl.BlockSpec(memory_space=pltpu.SMEM), wide]
        + [whole(columns, width)] * 3
        + [whole(columns, 1)] * 2,
        out_specs=[tall, tall, tall, wide],
        out_shape=[jax.ShapeDtypeStruct((columns, length), BF16)] * 3
        + [jax.ShapeDtypeStruct((length, width), BF16)],
        compiler_params=pltpu.CompilerParams(vmem_limit_bytes=VMEM_LIMIT),
        cost_estimate=pl.CostEstimate(
            flops=6 * length * width * columns,
            bytes_accessed=2 * (2 * length * width + 3 * columns * (width + length)),
            transcendentals=length * columns,
        ),
        name="glu_forward",
    )(live, hidden, wg, wu, wd, bg, bu)


def glu_backward_kernel(
    live_ref,
    g_ref,
    wg_ref,
    wu_ref,
    wd_ref,
    gelu_ref,
    slope_ref,
    gate_ref,
    up_ref,
    gate_bias_ref,
    up_bias_ref,
    out_ref,
):
    @pl.when(pl.program_id(0) == 0)
    def _():
        gate_bias_ref[...] = jnp.zeros_like(gate_bias_ref)
        up_bias_ref[...] = jnp.zeros_like(up_bias_ref)

    grad = dot_nt(wd_ref[...], g_ref[...])
    column = lax.broadcasted_iota(jnp.int32, grad.shape, 0)
    grad = jnp.where(column < live_ref[0], grad, 0.0)
    gate_grad = grad * slope_ref[...].astype(F32)
    up_grad = grad * gelu_ref[...].astype(F32)
    gate_bias_ref[...] += jnp.sum(gate_grad, axis=1, keepdims=True)
    up_bias_ref[...] += jnp.sum(up_grad, axis=1, keepdims=True)
    gate_low = gate_grad.astype(BF16)
    up_low = up_grad.astype(BF16)
    gate_ref[...] = gate_low
    up_ref[...] = up_low
    out_ref[...] = (dot_tn(gate_low, wg_ref[...]) + dot_tn(up_low, wu_ref[...])).astype(BF16)


def glu_backward(live, grad, wg, wu, wd, gelu, slope):
    length, width = grad.shape
    columns = wg.shape[0]
    whole = lambda *shape: pl.BlockSpec(shape, lambda i: (0,) * len(shape))
    tall = pl.BlockSpec((columns, ROW_TILE), lambda i: (0, i))
    wide = pl.BlockSpec((ROW_TILE, width), lambda i: (i, 0))
    return pl.pallas_call(
        glu_backward_kernel,
        grid=(length // ROW_TILE,),
        in_specs=[pl.BlockSpec(memory_space=pltpu.SMEM), wide]
        + [whole(columns, width)] * 3
        + [tall, tall],
        out_specs=[tall, tall, whole(columns, 1), whole(columns, 1), wide],
        out_shape=[jax.ShapeDtypeStruct((columns, length), BF16)] * 2
        + [jax.ShapeDtypeStruct((columns, 1), F32)] * 2
        + [jax.ShapeDtypeStruct((length, width), BF16)],
        compiler_params=pltpu.CompilerParams(vmem_limit_bytes=VMEM_LIMIT),
        cost_estimate=pl.CostEstimate(
            flops=6 * length * width * columns,
            bytes_accessed=2 * (2 * length * width + 3 * columns * (width + length)),
            transcendentals=0,
        ),
        name="glu_backward",
    )(live, grad, wg, wu, wd, gelu, slope)


def weight_grad_kernel(packs, outs, *refs):
    lefts = refs[: packs * outs]
    rights = refs[packs * outs : packs * (outs + 1)]
    for out in range(outs):
        total = dot_nn(lefts[out][...], rights[0][...])
        for pack in range(1, packs):
            total += dot_nn(lefts[pack * outs + out][...], rights[pack][...])
        refs[packs * (outs + 1)][out] = total.astype(BF16)


def weight_grad(lefts, rights):
    packs = len(rights)
    outs = len(lefts[0])
    length, width = rights[0].shape
    columns = lefts[0][0].shape[0]
    tile = 512
    return pl.pallas_call(
        functools.partial(weight_grad_kernel, packs, outs),
        grid=(width // tile,),
        in_specs=[pl.BlockSpec((columns, length), lambda i: (0, 0))] * (packs * outs)
        + [pl.BlockSpec((length, tile), lambda i: (0, i))] * packs,
        out_specs=pl.BlockSpec((outs, columns, tile), lambda i: (0, 0, i)),
        out_shape=jax.ShapeDtypeStruct((outs, columns, width), BF16),
        compiler_params=pltpu.CompilerParams(vmem_limit_bytes=VMEM_LIMIT),
        cost_estimate=pl.CostEstimate(
            flops=2 * packs * outs * length * width * columns,
            bytes_accessed=2 * packs * length * (width + outs * columns)
            + 2 * outs * columns * width,
            transcendentals=0,
        ),
        name="weight_grad",
    )(*[left for pack in lefts for left in pack], *rights)


def add_low(a, b):
    return (a.astype(F32) + b.astype(F32)).astype(BF16)


def swap_bit(x, axis_name, bit):
    size = lax.axis_size(axis_name)
    return lax.ppermute(x, axis_name, [(i, i ^ (1 << bit)) for i in range(size)])


def scatter_bits(x, rank, bits, dim, axis_name="batch"):
    for bit in bits:
        half = x.shape[dim] // 2
        mine = (rank >> bit) & 1
        send = lax.dynamic_slice_in_dim(x, (1 - mine) * half, half, dim)
        keep = lax.dynamic_slice_in_dim(x, mine * half, half, dim)
        x = add_low(keep, swap_bit(send, axis_name, bit))
    return x


def gather_bits(x, rank, bits, dim, axis_name="batch"):
    for bit in reversed(bits):
        other = swap_bit(x, axis_name, bit)
        mine = ((rank >> bit) & 1) == 1
        x = jnp.concatenate([jnp.where(mine, other, x), jnp.where(mine, x, other)], axis=dim)
    return x


def bit_orders(size):
    count = size.bit_length() - 1
    return [[(start + k) % count for k in range(count)] for start in range(min(count, 2))]


def sum_over_batch(x, rank, size, dim):
    if size & (size - 1):
        return lax.psum(x, "batch")
    orders = bit_orders(size)
    if not orders:
        return x
    unit = 128 * size if dim == x.ndim - 1 else 16 * size
    width = x.shape[dim]
    cuts = [unit * round(width * k / len(orders) / unit) for k in range(len(orders))] + [width]
    parts = []
    for order, first, last in zip(orders, cuts[:-1], cuts[1:]):
        piece = lax.slice_in_dim(x, first, last, axis=dim)
        piece = scatter_bits(piece, rank, order, dim)
        parts.append(gather_bits(piece, rank, order, dim))
    return jnp.concatenate(parts, axis=dim)


def ring_gather(x, rank, axis_size, shift):
    up = down = x
    ups, downs = [], []
    for _ in range(axis_size - 1):
        up, down = shift(up, 1), shift(down, -1)
        ups.append(up)
        downs.append(down)
    whole = jnp.zeros((axis_size,) + x.shape, x.dtype)
    whole = lax.dynamic_update_index_in_dim(whole, x, rank, 0)
    for away in range(1, axis_size):
        block = jnp.where(rank >= away, ups[away - 1], downs[axis_size - away - 1])
        whole = lax.dynamic_update_index_in_dim(
            whole, block, lax.rem(rank - away + axis_size, axis_size), 0
        )
    return whole


def line_scatter(x, rank, axis_size, shift):
    total = lax.dynamic_index_in_dim(x, rank, 0, keepdims=False).astype(F32)
    for away in range(1, axis_size):
        for step in (away, -away):
            target = jnp.clip(rank + step, 0, axis_size - 1)
            block = lax.dynamic_index_in_dim(x, target, 0, keepdims=False)
            total = total + shift(block, step).astype(F32)
    return total.astype(BF16)


def sum_all(x, axis_name):
    size = lax.axis_size(axis_name)
    if size & (size - 1):
        return lax.psum(x, axis_name)
    for bit in range(size.bit_length() - 1):
        x = x + swap_bit(x, axis_name, bit)
    return x


def norm_forward(values, gain_vector, shift_vector):
    average = jnp.mean(values, axis=-1, keepdims=True)
    centred = values - average
    spread = jnp.mean(centred * centred, axis=-1, keepdims=True)
    inverse = lax.rsqrt(spread + EPSILON)
    normal = centred * inverse
    return (normal * gain_vector + shift_vector, normal, inverse)


def norm_backward(grad_rows, gain_vector, normal, inverse):
    scaled = grad_rows * gain_vector
    return inverse * (
        scaled
        - jnp.mean(scaled, axis=-1, keepdims=True)
        - normal * jnp.mean(scaled * normal, axis=-1, keepdims=True)
    )


def rotary_tables(positions):
    half_dim = HEAD_DIM // 2
    frequency = jnp.exp(
        jnp.arange(half_dim, dtype=F32) * (-2.0 * math.log(ROPE_BASE) / HEAD_DIM)
    )
    angles = positions.astype(F32)[..., None] * frequency
    cosine, sine = jnp.cos(angles), jnp.sin(angles)
    return (
        jnp.concatenate([cosine, cosine], axis=-1),
        jnp.concatenate([-sine, sine], axis=-1),
    )


def visible_range(segment, prefix):
    member = (segment[:, None] == jnp.arange(SEGS, dtype=jnp.int32)[None, :]).astype(jnp.int32)
    counts = jnp.sum(member, axis=0)
    starts = jnp.cumsum(counts) - counts
    ordinal = jnp.arange(segment.shape[0], dtype=jnp.int32)
    first = jnp.sum(member * starts[None, :], axis=1)
    seen = jnp.sum(member * jnp.minimum(prefix, counts)[None, :], axis=1)
    last = jnp.maximum(ordinal, first + seen - 1)
    tiled = (segment.shape[0] // QUERY_TILE, 1, QUERY_TILE)
    return first.reshape(tiled), last.reshape(tiled)


def per_device(
    batch_size,
    tensor_size,
    tokens,
    cotangent,
    segment_ids,
    prefix_lengths,
    rotary_positions,
    residual_scale,
    qkv_weight,
    qkv_bias,
    out_weight,
    out_bias,
    norm_gain,
    norm_shift,
    gate_weight,
    gate_bias,
    up_weight,
    up_bias,
    down_weight,
    down_bias,
    final_gain,
    final_shift,
):
    packs, local_rows, width = tokens.shape
    head_width = qkv_weight.shape[2]
    columns = down_weight.shape[0]
    pack_range = range(packs)
    batch_rank = lax.axis_index("batch")
    tensor_rank = lax.axis_index("tensor")
    chips = tensor_size // 2
    chip_rank = tensor_rank // 2
    core = lax.rem(tensor_rank, 2)
    orders = bit_orders(batch_size)
    scale_value = residual_scale[0]

    def shift(x, step):
        moves = [
            (chip * 2 + side, (chip + step) * 2 + side)
            for chip in range(chips)
            for side in range(2)
            if 0 <= chip + step < chips
        ]
        return lax.ppermute(x, "tensor", moves)

    gate_rows = gate_weight.T
    up_rows = up_weight.T
    qkv_slabs = jnp.transpose(qkv_weight, (1, 0, 2))
    qkv_bias_rows = qkv_bias[:, None, :]
    gate_bias_column = gate_bias[:, None]
    up_bias_column = up_bias[:, None]
    live = (FF_LIVE - tensor_rank * columns).astype(jnp.int32)[None]

    half = width // 2
    part = half // len(orders)

    def own_piece(x, side):
        pieces = []
        for index, order in enumerate(orders):
            piece = lax.dynamic_slice_in_dim(x, side * half + index * part, part, 1)
            for bit in order:
                size = piece.shape[1] // 2
                piece = lax.dynamic_slice_in_dim(piece, ((batch_rank >> bit) & 1) * size, size, 1)
            pieces.append(piece)
        return jnp.concatenate(pieces, axis=1)

    def join_pieces(x):
        size = x.shape[1] // len(orders)
        return jnp.concatenate(
            [
                gather_bits(x[:, index * size : (index + 1) * size], batch_rank, order, 1)
                for index, order in enumerate(orders)
            ],
            axis=1,
        )

    def by_core(mine, other, axis):
        first = core == 0
        return jnp.concatenate(
            [jnp.where(first, mine, other), jnp.where(first, other, mine)], axis=axis
        )

    chunk = by_core(
        own_piece(out_weight, core), swap_bit(own_piece(out_weight, 1 - core), "tensor", 0), 0
    )
    chunk = ring_gather(chunk, chip_rank, chips, shift).reshape(-1, chunk.shape[1])
    out_half = join_pieces(chunk)
    whole_out = by_core(out_half, swap_bit(out_half, "tensor", 0), 1)

    tables = [rotary_tables(rotary_positions[p]) for p in pack_range]
    ranges = [visible_range(segment_ids[p], prefix_lengths[p]) for p in pack_range]
    whole_tokens = [lax.all_gather(tokens[p], "tensor", axis=0, tiled=True) for p in pack_range]
    qkvs, log_sums, context_rows = [], [], []
    for p in pack_range:
        qkv, context, log_sum = attend_forward(
            whole_tokens[p], qkv_slabs, qkv_bias_rows, *tables[p], *ranges[p]
        )
        qkvs.append(qkv)
        log_sums.append(log_sum)
        context_rows.append(
            lax.all_to_all(context, "tensor", split_axis=0, concat_axis=1, tiled=True)
        )
    normed, normal_one, inverse_one, hidden = [], [], [], []
    for p in pack_range:
        attended = dot_nn(context_rows[p], whole_out) + out_bias
        value, normal, inverse = norm_forward(
            scale_value * tokens[p].astype(F32) + attended, norm_gain, norm_shift
        )
        normed.append(value)
        normal_one.append(normal)
        inverse_one.append(inverse)
        hidden.append(lax.all_gather(value.astype(BF16), "tensor", axis=0, tiled=True))
    activated, gelus, slopes, branches = [], [], [], []
    for p in pack_range:
        act, gelu, slope, branch = glu_forward(
            live, hidden[p], gate_rows, up_rows, down_weight, gate_bias_column, up_bias_column
        )
        activated.append(act)
        gelus.append(gelu)
        slopes.append(slope)
        branches.append(lax.psum_scatter(branch, "tensor", scatter_dimension=0, tiled=True))
    outputs, grads_two, branch_grads = [], [], []
    final_gain_part = final_shift_part = down_bias_part = 0.0
    for p in pack_range:
        rows, normal_two, inverse_two = norm_forward(
            scale_value * normed[p] + (branches[p].astype(F32) + down_bias),
            final_gain,
            final_shift,
        )
        outputs.append(rows.astype(BF16))
        grad_final = cotangent[p].astype(F32)
        final_gain_part += jnp.sum(grad_final * normal_two, axis=0)
        final_shift_part += jnp.sum(grad_final, axis=0)
        grad_two = norm_backward(grad_final, final_gain, normal_two, inverse_two)
        down_bias_part += jnp.sum(grad_two, axis=0)
        grads_two.append(grad_two)
        branch_grads.append(lax.all_gather(grad_two.astype(BF16), "tensor", axis=0, tiled=True))

    gate_lows, up_lows, normed_sums = [], [], []
    gate_bias_part = up_bias_part = 0.0
    for p in pack_range:
        gate_low, up_low, gate_sum, up_sum, normed_part = glu_backward(
            live, branch_grads[p], gate_rows, up_rows, down_weight, gelus[p], slopes[p]
        )
        gate_lows.append(gate_low)
        up_lows.append(up_low)
        gate_bias_part += gate_sum
        up_bias_part += up_sum
        normed_sums.append(lax.psum_scatter(normed_part, "tensor", scatter_dimension=0, tiled=True))
    down_part = weight_grad([[act] for act in activated], branch_grads)
    down_grad = sum_over_batch(down_part[0], batch_rank, batch_size, 1).astype(F32)
    glu_part = weight_grad(list(zip(gate_lows, up_lows)), hidden)
    glu_grad = sum_over_batch(glu_part, batch_rank, batch_size, 2).astype(F32)

    grads_one, context_grads, attended_lows = [], [], []
    norm_gain_part = norm_shift_part = out_bias_part = 0.0
    for p in pack_range:
        normed_grad = normed_sums[p].astype(F32) + scale_value * grads_two[p]
        norm_gain_part += jnp.sum(normed_grad * normal_one[p], axis=0)
        norm_shift_part += jnp.sum(normed_grad, axis=0)
        grad_one = norm_backward(normed_grad, norm_gain, normal_one[p], inverse_one[p])
        out_bias_part += jnp.sum(grad_one, axis=0)
        attended_low = grad_one.astype(BF16)
        grads_one.append(grad_one)
        attended_lows.append(attended_low)
        context_grads.append(
            lax.all_to_all(
                dot_nt(attended_low, whole_out).astype(BF16),
                "tensor",
                split_axis=1,
                concat_axis=0,
                tiled=True,
            )
        )
    input_grads, lows = [], []
    qkv_bias_part = 0.0
    for p in pack_range:
        low, bias_sum, input_part = attend_backward(
            qkvs[p], context_grads[p], log_sums[p], *ranges[p], *tables[p], qkv_slabs
        )
        lows.append(low)
        qkv_bias_part += bias_sum
        input_sum = lax.psum_scatter(input_part, "tensor", scatter_dimension=0, tiled=True)
        input_grads.append(input_sum.astype(F32) + scale_value * grads_one[p])

    out_part = sum(dot_tn(context_rows[p], attended_lows[p]) for p in pack_range).astype(BF16)
    out_sum = add_low(
        lax.dynamic_slice_in_dim(out_part, core * half, half, 1),
        swap_bit(lax.dynamic_slice_in_dim(out_part, (1 - core) * half, half, 1), "tensor", 0),
    )
    out_sum = jnp.concatenate(
        [
            scatter_bits(out_sum[:, index * part : (index + 1) * part], batch_rank, order, 1)
            for index, order in enumerate(orders)
        ],
        axis=1,
    )
    out_sum = line_scatter(
        out_sum.reshape(chips, -1, out_sum.shape[1]), chip_rank, chips, shift
    )
    own_rows = out_sum.shape[0] // 2
    mine = lax.dynamic_slice_in_dim(out_sum, core * own_rows, own_rows, 0)
    other = swap_bit(
        lax.dynamic_slice_in_dim(out_sum, (1 - core) * own_rows, own_rows, 0), "tensor", 0
    )
    out_grad = jnp.concatenate(
        [
            join_pieces(jnp.where(core == 0, mine, other)),
            join_pieces(jnp.where(core == 0, other, mine)),
        ],
        axis=1,
    ).astype(F32)

    qkv_part = sum(
        lax.dot_general(
            whole_tokens[p], lows[p], (((0,), (1,)), ((), ())), preferred_element_type=F32
        )
        for p in pack_range
    )
    qkv_part = jnp.transpose(qkv_part, (1, 0, 2)).astype(BF16)
    qkv_grad = sum_over_batch(qkv_part, batch_rank, batch_size, 1).astype(F32)

    shared = jnp.stack(
        [
            out_bias_part,
            norm_gain_part,
            norm_shift_part,
            down_bias_part,
            final_gain_part,
            final_shift_part,
        ]
    )
    shared = sum_all(sum_all(shared, "tensor"), "batch")
    glu_bias = sum_all(jnp.concatenate([gate_bias_part[:, 0], up_bias_part[:, 0]]), "batch")
    qkv_bias_grad = sum_all(qkv_bias_part[:, 0, :], "batch")
    return (
        jnp.stack(outputs),
        jnp.stack(input_grads),
        jnp.transpose(qkv_grad, (1, 0, 2)),
        qkv_bias_grad,
        out_grad,
        shared[0],
        shared[1],
        shared[2],
        glu_grad[0].T,
        glu_bias[:columns],
        glu_grad[1].T,
        glu_bias[columns:],
        down_grad,
        shared[3],
        shared[4],
        shared[5],
    )


def solution(mesh):
    return jax.shard_map(
        functools.partial(per_device, mesh.shape["batch"], mesh.shape["tensor"]),
        mesh=mesh,
        in_specs=(
            P("batch", "tensor", None),
            P("batch", "tensor", None),
            P("batch", None),
            P("batch", None),
            P("batch", None),
            P(),
            P(None, None, "tensor"),
            P(None, "tensor"),
            P("tensor", None),
            P(),
            P(),
            P(),
            P(None, "tensor"),
            P("tensor"),
            P(None, "tensor"),
            P("tensor"),
            P("tensor", None),
            P(),
            P(),
            P(),
        ),
        out_specs=(
            P("batch", "tensor", None),
            P("batch", "tensor", None),
            P(None, None, "tensor"),
            P(None, "tensor"),
            P("tensor", None),
            P(),
            P(),
            P(),
            P(None, "tensor"),
            P("tensor"),
            P(None, "tensor"),
            P("tensor"),
            P("tensor", None),
            P(),
            P(),
            P(),
        ),
        check_vma=False,
    )
```

time: 1310 us -> 1020 us (0.78)
  waiting for transfers between devices: 731 us -> 482 us
  matrix products: 258 us -> 45.7 us
  Pallas kernels: 0 us -> 178 us
  starting transfers between devices: 29.4 us -> 130 us
  local copies, waits for them, and re-layouts: 125 us -> 65 us
  blocking collectives: 52.8 us -> 0 us
  other arithmetic: 71.7 us -> 95 us
    ppermute x0 -> x65, waiting for transfers between devices: none -> 246 us  [the longest x53 213 us: swap_bit(): return lax.ppermute(x, axis_name, [(i, i ^ 1 << bit) for i in range(size)])]
    dot_general x58 -> x8, matrix products: 258 us -> 45.7 us  [the longest x2 18 us: dot_tn(): lax.dot_general(a, b, (((0,), (0,)), ((), ())), preferred_element_type=F32)]
    psum x1 -> x0, waiting for transfers between devices: 194 us -> none  [per_device(): lax.psum(column_total[0].astype(jnp.bfloat16), 'batch').astype(jnp.float32)]
    pallas_call x0 -> x10, Pallas kernels: none -> 178 us  [the longest x2 44.3 us: glu_backward(): pl.pallas_call(glu_backward_kernel, grid=(length // ROW_TILE,), in_specs=...]
    reduce_scatter x7 -> x6, waiting for transfers between devices: 255 us -> 85.4 us  [the longest x2 85.4 us: per_device(): lax.psum_scatter(branch, 'tensor', scatter_dimension=0, tiled=True)]
    ppermute x0 -> x65, starting transfers between devices: none -> 105 us  [the longest x53 55.3 us: swap_bit(): return lax.ppermute(x, axis_name, [(i, i ^ 1 << bit) for i in range(size)])]
    all_gather x7 -> x6, waiting for transfers between devices: 236 us -> 140 us  [the longest x2 74 us: per_device(): lax.all_gather(value.astype(BF16), 'tensor', axis=0, tiled=True)]
    psum x2 -> x0, blocking collectives: 52.8 us -> none  [the longest x1 42.5 us: per_device(): lax.psum((shared_total[0], shared_total[1], shared_total[2], shared_total...]
  transfers between devices with their start and end apart: 19 -> 81, of which waited for: 14 -> 42; matrix products, arithmetic and copies ran while one was open for 26% -> 18% of each run, Pallas kernels for 0% -> 16%
where the time goes in v1:
time: 1020 us; the launch traced here: 1010 us
  waiting for transfers between devices  482 us (47%)
  Pallas kernels  178 us (17%)
  starting transfers between devices  130 us (13%)
  other arithmetic  95 us (9%)
  local copies, waits for them, and re-layouts  65 us (6%)
  matrix products  45.7 us (4%)
  between operations  17.1 us (2%)
    ppermute x53, waiting for transfers between devices, swap_bit(): return lax.ppermute(x, axis_name, [(i, i ^ 1 << bit) for i in range(size)])  213 us
    reduce_scatter x2, waiting for transfers between devices, per_device(): lax.psum_scatter(branch, 'tensor', scatter_dimension=0, tiled=True)  85.4 us
    all_gather x2, waiting for transfers between devices, per_device(): lax.all_gather(value.astype(BF16), 'tensor', axis=0, tiled=True)  74 us
    all_gather x2, waiting for transfers between devices, per_device(): lax.all_gather(grad_two.astype(BF16), 'tensor', axis=0, tiled=True)  65.9 us
    ppermute x53, starting transfers between devices, swap_bit(): return lax.ppermute(x, axis_name, [(i, i ^ 1 << bit) for i in range(size)])  55.3 us
    ppermute x12, starting transfers between devices, shift(): return lax.ppermute(x, 'tensor', moves)  49.4 us
    pallas_call x2, Pallas kernels, glu_backward(): pl.pallas_call(glu_backward_kernel, grid=(length // ROW_TILE,), in_specs=...  44.3 us
    pallas_call x2, Pallas kernels, attend_backward(): pl.pallas_call(attend_backward_kernel, grid=(length // ROW_TILE,), in_spe...  38.5 us
  transfers between devices with their start and end apart: 81, of which 42 were waited for; matrix products, arithmetic and copies ran while one was open for 18% of the time, Pallas kernels for 16%

profile of v1, /device:TPU:0, one launch (start us, length us, event | category | flops | bytes accessed | tf_op | source)
XLA Modules:
  0.0 1012.9 jit_solution(3167236102572041005)
XLA Ops:
  13.8 5.5 collective-permute-start.1
  19.3 6.2 collective-permute-done.2
  30.0 8.6 collective-permute-start.5
  38.6 9.5 collective-permute-done.3
  49.6 11.3 %collective-permute-start.6 = (bf16[512,256]{1,0:T(8,128)(2,1)S(1)}, bf16[512,256]{1,0:T(8,128)(2,1)S(1)}, u32[]{:S(2)}, u32[]{:S(2)}) collective-permute-start(bf16[512,256]{1,0:T(8,128)(2,1)S(1)} %collective-permute-done.5), channel_id=1, source_target_pairs={{0,2},{1,3},{2,4},{3,5},{4,6},{5,7},{8,10},{9,11},{10,12},{11,13},... | collective-permute-start | bytes 786440 | tf_op jit(solution)/shard_map/ppermute | solution.py:548
  60.9 8.0 collective-permute-done.4
  73.0 8.0 collective-permute-done.7
  86.3 18.2 %collective-permute-done.10 = bf16[2048,256]{1,0:T(8,128)(2,1)} collective-permute-done((bf16[2048,256]{1,0:T(8,128)(2,1)S(1)}, bf16[2048,256]{1,0:T(8,128)(2,1)}, u32[]{:S(2)}, u32[]{:S(2)}) %collective-permute-start.10) | collective-permute-done | bytes 1048608 | tf_op jit(solution)/shard_map/ppermute | solution.py:383
  119.0 17.2 %attend_forward.3 = (bf16[6,1024,128]{2,1,0:T(8,128)(2,1)}, bf16[1024,256]{1,0:T(8,128)(2,1)}, f32[2,4,1,256]{3,2,1,0:T(1,128)}) custom-call(bf16[1024,2048]{1,0:T(8,128)(2,1)} %bitcast.184, bf16[3,2048,256]{2,1,0:T(8,128)(2,1)} %bitcast.224, f32[3,1,256]{2,1,0:T(1,128)} %broadcast_in_dim.23.b_ref, f32[1024,128]{1,0:T(8,128)} %get-tuple-element.284.cos_ref, ...), custom_call_target="tpu_custom_call" | custom-call | flops 5368709120 | bytes 7340032 | tf_op jit(solution)/shard_map/attend_forward/pallas_call | solution.py:92
  138.2 10.9 %all-to-all-start.1 = ((bf16[8,128,256]{1,2,0:T(8,128)(2,1)}), bf16[8,128,256]{1,2,0:T(8,128)(2,1)}, u32[]{:S(2)}, u32[]{:S(2)}) async-start(bf16[8,128,256]{1,2,0:T(8,128)(2,1)} %copy.69), calls=%async_computation.2 | async-start | bytes 1048576 | tf_op jit(solution)/shard_map/all_to_all | solution.py:605
  149.2 6.1 broadcast_select_fusion.1
  155.3 17.3 %attend_forward.2 = (bf16[6,1024,128]{2,1,0:T(8,128)(2,1)}, bf16[1024,256]{1,0:T(8,128)(2,1)}, f32[2,4,1,256]{3,2,1,0:T(1,128)}) custom-call(bf16[1024,2048]{1,0:T(8,128)(2,1)} %bitcast.223, bf16[3,2048,256]{2,1,0:T(8,128)(2,1)} %bitcast.225, f32[3,1,256]{2,1,0:T(1,128)} %broadcast_in_dim.23.b_ref, f32[1024,128]{1,0:T(8,128)} %get-tuple-element.282.cos_ref, ...), custom_call_target="tpu_custom_call" | custom-call | flops 5368709120 | bytes 7340032 | tf_op jit(solution)/shard_map/attend_forward/pallas_call | solution.py:92
  185.0 10.0 all-to-all-done
  204.1 43.6 %all-gather.11.cloned.1.call-done.h_ref.refs_5_ = bf16[1024,2048]{1,0:T(8,128)(2,1)} async-done(((bf16[128,2048]{1,0:T(8,128)(2,1)}), bf16[1024,2048]{1,0:T(8,128)(2,1)}) %all-gather.11.cloned.1.call-update) | async-done | bytes 4194320 | tf_op jit(solution)/shard_map/all_gather | solution.py:616
  247.6 17.0 %glu_forward.3 = (bf16[688,1024]{1,0:T(8,128)(2,1)}, bf16[688,1024]{1,0:T(8,128)(2,1)}, bf16[688,1024]{1,0:T(8,128)(2,1)}, bf16[1024,2048]{1,0:T(8,128)(2,1)}) custom-call(s32[1]{0:T(128)} %bitcast.20.live_ref, bf16[1024,2048]{1,0:T(8,128)(2,1)} %all-gather.11.cloned.1.call-done.h_ref.refs_5_, bf16[688,2048]{1,0:T(8,128)(2,1)} %bitcast.228, ...), custom_call_target="tpu_custom_call" | custom-call | flops 8657043456 | bytes 21069824 | tf_op jit(solution)/shard_map/glu_forward/pallas_call | solution.py:265
  265.1 30.5 %all-gather.9.cloned.1.call-done.h_ref.refs_4_ = bf16[1024,2048]{1,0:T(8,128)(2,1)} async-done(((bf16[128,2048]{1,0:T(8,128)(2,1)}), bf16[1024,2048]{1,0:T(8,128)(2,1)}) %all-gather.9.cloned.1.call-update) | async-done | bytes 4194320 | tf_op jit(solution)/shard_map/all_gather | solution.py:616
  295.5 16.9 %glu_forward.2 = (bf16[688,1024]{1,0:T(8,128)(2,1)}, bf16[688,1024]{1,0:T(8,128)(2,1)}, bf16[688,1024]{1,0:T(8,128)(2,1)}, bf16[1024,2048]{1,0:T(8,128)(2,1)}) custom-call(s32[1]{0:T(128)} %bitcast.20.live_ref, bf16[1024,2048]{1,0:T(8,128)(2,1)} %all-gather.9.cloned.1.call-done.h_ref.refs_4_, bf16[688,2048]{1,0:T(8,128)(2,1)} %bitcast.229, ...), custom_call_target="tpu_custom_call" | custom-call | flops 8657043456 | bytes 21069824 | tf_op jit(solution)/shard_map/glu_forward/pallas_call | solution.py:265
  312.6 34.4 %reduce-scatter.9.cloned.1.call-done = bf16[128,2048]{1,0:T(8,128)(2,1)} async-done(((bf16[1024,2048]{1,0:T(8,128)(2,1)}), bf16[128,2048]{1,0:T(8,128)(2,1)}) %reduce-scatter.9.cloned.1.call-update) | async-done | bytes 524304 | tf_op jit(solution)/shard_map/reduce_scatter | solution.py:625
  347.0 50.9 %reduce-scatter.7.cloned.1.call-done = bf16[128,2048]{1,0:T(8,128)(2,1)} async-done(((bf16[1024,2048]{1,0:T(8,128)(2,1)}), bf16[128,2048]{1,0:T(8,128)(2,1)}) %reduce-scatter.7.cloned.1.call-update) | async-done | bytes 524304 | tf_op jit(solution)/shard_map/reduce_scatter | solution.py:625
  406.4 44.4 %all-gather.13.cloned.1.call-done.g_ref.refs_2_ = bf16[1024,2048]{1,0:T(8,128)(2,1)} async-done(((bf16[128,2048]{1,0:T(8,128)(2,1)}), bf16[1024,2048]{1,0:T(8,128)(2,1)}) %all-gather.13.cloned.1.call-update) | async-done | bytes 4194320 | tf_op jit(solution)/shard_map/all_gather | solution.py:641
  450.8 22.1 %glu_backward.2 = (bf16[688,1024]{1,0:T(8,128)(2,1)}, bf16[688,1024]{1,0:T(8,128)(2,1)}, f32[688,1]{1,0:T(8,128)}, f32[688,1]{1,0:T(8,128)}, bf16[1024,2048]{1,0:T(8,128)(2,1)}) custom-call(s32[1]{0:T(128)} %bitcast.20.live_ref, bf16[1024,2048]{1,0:T(8,128)(2,1)} %all-gather.13.cloned.1.call-done.g_ref.refs_2_, bf16[688,2048]{1,0:T(8,128)(2,1)} %bitcast.230, ...), custom_call_target="tpu_custom_call" | custom-call | flops 8657043456 | bytes 21069824 | tf_op jit(solution)/shard_map/glu_backward/pallas_call | solution.py:323
  476.6 21.5 %all-gather.15.cloned.1.call-done.g_ref.refs_3_ = bf16[1024,2048]{1,0:T(8,128)(2,1)} async-done(((bf16[128,2048]{1,0:T(8,128)(2,1)}), bf16[1024,2048]{1,0:T(8,128)(2,1)}) %all-gather.15.cloned.1.call-update) | async-done | bytes 4194320 | tf_op jit(solution)/shard_map/all_gather | solution.py:641
  498.1 10.0 weight_grad.3
  511.3 22.2 %glu_backward.3 = (bf16[688,1024]{1,0:T(8,128)(2,1)}, bf16[688,1024]{1,0:T(8,128)(2,1)}, f32[688,1]{1,0:T(8,128)}, f32[688,1]{1,0:T(8,128)}, bf16[1024,2048]{1,0:T(8,128)(2,1)}) custom-call(s32[1]{0:T(128)} %bitcast.20.live_ref, bf16[1024,2048]{1,0:T(8,128)(2,1)} %all-gather.15.cloned.1.call-done.g_ref.refs_3_, bf16[688,2048]{1,0:T(8,128)(2,1)} %bitcast.231, ...), custom_call_target="tpu_custom_call" | custom-call | flops 8657043456 | bytes 21069824 | tf_op jit(solution)/shard_map/glu_backward/pallas_call | solution.py:323
  538.8 17.0 %weight_grad.2 = bf16[2,688,2048]{2,1,0:T(8,128)(2,1)} custom-call(bf16[688,1024]{1,0:T(8,128)(2,1)} %get-tuple-element.66.refs_0_, bf16[688,1024]{1,0:T(8,128)(2,1)} %get-tuple-element.67.refs_1_, bf16[688,1024]{1,0:T(8,128)(2,1)} %get-tuple-element.68.refs_2_, bf16[688,1024]{1,0:T(8,128)(2,1)} %get-tuple-element.69.refs_3_, ...), custom_call_target="tpu_custom_call" | custom-call | flops 11542724608 | bytes 19660800 | tf_op jit(solution)/shard_map/weight_grad/pallas_call | solution.py:359
  568.8 10.9 %collective-permute-done.57 = bf16[688,512]{1,0:T(8,128)(2,1)S(1)} collective-permute-done((bf16[688,512]{1,0:T(8,128)(2,1)S(1)}, bf16[688,512]{1,0:T(8,128)(2,1)S(1)}, u32[]{:S(2)}, u32[]{:S(2)}) %collective-permute-start.57) | collective-permute-done | bytes 704544 | tf_op jit(solution)/shard_map/ppermute | solution.py:383
  580.8 35.4 %collective-permute-done.62 = bf16[688,256]{1,0:T(8,128)(2,1)S(1)} collective-permute-done((bf16[688,256]{1,0:T(8,128)(2,1)S(1)}, bf16[688,256]{1,0:T(8,128)(2,1)S(1)}, u32[]{:S(2)}, u32[]{:S(2)}) %collective-permute-start.62) | collective-permute-done | bytes 352288 | tf_op jit(solution)/shard_map/ppermute | solution.py:383
  618.4 7.0 collective-permute-done.63
  631.2 14.1 %collective-permute-done.52 = bf16[2,688,256]{2,1,0:T(8,128)(2,1)S(1)} collective-permute-done((bf16[2,688,256]{2,1,0:T(8,128)(2,1)S(1)}, bf16[2,688,256]{2,1,0:T(8,128)(2,1)S(1)}, u32[]{:S(2)}, u32[]{:S(2)}) %collective-permute-start.52) | collective-permute-done | bytes 704544 | tf_op jit(solution)/shard_map/ppermute | solution.py:383
  647.7 9.2 collective-permute-done.48
  661.9 10.3 %collective-permute-done.53 = bf16[2,688,256]{2,1,0:T(8,128)(2,1)S(1)} collective-permute-done((bf16[2,688,256]{2,1,0:T(8,128)(2,1)S(1)}, bf16[2,688,256]{2,1,0:T(8,128)(2,1)S(1)}, u32[]{:S(2)}, u32[]{:S(2)}) %collective-permute-start.53) | collective-permute-done | bytes 704544 | tf_op jit(solution)/shard_map/ppermute | solution.py:383
  684.4 5.5 convolution_convert_fusion.1
  710.8 19.2 %attend_backward.2 = (bf16[3,1024,256]{2,1,0:T(8,128)(2,1)}, f32[3,1,256]{2,1,0:T(1,128)}, bf16[1024,2048]{1,0:T(8,128)(2,1)}) custom-call(bf16[6,1024,128]{2,1,0:T(8,128)(2,1)} %get-tuple-element.50.qkv_ref, bf16[1024,256]{1,0:T(8,128)(2,1)} %bitcast.40.grad_ref, f32[2,4,1,256]{3,2,1,0:T(1,128)} %get-tuple-element.54.lse_ref, s32[4,1,256]{2,1,0:T(1,128)} %bitcast.211, ...), custom_call_target="tpu_custom_call" | custom-call | flops 8589934592 | bytes 7340032 | tf_op jit(solution)/shard_map/attend_backward/pallas_call | solution.py:201
  730.1 7.3 maximum_convert_fusion
  738.1 9.6 fusion.39
  758.5 8.4 add_convert_fusion
  766.9 18.1 %collective-permute-done.44 = f32[6,2048]{1,0:T(8,128)S(1)} collective-permute-done((f32[6,2048]{1,0:T(8,128)S(1)}, f32[6,2048]{1,0:T(8,128)S(1)}, u32[]{:S(2)}, u32[]{:S(2)}) %collective-permute-start.44) | collective-permute-done | bytes 49184 | tf_op jit(solution)/shard_map/ppermute | solution.py:383
  791.8 19.2 %attend_backward.3 = (bf16[3,1024,256]{2,1,0:T(8,128)(2,1)}, f32[3,1,256]{2,1,0:T(1,128)}, bf16[1024,2048]{1,0:T(8,128)(2,1)}) custom-call(bf16[6,1024,128]{2,1,0:T(8,128)(2,1)} %get-tuple-element.56.qkv_ref, bf16[1024,256]{1,0:T(8,128)(2,1)} %bitcast.188, f32[2,4,1,256]{3,2,1,0:T(1,128)} %get-tuple-element.60.lse_ref, s32[4,1,256]{2,1,0:T(1,128)} %bitcast.208, ...), custom_call_target="tpu_custom_call" | custom-call | flops 8589934592 | bytes 7340032 | tf_op jit(solution)/shard_map/attend_backward/pallas_call | solution.py:201
  824.5 5.3 slice_bitcast_fusion
  835.5 7.5 collective-permute-done.16
  847.7 5.9 collective-permute-done.12
  861.0 5.5 add_convert_fusion.1
  872.9 28.6 %collective-permute-done.14 = bf16[3,256,256]{1,2,0:T(8,128)(2,1)S(1)} collective-permute-done((bf16[3,256,256]{1,2,0:T(8,128)(2,1)S(1)}, bf16[3,256,256]{1,2,0:T(8,128)(2,1)S(1)}, u32[]{:S(2)}, u32[]{:S(2)}) %collective-permute-start.14) | collective-permute-done | bytes 393248 | tf_op jit(solution)/shard_map/ppermute | solution.py:383
  907.0 9.9 collective-permute-done.26
  917.1 9.1 collective-permute-done.24
  946.8 5.9 collective-permute-start.29
  954.0 9.0 collective-permute-start.31
  978.9 6.6 copy.83
  (462 shorter events, 260.6 us)
Async XLA Ops:
  7.2 111.8 %all-gather.19.cloned.1.call-start = ((), (), s32[]{:S(2)}) async-start(), calls=%async_computation.21 | async-start | bytes 4718592 | tf_op jit(solution)/shard_map/all_gather | solution.py:596
  9.5 145.7 %all-gather.17.cloned.1.call-start = ((), (), s32[]{:S(2)}) async-start(), calls=%async_computation.20 | async-start | bytes 4718592 | tf_op jit(solution)/shard_map/all_gather | solution.py:596
  25.5 22.7 %collective-permute-start.3 = (bf16[512,256]{1,0:T(8,128)(2,1)S(1)}, bf16[512,256]{1,0:T(8,128)(2,1)S(1)}, u32[]{:S(2)}, u32[]{:S(2)}) collective-permute-start(bf16[512,256]{1,0:T(8,128)(2,1)S(1)} %collective-permute-done.2), channel_id=1, source_target_pairs={{2,0},{3,1},{4,2},{5,3},{6,4},{7,5},{10,8},{11,9},{12,10},{13,11},... | collective-permute-start | bytes 786440 | tf_op jit(solution)/shard_map/ppermute | solution.py:548
  30.0 19.6 %collective-permute-start.5 = (bf16[512,256]{1,0:T(8,128)(2,1)S(1)}, bf16[512,256]{1,0:T(8,128)(2,1)S(1)}, u32[]{:S(2)}, u32[]{:S(2)}) collective-permute-start(bf16[512,256]{1,0:T(8,128)(2,1)S(1)} %collective-permute-done.1), channel_id=1, source_target_pairs={{0,2},{1,3},{2,4},{3,5},{4,6},{5,7},{8,10},{9,11},{10,12},{11,13},... | collective-permute-start | bytes 786440 | tf_op jit(solution)/shard_map/ppermute | solution.py:548
  48.1 20.8 %collective-permute-start.4 = (bf16[512,256]{1,0:T(8,128)(2,1)S(1)}, bf16[512,256]{1,0:T(8,128)(2,1)S(1)}, u32[]{:S(2)}, u32[]{:S(2)}) collective-permute-start(bf16[512,256]{1,0:T(8,128)(2,1)S(1)} %collective-permute-done.3), channel_id=1, source_target_pairs={{2,0},{3,1},{4,2},{5,3},{6,4},{7,5},{10,8},{11,9},{12,10},{13,11},... | collective-permute-start | bytes 786440 | tf_op jit(solution)/shard_map/ppermute | solution.py:548
  49.6 20.6 %collective-permute-start.6 = (bf16[512,256]{1,0:T(8,128)(2,1)S(1)}, bf16[512,256]{1,0:T(8,128)(2,1)S(1)}, u32[]{:S(2)}, u32[]{:S(2)}) collective-permute-start(bf16[512,256]{1,0:T(8,128)(2,1)S(1)} %collective-permute-done.5), channel_id=1, source_target_pairs={{0,2},{1,3},{2,4},{3,5},{4,6},{5,7},{8,10},{9,11},{10,12},{11,13},... | collective-permute-start | bytes 786440 | tf_op jit(solution)/shard_map/ppermute | solution.py:548
  83.6 20.9 %collective-permute-start.10 = (bf16[2048,256]{1,0:T(8,128)(2,1)S(1)}, bf16[2048,256]{1,0:T(8,128)(2,1)}, u32[]{:S(2)}, u32[]{:S(2)}) collective-permute-start(bf16[2048,256]{1,0:T(8,128)(2,1)S(1)} %pad_maximum_fusion.6), channel_id=1, source_target_pairs={{0,16},{8,24},{16,0},{24,8},{1,17},{9,25},{17,1},{25,9},{2,18},{10... | collective-permute-start | bytes 3145736 | tf_op jit(solution)/shard_map/ppermute | solution.py:383
  84.8 21.5 %collective-permute-start.8 = (bf16[2048,256]{1,0:T(8,128)(2,1)S(1)}, bf16[2048,256]{1,0:T(8,128)(2,1)S(1)}, u32[]{:S(2)}, u32[]{:S(2)}) collective-permute-start(bf16[2048,256]{1,0:T(8,128)(2,1)S(1)} %pad_maximum_fusion.5), channel_id=1, source_target_pairs={{0,8},{8,0},{16,24},{24,16},{1,9},{9,1},{17,25},{25,17},{2,10},{10... | collective-permute-start | bytes 3145736 | tf_op jit(solution)/shard_map/ppermute | solution.py:383
  109.3 39.9 %collective-permute-start.11 = (bf16[2048,1024]{1,0:T(8,128)(2,1)}, bf16[2048,1024]{1,0:T(8,128)(2,1)}, u32[]{:S(2)}, u32[]{:S(2)}) collective-permute-start(bf16[2048,1024]{1,0:T(8,128)(2,1)} %pad_maximum_fusion.1), channel_id=1, source_target_pairs={{0,1},{1,0},{2,3},{3,2},{4,5},{5,4},{6,7},{7,6},{8,9},{9,8},{10,11... | collective-permute-start | bytes 12582920 | tf_op jit(solution)/shard_map/ppermute | solution.py:383
  138.2 36.3 %all-to-all-start.1 = ((bf16[8,128,256]{1,2,0:T(8,128)(2,1)}), bf16[8,128,256]{1,2,0:T(8,128)(2,1)}, u32[]{:S(2)}, u32[]{:S(2)}) async-start(bf16[8,128,256]{1,2,0:T(8,128)(2,1)} %copy.69), calls=%async_computation.2 | async-start | bytes 1048576 | tf_op jit(solution)/shard_map/all_to_all | solution.py:605
  174.6 20.5 %all-to-all-start = ((bf16[8,128,256]{1,2,0:T(8,128)(2,1)}), bf16[8,128,256]{1,2,0:T(8,128)(2,1)S(1)}, u32[]{:S(2)}, u32[]{:S(2)}) async-start(bf16[8,128,256]{1,2,0:T(8,128)(2,1)} %copy.66), calls=%async_computation | async-start | bytes 1048576 | tf_op jit(solution)/shard_map/all_to_all | solution.py:605
  179.7 67.9 %all-gather.11.cloned.1.call-start = ((), (), s32[]{:S(2)}) async-start(), calls=%async_computation.12 | async-start | bytes 4718592 | tf_op jit(solution)/shard_map/all_gather | solution.py:616
  201.6 93.9 %all-gather.9.cloned.1.call-start = ((), (), s32[]{:S(2)}) async-start(), calls=%async_computation.10 | async-start | bytes 4718592 | tf_op jit(solution)/shard_map/all_gather | solution.py:616
  202.2 144.8 %reduce-scatter.9.cloned.1.call-start = ((), (), s32[]{:S(2)}) async-start(), calls=%async_computation.13 | async-start | bytes 4718592 | tf_op jit(solution)/shard_map/reduce_scatter | solution.py:625
  264.6 133.3 %reduce-scatter.7.cloned.1.call-start = ((), (), s32[]{:S(2)}) async-start(), calls=%async_computation.11 | async-start | bytes 4718592 | tf_op jit(solution)/shard_map/reduce_scatter | solution.py:625
  312.5 138.3 %all-gather.13.cloned.1.call-start = ((), (), s32[]{:S(2)}) async-start(), calls=%async_computation.14 | async-start | bytes 4718592 | tf_op jit(solution)/shard_map/all_gather | solution.py:641
  405.4 92.7 %all-gather.15.cloned.1.call-start = ((), (), s32[]{:S(2)}) async-start(), calls=%async_computation.17 | async-start | bytes 4718592 | tf_op jit(solution)/shard_map/all_gather | solution.py:641
  406.3 272.2 %reduce-scatter.11.cloned.1.call-start = ((), (), s32[]{:S(2)}) async-start(), calls=%async_computation.15 | async-start | bytes 4718592 | tf_op jit(solution)/shard_map/reduce_scatter | solution.py:653
  472.9 207.9 %reduce-scatter.15.cloned.1.call-start = ((), (), s32[]{:S(2)}) async-start(), calls=%async_computation.18 | async-start | bytes 4718592 | tf_op jit(solution)/shard_map/reduce_scatter | solution.py:653
  534.7 32.3 %collective-permute-start.61 = (bf16[688,512]{1,0:T(8,128)(2,1)S(1)}, bf16[688,512]{1,0:T(8,128)(2,1)S(1)}, u32[]{:S(2)}, u32[]{:S(2)}) collective-permute-start(bf16[688,512]{1,0:T(8,128)(2,1)S(1)} %constant_dynamic-slice_fusion.1), channel_id=1, source_target_pairs={{0,16},{8,24},{16,0},{24,8},{1,17},{9,25},{17,1},{25,9},{2,18},{10... | collective-permute-start | bytes 2113544 | tf_op jit(solution)/shard_map/ppermute | solution.py:383
  564.0 61.9 %collective-permute-start.51 = (bf16[2,688,512]{2,1,0:T(8,128)(2,1)S(1)}, bf16[2,688,512]{2,1,0:T(8,128)(2,1)S(1)}, u32[]{:S(2)}, u32[]{:S(2)}) collective-permute-start(bf16[2,688,512]{2,1,0:T(8,128)(2,1)S(1)} %constant_dynamic-slice_fusion.5), channel_id=1, source_target_pairs={{0,16},{8,24},{16,0},{24,8},{1,17},{9,25},{17,1},{25,9},{2,18},{10... | collective-permute-start | bytes 4227080 | tf_op jit(solution)/shard_map/ppermute | solution.py:383
  565.3 62.1 %collective-permute-start.47 = (bf16[2,688,512]{2,1,0:T(8,128)(2,1)S(1)}, bf16[2,688,512]{2,1,0:T(8,128)(2,1)S(1)}, u32[]{:S(2)}, u32[]{:S(2)}) collective-permute-start(bf16[2,688,512]{2,1,0:T(8,128)(2,1)S(1)} %constant_dynamic-slice_fusion.7), channel_id=1, source_target_pairs={{0,8},{8,0},{16,24},{24,16},{1,9},{9,1},{17,25},{25,17},{2,10},{10... | collective-permute-start | bytes 4227080 | tf_op jit(solution)/shard_map/ppermute | solution.py:383
  567.3 49.0 %collective-permute-start.62 = (bf16[688,256]{1,0:T(8,128)(2,1)S(1)}, bf16[688,256]{1,0:T(8,128)(2,1)S(1)}, u32[]{:S(2)}, u32[]{:S(2)}) collective-permute-start(bf16[688,256]{1,0:T(8,128)(2,1)S(1)} %constant_dynamic-slice_fusion), channel_id=1, source_target_pairs={{0,8},{8,0},{16,24},{24,16},{1,9},{9,1},{17,25},{25,17},{2,10},{10... | collective-permute-start | bytes 1056776 | tf_op jit(solution)/shard_map/ppermute | solution.py:383
  580.0 37.6 %collective-permute-start.58 = (bf16[688,256]{1,0:T(8,128)(2,1)S(1)}, bf16[688,256]{1,0:T(8,128)(2,1)S(1)}, u32[]{:S(2)}, u32[]{:S(2)}) collective-permute-start(bf16[688,256]{1,0:T(8,128)(2,1)S(1)} %constant_dynamic-slice_fusion.2), channel_id=1, source_target_pairs={{0,16},{8,24},{16,0},{24,8},{1,17},{9,25},{17,1},{25,9},{2,18},{10... | collective-permute-start | bytes 1056776 | tf_op jit(solution)/shard_map/ppermute | solution.py:383
  625.6 20.8 %collective-permute-start.64 = (bf16[688,512]{1,0:T(8,128)(2,1)S(1)}, bf16[688,512]{1,0:T(8,128)(2,1)S(1)}, u32[]{:S(2)}, u32[]{:S(2)}) collective-permute-start(bf16[688,512]{1,0:T(8,128)(2,1)S(1)} %pad_maximum_fusion.12), channel_id=1, source_target_pairs={{0,16},{8,24},{16,0},{24,8},{1,17},{9,25},{17,1},{25,9},{2,18},{10... | collective-permute-start | bytes 2113544 | tf_op jit(solution)/shard_map/ppermute | solution.py:383
  628.0 28.9 %collective-permute-start.48 = (bf16[2,688,256]{2,1,0:T(8,128)(2,1)S(1)}, bf16[2,688,256]{2,1,0:T(8,128)(2,1)S(1)}, u32[]{:S(2)}, u32[]{:S(2)}) collective-permute-start(bf16[2,688,256]{2,1,0:T(8,128)(2,1)S(1)} %constant_dynamic-slice_fusion.6), channel_id=1, source_target_pairs={{0,16},{8,24},{16,0},{24,8},{1,17},{9,25},{17,1},{25,9},{2,18},{10... | collective-permute-start | bytes 2113544 | tf_op jit(solution)/shard_map/ppermute | solution.py:383
  629.8 30.6 %collective-permute-start.60 = (bf16[688,512]{1,0:T(8,128)(2,1)S(1)}, bf16[688,512]{1,0:T(8,128)(2,1)S(1)}, u32[]{:S(2)}, u32[]{:S(2)}) collective-permute-start(bf16[688,512]{1,0:T(8,128)(2,1)S(1)} %pad_maximum_fusion.11), channel_id=1, source_target_pairs={{0,8},{8,0},{16,24},{24,16},{1,9},{9,1},{17,25},{25,17},{2,10},{10... | collective-permute-start | bytes 2113544 | tf_op jit(solution)/shard_map/ppermute | solution.py:383
  645.5 26.7 %collective-permute-start.53 = (bf16[2,688,256]{2,1,0:T(8,128)(2,1)S(1)}, bf16[2,688,256]{2,1,0:T(8,128)(2,1)S(1)}, u32[]{:S(2)}, u32[]{:S(2)}) collective-permute-start(bf16[2,688,256]{2,1,0:T(8,128)(2,1)S(1)} %add_convert_fusion.11), channel_id=1, source_target_pairs={{0,8},{8,0},{16,24},{24,16},{1,9},{9,1},{17,25},{25,17},{2,10},{10... | collective-permute-start | bytes 2113544 | tf_op jit(solution)/shard_map/ppermute | solution.py:383
  673.7 29.9 %collective-permute-start.54 = (bf16[2,688,512]{2,1,0:T(8,128)(2,1)}, bf16[2,688,512]{2,1,0:T(8,128)(2,1)}, u32[]{:S(2)}, u32[]{:S(2)}) collective-permute-start(bf16[2,688,512]{2,1,0:T(8,128)(2,1)} %pad_maximum_fusion.4), channel_id=1, source_target_pairs={{0,16},{8,24},{16,0},{24,8},{1,17},{9,25},{17,1},{25,9},{2,18},{10... | collective-permute-start | bytes 4227080 | tf_op jit(solution)/shard_map/ppermute | solution.py:383
  677.7 29.6 %collective-permute-start.50 = (bf16[2,688,512]{2,1,0:T(8,128)(2,1)}, bf16[2,688,512]{2,1,0:T(8,128)(2,1)}, u32[]{:S(2)}, u32[]{:S(2)}) collective-permute-start(bf16[2,688,512]{2,1,0:T(8,128)(2,1)} %pad_maximum_fusion.3), channel_id=1, source_target_pairs={{0,8},{8,0},{16,24},{24,16},{1,9},{9,1},{17,25},{25,17},{2,10},{10... | collective-permute-start | bytes 4227080 | tf_op jit(solution)/shard_map/ppermute | solution.py:383
  690.7 20.1 %all-to-all-start.2 = ((bf16[128,8,256]{2,0,1:T(8,128)(2,1)}), bf16[128,8,256]{2,0,1:T(8,128)(2,1)}, u32[]{:S(2)}, u32[]{:S(2)}) async-start(bf16[128,8,256]{2,0,1:T(8,128)(2,1)} %bitcast.171), calls=%async_computation.5 | async-start | bytes 1048576 | tf_op jit(solution)/shard_map/all_to_all | solution.py:671
  694.8 306.8 %reduce-scatter.13.cloned.1.call-start = ((), (), s32[]{:S(2)}) async-start(), calls=%async_computation.16 | async-start | bytes 4718592 | tf_op jit(solution)/shard_map/reduce_scatter | solution.py:687
  751.8 39.2 %all-to-all-start.3 = ((bf16[128,8,256]{2,0,1:T(8,128)(2,1)}), bf16[128,8,256]{2,0,1:T(8,128)(2,1)S(1)}, u32[]{:S(2)}, u32[]{:S(2)}) async-start(bf16[128,8,256]{2,0,1:T(8,128)(2,1)} %bitcast.170), calls=%async_computation.8 | async-start | bytes 1048576 | tf_op jit(solution)/shard_map/all_to_all | solution.py:671
  755.3 247.6 %reduce-scatter.17.cloned.1.call-start = ((), (), s32[]{:S(2)}) async-start(), calls=%async_computation.19 | async-start | bytes 4718592 | tf_op jit(solution)/shard_map/reduce_scatter | solution.py:687
  755.5 29.5 %collective-permute-start.44 = (f32[6,2048]{1,0:T(8,128)S(1)}, f32[6,2048]{1,0:T(8,128)S(1)}, u32[]{:S(2)}, u32[]{:S(2)}) collective-permute-start(f32[6,2048]{1,0:T(8,128)S(1)} %add.606), channel_id=1, source_target_pairs={{0,4},{1,5},{2,6},{3,7},{4,0},{5,1},{6,2},{7,3},{8,12},{9,13},{10,... | collective-permute-start | bytes 147464 | tf_op jit(solution)/shard_map/ppermute | solution.py:383
  788.5 72.5 %collective-permute-start.22 = (bf16[2048,1024]{0,1:T(8,128)(2,1)}, bf16[2048,1024]{0,1:T(8,128)(2,1)}, u32[]{:S(2)}, u32[]{:S(2)}) collective-permute-start(bf16[2048,1024]{0,1:T(8,128)(2,1)} %constant_dynamic-slice_fusion.20), channel_id=1, source_target_pairs={{0,1},{1,0},{2,3},{3,2},{4,5},{5,4},{6,7},{7,6},{8,9},{9,8},{10,11... | collective-permute-start | bytes 12582920 | tf_op jit(solution)/shard_map/ppermute | solution.py:383
  789.4 40.4 %collective-permute-start.46 = (f32[6,2048]{1,0:T(8,128)S(1)}, f32[6,2048]{1,0:T(8,128)S(1)}, u32[]{:S(2)}, u32[]{:S(2)}) collective-permute-start(f32[6,2048]{1,0:T(8,128)S(1)} %add.608), channel_id=1, source_target_pairs={{0,16},{8,24},{16,0},{24,8},{1,17},{9,25},{17,1},{25,9},{2,18},{10... | collective-permute-start | bytes 147464 | tf_op jit(solution)/shard_map/ppermute | solution.py:383
  823.9 19.1 %collective-permute-start.16 = (bf16[3,512,256]{1,2,0:T(8,128)(2,1)}, bf16[3,512,256]{1,2,0:T(8,128)(2,1)}, u32[]{:S(2)}, u32[]{:S(2)}) collective-permute-start(bf16[3,512,256]{1,2,0:T(8,128)(2,1)} %constant_dynamic-slice_fusion.22), channel_id=1, source_target_pairs={{0,16},{8,24},{16,0},{24,8},{1,17},{9,25},{17,1},{25,9},{2,18},{10... | collective-permute-start | bytes 2359304 | tf_op jit(solution)/shard_map/ppermute | solution.py:383
  833.0 20.7 %collective-permute-start.12 = (bf16[3,512,256]{1,2,0:T(8,128)(2,1)}, bf16[3,512,256]{1,2,0:T(8,128)(2,1)S(1)}, u32[]{:S(2)}, u32[]{:S(2)}) collective-permute-start(bf16[3,512,256]{1,2,0:T(8,128)(2,1)} %constant_dynamic-slice_fusion.24), channel_id=1, source_target_pairs={{0,8},{8,0},{16,24},{24,16},{1,9},{9,1},{17,25},{25,17},{2,10},{10... | collective-permute-start | bytes 2359304 | tf_op jit(solution)/shard_map/ppermute | solution.py:383
  866.9 34.7 %collective-permute-start.25 = (bf16[2048,256]{0,1:T(8,128)(2,1)S(1)}, bf16[2048,256]{0,1:T(8,128)(2,1)S(1)}, u32[]{:S(2)}, u32[]{:S(2)}) collective-permute-start(bf16[2048,256]{0,1:T(8,128)(2,1)S(1)} %constant_dynamic-slice_fusion.17), channel_id=1, source_target_pairs={{0,16},{8,24},{16,0},{24,8},{1,17},{9,25},{17,1},{25,9},{2,18},{10... | collective-permute-start | bytes 3145736 | tf_op jit(solution)/shard_map/ppermute | solution.py:383
  868.5 33.0 %collective-permute-start.14 = (bf16[3,256,256]{1,2,0:T(8,128)(2,1)S(1)}, bf16[3,256,256]{1,2,0:T(8,128)(2,1)S(1)}, u32[]{:S(2)}, u32[]{:S(2)}) collective-permute-start(bf16[3,256,256]{1,2,0:T(8,128)(2,1)S(1)} %add_convert_fusion.18), channel_id=1, source_target_pairs={{0,16},{8,24},{16,0},{24,8},{1,17},{9,25},{17,1},{25,9},{2,18},{10... | collective-permute-start | bytes 1179656 | tf_op jit(solution)/shard_map/ppermute | solution.py:383
  869.4 33.8 %collective-permute-start.23 = (bf16[2048,256]{0,1:T(8,128)(2,1)S(1)}, bf16[2048,256]{0,1:T(8,128)(2,1)S(1)}, u32[]{:S(2)}, u32[]{:S(2)}) collective-permute-start(bf16[2048,256]{0,1:T(8,128)(2,1)S(1)} %constant_dynamic-slice_fusion.19), channel_id=1, source_target_pairs={{0,8},{8,0},{16,24},{24,16},{1,9},{9,1},{17,25},{25,17},{2,10},{10... | collective-permute-start | bytes 3145736 | tf_op jit(solution)/shard_map/ppermute | solution.py:383
  871.4 63.2 %collective-permute-start.19 = (bf16[3,512,256]{1,2,0:T(8,128)(2,1)}, bf16[3,512,256]{1,2,0:T(8,128)(2,1)}, u32[]{:S(2)}, u32[]{:S(2)}) collective-permute-start(bf16[3,512,256]{1,2,0:T(8,128)(2,1)} %pad_maximum_fusion.10), channel_id=1, source_target_pairs={{0,16},{8,24},{16,0},{24,8},{1,17},{9,25},{17,1},{25,9},{2,18},{10... | collective-permute-start | bytes 2359304 | tf_op jit(solution)/shard_map/ppermute | solution.py:383
  903.6 22.6 %collective-permute-start.24 = (bf16[2048,128]{0,1:T(8,128)(2,1)S(1)}, bf16[2048,128]{0,1:T(8,128)(2,1)S(1)}, u32[]{:S(2)}, u32[]{:S(2)}) collective-permute-start(bf16[2048,128]{0,1:T(8,128)(2,1)S(1)} %constant_dynamic-slice_fusion.18), channel_id=1, source_target_pairs={{0,16},{8,24},{16,0},{24,8},{1,17},{9,25},{17,1},{25,9},{2,18},{10... | collective-permute-start | bytes 1572872 | tf_op jit(solution)/shard_map/ppermute | solution.py:383
  906.1 47.9 %collective-permute-start.15 = (bf16[3,512,256]{1,2,0:T(8,128)(2,1)}, bf16[3,512,256]{1,2,0:T(8,128)(2,1)}, u32[]{:S(2)}, u32[]{:S(2)}) collective-permute-start(bf16[3,512,256]{1,2,0:T(8,128)(2,1)} %pad_maximum_fusion.9), channel_id=1, source_target_pairs={{0,8},{8,0},{16,24},{24,16},{1,9},{9,1},{17,25},{25,17},{2,10},{10... | collective-permute-start | bytes 2359304 | tf_op jit(solution)/shard_map/ppermute | solution.py:383
  933.3 29.7 %collective-permute-start.27 = (bf16[512,256]{1,0:T(8,128)(2,1)S(1)}, bf16[512,256]{1,0:T(8,128)(2,1)S(1)}, u32[]{:S(2)}, u32[]{:S(2)}) collective-permute-start(bf16[512,256]{1,0:T(8,128)(2,1)S(1)} %bitcast.193), channel_id=1, source_target_pairs={{0,2},{1,3},{2,4},{3,5},{4,6},{5,7},{8,10},{9,11},{10,12},{11,13},... | collective-permute-start | bytes 786440 | tf_op jit(solution)/shard_map/ppermute | solution.py:548
  945.5 23.1 %collective-permute-start.28 = (bf16[512,256]{1,0:T(8,128)(2,1)}, bf16[512,256]{1,0:T(8,128)(2,1)}, u32[]{:S(2)}, u32[]{:S(2)}) collective-permute-start(bf16[512,256]{1,0:T(8,128)(2,1)} %bitcast.54), channel_id=1, source_target_pairs={{2,0},{3,1},{4,2},{5,3},{6,4},{7,5},{10,8},{11,9},{12,10},{13,11},... | collective-permute-start | bytes 786440 | tf_op jit(solution)/shard_map/ppermute | solution.py:548
  946.8 21.8 %collective-permute-start.29 = (bf16[512,256]{1,0:T(8,128)(2,1)}, bf16[512,256]{1,0:T(8,128)(2,1)}, u32[]{:S(2)}, u32[]{:S(2)}) collective-permute-start(bf16[512,256]{1,0:T(8,128)(2,1)} %bitcast.55), channel_id=1, source_target_pairs={{0,4},{1,5},{2,6},{3,7},{8,12},{9,13},{10,14},{11,15},{16,20},{17,... | collective-permute-start | bytes 786440 | tf_op jit(solution)/shard_map/ppermute | solution.py:548
  (97 other events, 941.6 us)
Sparse Core Ops, SparseCore 0:
  10.2 60.3 all-gather.18
  84.8 51.4 all-gather.16
  201.8 45.8 all-gather.10
  249.6 45.8 all-gather.8
  298.3 48.6 reduce-scatter.8
  349.7 48.1 reduce-scatter.6
  405.5 45.2 all-gather.12
  452.4 45.6 all-gather.14
  500.9 48.9 reduce-scatter.10
  552.1 48.1 reduce-scatter.14
  730.2 59.2 reduce-scatter.12
  847.2 47.7 reduce-scatter.16

commit v2 on v1

--- a/solution.py
+++ b/solution.py
@@ -21,6 +21,7 @@
 QUERY_TILE = 256
 ROW_TILE = 256
 VMEM_LIMIT = 56 * 1024 * 1024
+LONG = pl.CostEstimate(flops=200_000_000_000, bytes_accessed=1024, transcendentals=0)
 BF16 = jnp.bfloat16
 F32 = jnp.float32
 
@@ -112,11 +113,7 @@
             jax.ShapeDtypeStruct((heads, tiles, 1, QUERY_TILE), F32),
         ],
         compiler_params=pltpu.CompilerParams(vmem_limit_bytes=VMEM_LIMIT),
-        cost_estimate=pl.CostEstimate(
-            flops=2 * length * width * 3 * head_width + 8 * heads * length * length * HEAD_DIM,
-            bytes_accessed=2 * (length * width + 3 * width * head_width),
-            transcendentals=heads * length * length,
-        ),
+        cost_estimate=LONG,
         name="attend_forward",
     )(x, w, b, cosine, sine, lo, hi)
 
@@ -226,11 +223,7 @@
             pltpu.VMEM((length, HEAD_DIM), F32),
         ],
         compiler_params=pltpu.CompilerParams(vmem_limit_bytes=VMEM_LIMIT),
-        cost_estimate=pl.CostEstimate(
-            flops=2 * length * width * 3 * head_width + 20 * heads * length * length * HEAD_DIM,
-            bytes_accessed=2 * (length * width + 3 * width * head_width),
-            transcendentals=heads * length * length,
-        ),
+        cost_estimate=LONG,
         name="attend_backward",
     )(qkv, grad, lse, lo, hi, cosine, sine, w)
 
@@ -272,11 +265,7 @@
         out_shape=[jax.ShapeDtypeStruct((columns, length), BF16)] * 3
         + [jax.ShapeDtypeStruct((length, width), BF16)],
         compiler_params=pltpu.CompilerParams(vmem_limit_bytes=VMEM_LIMIT),
-        cost_estimate=pl.CostEstimate(
-            flops=6 * length * width * columns,
-            bytes_accessed=2 * (2 * length * width + 3 * columns * (width + length)),
-            transcendentals=length * columns,
-        ),
+        cost_estimate=LONG,
         name="glu_forward",
     )(live, hidden, wg, wu, wd, bg, bu)
 
@@ -294,19 +283,28 @@
     gate_bias_ref,
     up_bias_ref,
     out_ref,
+    gate_sum,
+    up_sum,
 ):
     @pl.when(pl.program_id(0) == 0)
     def _():
-        gate_bias_ref[...] = jnp.zeros_like(gate_bias_ref)
-        up_bias_ref[...] = jnp.zeros_like(up_bias_ref)
+        gate_sum[...] = jnp.zeros_like(gate_sum)
+        up_sum[...] = jnp.zeros_like(up_sum)
 
     grad = dot_nt(wd_ref[...], g_ref[...])
     column = lax.broadcasted_iota(jnp.int32, grad.shape, 0)
     grad = jnp.where(column < live_ref[0], grad, 0.0)
     gate_grad = grad * slope_ref[...].astype(F32)
     up_grad = grad * gelu_ref[...].astype(F32)
-    gate_bias_ref[...] += jnp.sum(gate_grad, axis=1, keepdims=True)
-    up_bias_ref[...] += jnp.sum(up_grad, axis=1, keepdims=True)
+    for first in range(0, grad.shape[1], 128):
+        gate_sum[...] += gate_grad[:, first : first + 128]
+        up_sum[...] += up_grad[:, first : first + 128]
+
+    @pl.when(pl.program_id(0) == pl.num_programs(0) - 1)
+    def _():
+        gate_bias_ref[...] = jnp.sum(gate_sum[...], axis=1, keepdims=True)
+        up_bias_ref[...] = jnp.sum(up_sum[...], axis=1, keepdims=True)
+
     gate_low = gate_grad.astype(BF16)
     up_low = up_grad.astype(BF16)
     gate_ref[...] = gate_low
@@ -330,52 +328,126 @@
         out_shape=[jax.ShapeDtypeStruct((columns, length), BF16)] * 2
         + [jax.ShapeDtypeStruct((columns, 1), F32)] * 2
         + [jax.ShapeDtypeStruct((length, width), BF16)],
+        scratch_shapes=[pltpu.VMEM((columns, 128), F32)] * 2,
         compiler_params=pltpu.CompilerParams(vmem_limit_bytes=VMEM_LIMIT),
-        cost_estimate=pl.CostEstimate(
-            flops=6 * length * width * columns,
-            bytes_accessed=2 * (2 * length * width + 3 * columns * (width + length)),
-            transcendentals=0,
-        ),
+        cost_estimate=LONG,
         name="glu_backward",
     )(live, grad, wg, wu, wd, gelu, slope)
 
 
-def weight_grad_kernel(packs, outs, *refs):
+def weight_grad_kernel(packs, outs, blocks_ref, *refs):
     lefts = refs[: packs * outs]
     rights = refs[packs * outs : packs * (outs + 1)]
-    for out in range(outs):
-        total = dot_nn(lefts[out][...], rights[0][...])
-        for pack in range(1, packs):
-            total += dot_nn(lefts[pack * outs + out][...], rights[pack][...])
-        refs[packs * (outs + 1)][out] = total.astype(BF16)
-
-
-def weight_grad(lefts, rights):
+    results = refs[packs * (outs + 1) :]
+    for index, result in enumerate(results):
+
+        @pl.when(pl.program_id(0) == index)
+        def _():
+            for out in range(outs):
+                total = dot_nn(lefts[out][...], rights[0][...])
+                for pack in range(1, packs):
+                    total += dot_nn(lefts[pack * outs + out][...], rights[pack][...])
+                result[out] = total.astype(BF16)
+
+
+def weight_grad(lefts, rights, blocks):
     packs = len(rights)
     outs = len(lefts[0])
     length, width = rights[0].shape
     columns = lefts[0][0].shape[0]
-    tile = 512
+    count = blocks.shape[0]
+    tile = width // count
     return pl.pallas_call(
         functools.partial(weight_grad_kernel, packs, outs),
-        grid=(width // tile,),
-        in_specs=[pl.BlockSpec((columns, length), lambda i: (0, 0))] * (packs * outs)
-        + [pl.BlockSpec((length, tile), lambda i: (0, i))] * packs,
-        out_specs=pl.BlockSpec((outs, columns, tile), lambda i: (0, 0, i)),
-        out_shape=jax.ShapeDtypeStruct((outs, columns, width), BF16),
+        grid_spec=pltpu.PrefetchScalarGridSpec(
+            num_scalar_prefetch=1,
+            grid=(count,),
+            in_specs=[pl.BlockSpec((columns, length), lambda i, at: (0, 0))] * (packs * outs)
+            + [pl.BlockSpec((length, tile), lambda i, at: (0, at[i]))] * packs,
+            out_specs=[pl.BlockSpec((outs, columns, tile), lambda i, at: (0, 0, 0))] * count,
+        ),
+        out_shape=[jax.ShapeDtypeStruct((outs, columns, tile), BF16)] * count,
         compiler_params=pltpu.CompilerParams(vmem_limit_bytes=VMEM_LIMIT),
-        cost_estimate=pl.CostEstimate(
-            flops=2 * packs * outs * length * width * columns,
-            bytes_accessed=2 * packs * length * (width + outs * columns)
-            + 2 * outs * columns * width,
-            transcendentals=0,
+        cost_estimate=LONG,
+        name="weight_grad",
+    )(blocks, *[left for pack in lefts for left in pack], *rights)
+
+
+def slab_grad_kernel(packs, blocks_ref, *refs):
+    results = refs[2 * packs :]
+    for index, result in enumerate(results):
+
+        @pl.when(pl.program_id(0) == index)
+        def _():
+            for part in range(3):
+                total = dot_tn(refs[0][...], refs[packs][part])
+                for pack in range(1, packs):
+                    total += dot_tn(refs[pack][...], refs[packs + pack][part])
+                result[part] = total.astype(BF16)
+
+
+def slab_grad(lefts, rights, blocks):
+    packs = len(rights)
+    length, width = lefts[0].shape
+    columns = rights[0].shape[2]
+    count = blocks.shape[0]
+    tile = width // count
+    return pl.pallas_call(
+        functools.partial(slab_grad_kernel, packs),
+        grid_spec=pltpu.PrefetchScalarGridSpec(
+            num_scalar_prefetch=1,
+            grid=(count,),
+            in_specs=[pl.BlockSpec((length, tile), lambda i, at: (0, at[i]))] * packs
+            + [pl.BlockSpec((3, length, columns), lambda i, at: (0, 0, 0))] * packs,
+            out_specs=[pl.BlockSpec((3, tile, columns), lambda i, at: (0, 0, 0))] * count,
         ),
-        name="weight_grad",
-    )(*[left for pack in lefts for left in pack], *rights)
+        out_shape=[jax.ShapeDtypeStruct((3, tile, columns), BF16)] * count,
+        compiler_params=pltpu.CompilerParams(vmem_limit_bytes=VMEM_LIMIT),
+        cost_estimate=LONG,
+        name="slab_grad",
+    )(blocks, *lefts, *rights)
+
+
+def row_grad_kernel(blocks_ref, left_ref, right_ref, *results):
+    depth = left_ref.shape[1]
+    for index, result in enumerate(results):
+
+        @pl.when(pl.program_id(0) == index)
+        def _():
+            for first in range(0, depth, 512):
+                result[first : first + 512, :] = dot_tn(
+                    left_ref[:, first : first + 512], right_ref[...]
+                ).astype(BF16)
+
+
+def row_grad(left, right, blocks):
+    rows, depth = left.shape
+    count = blocks.shape[0]
+    tile = right.shape[1] // count
+    return pl.pallas_call(
+        row_grad_kernel,
+        grid_spec=pltpu.PrefetchScalarGridSpec(
+            num_scalar_prefetch=1,
+            grid=(count,),
+            in_specs=[
+                pl.BlockSpec((rows, depth), lambda i, at: (0, 0)),
+                pl.BlockSpec((rows, tile), lambda i, at: (0, at[i])),
+            ],
+            out_specs=[pl.BlockSpec((depth, tile), lambda i, at: (0, 0))] * count,
+        ),
+        out_shape=[jax.ShapeDtypeStruct((depth, tile), BF16)] * count,
+        compiler_params=pltpu.CompilerParams(vmem_limit_bytes=VMEM_LIMIT),
+        cost_estimate=LONG,
+        name="row_grad",
+    )(blocks, left, right)
 
 
 def add_low(a, b):
     return (a.astype(F32) + b.astype(F32)).astype(BF16)
+
+
+def after(x, *earlier):
+    return lax.optimization_barrier((x, *earlier))[0]
 
 
 def swap_bit(x, axis_name, bit):
@@ -383,22 +455,79 @@
     return lax.ppermute(x, axis_name, [(i, i ^ (1 << bit)) for i in range(size)])
 
 
-def scatter_bits(x, rank, bits, dim, axis_name="batch"):
-    for bit in bits:
-        half = x.shape[dim] // 2
-        mine = (rank >> bit) & 1
-        send = lax.dynamic_slice_in_dim(x, (1 - mine) * half, half, dim)
-        keep = lax.dynamic_slice_in_dim(x, mine * half, half, dim)
-        x = add_low(keep, swap_bit(send, axis_name, bit))
-    return x
-
-
-def gather_bits(x, rank, bits, dim, axis_name="batch"):
-    for bit in reversed(bits):
-        other = swap_bit(x, axis_name, bit)
-        mine = ((rank >> bit) & 1) == 1
-        x = jnp.concatenate([jnp.where(mine, other, x), jnp.where(mine, x, other)], axis=dim)
-    return x
+class Flow:
+    def __init__(self, chain):
+        self.chain = chain
+        self.result = None
+        self.moving = None
+
+    def step(self, *earlier):
+        try:
+            if self.moving is None:
+                sends = next(self.chain)
+                if earlier:
+                    sends = [(after(x, *earlier), move) for x, move in sends]
+            else:
+                got = [after(x, *earlier) for x in self.moving] if earlier else self.moving
+                sends = self.chain.send(got)
+            self.sent = sends[0][0]
+            self.moving = [move(x) for x, move in sends]
+        except StopIteration as end:
+            self.moving = None
+            self.result = end.value
+        return self
+
+    def finish(self, *earlier):
+        while self.result is None:
+            self.step(*earlier)
+            earlier = ()
+        return self.result
+
+
+def by_bit(bit, axis_name="batch"):
+    return lambda x: swap_bit(x, axis_name, bit)
+
+
+def halving_blocks(rank, orders):
+    bits = [(rank >> order[0]) & 1 for order in orders]
+    sends = [2 * index + 1 - bit for index, bit in enumerate(bits)]
+    keeps = [2 * index + bit for index, bit in enumerate(bits)]
+    return jnp.stack(sends + keeps).astype(jnp.int32)
+
+
+def scatter_stages(parts, rank, orders, dim, blocks=None):
+    if blocks is not None:
+        count = len(orders)
+        got = yield [
+            (block, by_bit(order[0])) for block, order in zip(blocks[:count], orders)
+        ]
+        parts = [add_low(keep, other) for keep, other in zip(blocks[count:], got)]
+    for place in range(blocks is not None, len(orders[0])):
+        keeps, sends = [], []
+        for part, order in zip(parts, orders):
+            half = part.shape[dim] // 2
+            mine = (rank >> order[place]) & 1
+            send = lax.dynamic_slice_in_dim(part, (1 - mine) * half, half, dim)
+            keeps.append(lax.dynamic_slice_in_dim(part, mine * half, half, dim))
+            sends.append((send, by_bit(order[place])))
+        parts = [add_low(keep, got) for keep, got in zip(keeps, (yield sends))]
+    return parts
+
+
+def gather_stages(parts, rank, orders, dim):
+    for place in reversed(range(len(orders[0]))):
+        sends = [(part, by_bit(order[place])) for part, order in zip(parts, orders)]
+        others = yield sends
+        joined = []
+        for part, other, order in zip(parts, others, orders):
+            mine = ((rank >> order[place]) & 1) == 1
+            joined.append(
+                jnp.concatenate(
+                    [jnp.where(mine, other, part), jnp.where(mine, part, other)], axis=dim
+                )
+            )
+        parts = joined
+    return parts
 
 
 def bit_orders(size):
@@ -406,57 +535,39 @@
     return [[(start + k) % count for k in range(count)] for start in range(min(count, 2))]
 
 
-def sum_over_batch(x, rank, size, dim):
-    if size & (size - 1):
-        return lax.psum(x, "batch")
-    orders = bit_orders(size)
-    if not orders:
-        return x
-    unit = 128 * size if dim == x.ndim - 1 else 16 * size
-    width = x.shape[dim]
-    cuts = [unit * round(width * k / len(orders) / unit) for k in range(len(orders))] + [width]
-    parts = []
-    for order, first, last in zip(orders, cuts[:-1], cuts[1:]):
-        piece = lax.slice_in_dim(x, first, last, axis=dim)
-        piece = scatter_bits(piece, rank, order, dim)
-        parts.append(gather_bits(piece, rank, order, dim))
-    return jnp.concatenate(parts, axis=dim)
-
-
-def ring_gather(x, rank, axis_size, shift):
-    up = down = x
-    ups, downs = [], []
-    for _ in range(axis_size - 1):
-        up, down = shift(up, 1), shift(down, -1)
-        ups.append(up)
-        downs.append(down)
-    whole = jnp.zeros((axis_size,) + x.shape, x.dtype)
-    whole = lax.dynamic_update_index_in_dim(whole, x, rank, 0)
-    for away in range(1, axis_size):
-        block = jnp.where(rank >= away, ups[away - 1], downs[axis_size - away - 1])
-        whole = lax.dynamic_update_index_in_dim(
-            whole, block, lax.rem(rank - away + axis_size, axis_size), 0
-        )
-    return whole
-
-
-def line_scatter(x, rank, axis_size, shift):
+def cut(x, count, dim):
+    size = x.shape[dim] // count
+    return [lax.slice_in_dim(x, k * size, (k + 1) * size, axis=dim) for k in range(count)]
+
+
+def sum_stages(blocks, rank, orders, dim):
+    parts = yield from scatter_stages(None, rank, orders, dim, blocks)
+    parts = yield from gather_stages(parts, rank, orders, dim)
+    return jnp.concatenate(parts, axis=dim).astype(F32)
+
+
+def line_scatter_stages(x, rank, size, shift):
+    sends = []
+    for away in range(1, size):
+        for step in (away, -away):
+            target = jnp.clip(rank + step, 0, size - 1)
+            block = lax.dynamic_index_in_dim(x, target, 0, keepdims=False)
+            sends.append((block, functools.partial(shift, step=step)))
     total = lax.dynamic_index_in_dim(x, rank, 0, keepdims=False).astype(F32)
-    for away in range(1, axis_size):
-        for step in (away, -away):
-            target = jnp.clip(rank + step, 0, axis_size - 1)
-            block = lax.dynamic_index_in_dim(x, target, 0, keepdims=False)
-            total = total + shift(block, step).astype(F32)
+    for block in (yield sends):
+        total = total + block.astype(F32)
     return total.astype(BF16)
 
 
-def sum_all(x, axis_name):
-    size = lax.axis_size(axis_name)
-    if size & (size - 1):
-        return lax.psum(x, axis_name)
-    for bit in range(size.bit_length() - 1):
-        x = x + swap_bit(x, axis_name, bit)
-    return x
+def small_stages(everywhere, over_batch, batch_bits, tensor_bits):
+    for bit in range(tensor_bits):
+        (other,) = yield [(everywhere, by_bit(bit, "tensor"))]
+        everywhere = everywhere + other
+    values = [everywhere, *over_batch]
+    for bit in range(batch_bits):
+        others = yield [(value, by_bit(bit)) for value in values]
+        values = [value + other for value, other in zip(values, others)]
+    return values
 
 
 def norm_forward(values, gain_vector, shift_vector):
@@ -527,16 +638,16 @@
     final_shift,
 ):
     packs, local_rows, width = tokens.shape
-    head_width = qkv_weight.shape[2]
     columns = down_weight.shape[0]
-    pack_range = range(packs)
     batch_rank = lax.axis_index("batch")
     tensor_rank = lax.axis_index("tensor")
     chips = tensor_size // 2
     chip_rank = tensor_rank // 2
     core = lax.rem(tensor_rank, 2)
+    first_core = core == 0
     orders = bit_orders(batch_size)
     scale_value = residual_scale[0]
+    across = by_bit(0, "tensor")
 
     def shift(x, step):
         moves = [
@@ -547,6 +658,17 @@
         ]
         return lax.ppermute(x, "tensor", moves)
 
+    def by_core(mine, other, axis):
+        return jnp.concatenate(
+            [jnp.where(first_core, mine, other), jnp.where(first_core, other, mine)], axis=axis
+        )
+
+    def gather_rows(x):
+        return lax.all_gather(x, "tensor", axis=0, tiled=True)
+
+    def scatter_rows(x):
+        return lax.psum_scatter(x, "tensor", scatter_dimension=0, tiled=True)
+
     gate_rows = gate_weight.T
     up_rows = up_weight.T
     qkv_slabs = jnp.transpose(qkv_weight, (1, 0, 2))
@@ -554,13 +676,12 @@
     gate_bias_column = gate_bias[:, None]
     up_bias_column = up_bias[:, None]
     live = (FF_LIVE - tensor_rank * columns).astype(jnp.int32)[None]
-
     half = width // 2
-    part = half // len(orders)
 
     def own_piece(x, side):
         pieces = []
         for index, order in enumerate(orders):
+            part = half // len(orders)
             piece = lax.dynamic_slice_in_dim(x, side * half + index * part, part, 1)
             for bit in order:
                 size = piece.shape[1] // 2
@@ -568,44 +689,61 @@
             pieces.append(piece)
         return jnp.concatenate(pieces, axis=1)
 
-    def join_pieces(x):
-        size = x.shape[1] // len(orders)
-        return jnp.concatenate(
-            [
-                gather_bits(x[:, index * size : (index + 1) * size], batch_rank, order, 1)
-                for index, order in enumerate(orders)
-            ],
-            axis=1,
-        )
-
-    def by_core(mine, other, axis):
-        first = core == 0
-        return jnp.concatenate(
-            [jnp.where(first, mine, other), jnp.where(first, other, mine)], axis=axis
-        )
-
-    chunk = by_core(
-        own_piece(out_weight, core), swap_bit(own_piece(out_weight, 1 - core), "tensor", 0), 0
+    def out_gather_stages(piece):
+        side = piece.shape[1] // 2
+        piece = lax.dynamic_slice_in_dim(piece, core * side, side, 1)
+        parts = yield from gather_stages(cut(piece, len(orders), 1), batch_rank, orders, 1)
+        mine = jnp.concatenate(parts, axis=1)
+        (other,) = yield [(mine, across)]
+        return by_core(mine, other, 1)
+
+    def out_scatter_stages(send, keep):
+        (other,) = yield [(send, across)]
+        total = add_low(keep, other)
+        parts = yield from scatter_stages(cut(total, len(orders), 1), batch_rank, orders, 1)
+        total = jnp.concatenate(parts, axis=1)
+        total = yield from line_scatter_stages(
+            total.reshape(chips, -1, total.shape[1]), chip_rank, chips, shift
+        )
+        rows = total.shape[0] // 2
+        mine = lax.dynamic_slice_in_dim(total, core * rows, rows, 0)
+        (other,) = yield [
+            (lax.dynamic_slice_in_dim(total, (1 - core) * rows, rows, 0), across)
+        ]
+        sides = [jnp.where(first_core, mine, other), jnp.where(first_core, other, mine)]
+        parts = [part for side in sides for part in cut(side, len(orders), 1)]
+        parts = yield from gather_stages(parts, batch_rank, orders * 2, 1)
+        return jnp.concatenate(parts, axis=1).astype(F32)
+
+    tables = [rotary_tables(rotary_positions[p]) for p in range(packs)]
+    ranges = [visible_range(segment_ids[p], prefix_lengths[p]) for p in range(packs)]
+
+    out_piece = gather_rows(
+        jnp.concatenate([own_piece(out_weight, 0), own_piece(out_weight, 1)], axis=1)
     )
-    chunk = ring_gather(chunk, chip_rank, chips, shift).reshape(-1, chunk.shape[1])
-    out_half = join_pieces(chunk)
-    whole_out = by_core(out_half, swap_bit(out_half, "tensor", 0), 1)
-
-    tables = [rotary_tables(rotary_positions[p]) for p in pack_range]
-    ranges = [visible_range(segment_ids[p], prefix_lengths[p]) for p in pack_range]
-    whole_tokens = [lax.all_gather(tokens[p], "tensor", axis=0, tiled=True) for p in pack_range]
+    whole_tokens = []
+    last = out_piece
+    for p in range(packs):
+        whole_tokens.append(gather_rows(tokens[p]))
+    out_flow = Flow(out_gather_stages(out_piece))
+    for _ in range(len(orders[0])):
+        out_flow.step()
+    last = out_flow.sent
+
     qkvs, log_sums, context_rows = [], [], []
-    for p in pack_range:
+    normed, normal_one, inverse_one, hidden = [], [], [], []
+    for p in range(packs):
         qkv, context, log_sum = attend_forward(
-            whole_tokens[p], qkv_slabs, qkv_bias_rows, *tables[p], *ranges[p]
+            after(whole_tokens[p], last), qkv_slabs, qkv_bias_rows, *tables[p], *ranges[p]
         )
         qkvs.append(qkv)
         log_sums.append(log_sum)
         context_rows.append(
             lax.all_to_all(context, "tensor", split_axis=0, concat_axis=1, tiled=True)
         )
-    normed, normal_one, inverse_one, hidden = [], [], [], []
-    for p in pack_range:
+        if p == 0:
+            out_flow.step(context)
+            whole_out = out_flow.finish()
         attended = dot_nn(context_rows[p], whole_out) + out_bias
         value, normal, inverse = norm_forward(
             scale_value * tokens[p].astype(F32) + attended, norm_gain, norm_shift
@@ -613,21 +751,27 @@
         normed.append(value)
         normal_one.append(normal)
         inverse_one.append(inverse)
-        hidden.append(lax.all_gather(value.astype(BF16), "tensor", axis=0, tiled=True))
+        last = value.astype(BF16)
+        hidden.append(gather_rows(last))
+
     activated, gelus, slopes, branches = [], [], [], []
-    for p in pack_range:
+    for p in range(packs):
         act, gelu, slope, branch = glu_forward(
-            live, hidden[p], gate_rows, up_rows, down_weight, gate_bias_column, up_bias_column
+            live, after(hidden[p], last), gate_rows, up_rows, down_weight,
+            gate_bias_column, up_bias_column,
         )
         activated.append(act)
         gelus.append(gelu)
         slopes.append(slope)
-        branches.append(lax.psum_scatter(branch, "tensor", scatter_dimension=0, tiled=True))
-    outputs, grads_two, branch_grads = [], [], []
+        branches.append(scatter_rows(branch))
+        last = act
+
+    outputs, grads_two = [], []
     final_gain_part = final_shift_part = down_bias_part = 0.0
-    for p in pack_range:
+    branch_grads = []
+    for p in range(packs):
         rows, normal_two, inverse_two = norm_forward(
-            scale_value * normed[p] + (branches[p].astype(F32) + down_bias),
+            scale_value * normed[p] + (after(branches[p], last).astype(F32) + down_bias),
             final_gain,
             final_shift,
         )
@@ -638,28 +782,46 @@
         grad_two = norm_backward(grad_final, final_gain, normal_two, inverse_two)
         down_bias_part += jnp.sum(grad_two, axis=0)
         grads_two.append(grad_two)
-        branch_grads.append(lax.all_gather(grad_two.astype(BF16), "tensor", axis=0, tiled=True))
-
+        last = grad_two.astype(BF16)
+        branch_grads.append(gather_rows(last))
+
+    blocks = halving_blocks(batch_rank, orders)
     gate_lows, up_lows, normed_sums = [], [], []
     gate_bias_part = up_bias_part = 0.0
-    for p in pack_range:
+    for p in range(packs):
+        if p == packs - 1:
+            down_blocks = weight_grad(
+                [[after(act, last)] for act in activated], branch_grads, blocks
+            )
+            down_flow = Flow(
+                sum_stages([block[0] for block in down_blocks], batch_rank, orders, 1)
+            ).step()
+            last = down_flow.sent
         gate_low, up_low, gate_sum, up_sum, normed_part = glu_backward(
-            live, branch_grads[p], gate_rows, up_rows, down_weight, gelus[p], slopes[p]
+            live, after(branch_grads[p], last), gate_rows, up_rows, down_weight,
+            gelus[p], slopes[p],
         )
         gate_lows.append(gate_low)
         up_lows.append(up_low)
         gate_bias_part += gate_sum
         up_bias_part += up_sum
-        normed_sums.append(lax.psum_scatter(normed_part, "tensor", scatter_dimension=0, tiled=True))
-    down_part = weight_grad([[act] for act in activated], branch_grads)
-    down_grad = sum_over_batch(down_part[0], batch_rank, batch_size, 1).astype(F32)
-    glu_part = weight_grad(list(zip(gate_lows, up_lows)), hidden)
-    glu_grad = sum_over_batch(glu_part, batch_rank, batch_size, 2).astype(F32)
-
-    grads_one, context_grads, attended_lows = [], [], []
+        normed_sums.append(scatter_rows(normed_part))
+        last = gate_low
+    last = down_flow.step(last).sent
+    glu_blocks = weight_grad(
+        [[after(gate, last), up] for gate, up in zip(gate_lows, up_lows)], hidden, blocks
+    )
+    glu_flow = Flow(sum_stages(glu_blocks, batch_rank, orders, 2)).step()
+    down_flow.step(glu_flow.sent)
+    last = down_flow.sent
+
+    grads_one, attended_lows, lows, input_grads = [], [], [], []
     norm_gain_part = norm_shift_part = out_bias_part = 0.0
-    for p in pack_range:
-        normed_grad = normed_sums[p].astype(F32) + scale_value * grads_two[p]
+    qkv_bias_part = 0.0
+    for p in range(packs):
+        normed_grad = (
+            after(normed_sums[p], last).astype(F32) + scale_value * grads_two[p]
+        )
         norm_gain_part += jnp.sum(normed_grad * normal_one[p], axis=0)
         norm_shift_part += jnp.sum(normed_grad, axis=0)
         grad_one = norm_backward(normed_grad, norm_gain, normal_one[p], inverse_one[p])
@@ -667,76 +829,67 @@
         attended_low = grad_one.astype(BF16)
         grads_one.append(grad_one)
         attended_lows.append(attended_low)
-        context_grads.append(
-            lax.all_to_all(
-                dot_nt(attended_low, whole_out).astype(BF16),
-                "tensor",
-                split_axis=1,
-                concat_axis=0,
-                tiled=True,
+        context_grad = dot_nt(attended_low, whole_out).astype(BF16)
+        last = context_grad
+        context_grad = lax.all_to_all(
+            context_grad, "tensor", split_axis=1, concat_axis=0, tiled=True
+        )
+        if p == packs - 1:
+            glu_flow.step(last)
+            send, keep = row_grad(
+                after(jnp.concatenate(context_rows, axis=0), glu_flow.sent),
+                jnp.concatenate(attended_lows, axis=0),
+                jnp.stack([1 - core, core]).astype(jnp.int32),
             )
-        )
-    input_grads, lows = [], []
-    qkv_bias_part = 0.0
-    for p in pack_range:
+            out_flow = Flow(out_scatter_stages(send, keep)).step()
+            last = out_flow.sent
+            shared = jnp.stack(
+                [
+                    out_bias_part,
+                    norm_gain_part,
+                    norm_shift_part,
+                    down_bias_part,
+                    final_gain_part,
+                    final_shift_part,
+                ]
+            )
+        else:
+            last = down_flow.step(last).sent
         low, bias_sum, input_part = attend_backward(
-            qkvs[p], context_grads[p], log_sums[p], *ranges[p], *tables[p], qkv_slabs
-        )
+            qkvs[p], after(context_grad, last), log_sums[p], *ranges[p], *tables[p], qkv_slabs
+        )
+        last = low
         lows.append(low)
         qkv_bias_part += bias_sum
-        input_sum = lax.psum_scatter(input_part, "tensor", scatter_dimension=0, tiled=True)
-        input_grads.append(input_sum.astype(F32) + scale_value * grads_one[p])
-
-    out_part = sum(dot_tn(context_rows[p], attended_lows[p]) for p in pack_range).astype(BF16)
-    out_sum = add_low(
-        lax.dynamic_slice_in_dim(out_part, core * half, half, 1),
-        swap_bit(lax.dynamic_slice_in_dim(out_part, (1 - core) * half, half, 1), "tensor", 0),
+        input_grads.append(
+            scatter_rows(input_part).astype(F32) + scale_value * grads_one[p]
+        )
+        glu_flow.step(last)
+        last = glu_flow.sent
+        if p == packs - 1:
+            last = out_flow.step(last).sent
+    qkv_blocks = slab_grad(whole_tokens, [after(low, last) for low in lows], blocks)
+    qkv_flow = Flow(sum_stages(qkv_blocks, batch_rank, orders, 1)).step()
+    last = qkv_flow.sent
+    glu_bias = jnp.concatenate([gate_bias_part[:, 0], up_bias_part[:, 0]])
+    small_flow = Flow(
+        small_stages(
+            shared,
+            (glu_bias, qkv_bias_part[:, 0, :]),
+            batch_size.bit_length() - 1,
+            tensor_size.bit_length() - 1,
+        )
     )
-    out_sum = jnp.concatenate(
-        [
-            scatter_bits(out_sum[:, index * part : (index + 1) * part], batch_rank, order, 1)
-            for index, order in enumerate(orders)
-        ],
-        axis=1,
-    )
-    out_sum = line_scatter(
-        out_sum.reshape(chips, -1, out_sum.shape[1]), chip_rank, chips, shift
-    )
-    own_rows = out_sum.shape[0] // 2
-    mine = lax.dynamic_slice_in_dim(out_sum, core * own_rows, own_rows, 0)
-    other = swap_bit(
-        lax.dynamic_slice_in_dim(out_sum, (1 - core) * own_rows, own_rows, 0), "tensor", 0
-    )
-    out_grad = jnp.concatenate(
-        [
-            join_pieces(jnp.where(core == 0, mine, other)),
-            join_pieces(jnp.where(core == 0, other, mine)),
-        ],
-        axis=1,
-    ).astype(F32)
-
-    qkv_part = sum(
-        lax.dot_general(
-            whole_tokens[p], lows[p], (((0,), (1,)), ((), ())), preferred_element_type=F32
-        )
-        for p in pack_range
-    )
-    qkv_part = jnp.transpose(qkv_part, (1, 0, 2)).astype(BF16)
-    qkv_grad = sum_over_batch(qkv_part, batch_rank, batch_size, 1).astype(F32)
-
-    shared = jnp.stack(
-        [
-            out_bias_part,
-            norm_gain_part,
-            norm_shift_part,
-            down_bias_part,
-            final_gain_part,
-            final_shift_part,
-        ]
-    )
-    shared = sum_all(sum_all(shared, "tensor"), "batch")
-    glu_bias = sum_all(jnp.concatenate([gate_bias_part[:, 0], up_bias_part[:, 0]]), "batch")
-    qkv_bias_grad = sum_all(qkv_bias_part[:, 0, :], "batch")
+    flows = [down_flow, glu_flow, out_flow, qkv_flow, small_flow]
+    while any(flow.result is None for flow in flows):
+        for flow in flows:
+            if flow.result is None:
+                flow.step(last)
+                if flow.result is None:
+                    last = flow.sent
+    down_grad, glu_grad, out_grad, qkv_grad, (shared, glu_bias, qkv_bias_grad) = [
+        flow.result for flow in flows
+    ]
     return (
         jnp.stack(outputs),
         jnp.stack(input_grads),

time: 1020 us -> 866 us (0.85)
  waiting for transfers between devices: 482 us -> 389 us
  starting transfers between devices: 130 us -> 92.3 us
  matrix products: 45.7 us -> 12.4 us
  Pallas kernels: 178 us -> 205 us
  local copies, waits for them, and re-layouts: 65 us -> 40.2 us
    ppermute x53 -> x52, waiting for transfers between devices: 213 us -> 108 us  [swap_bit(): return lax.ppermute(x, axis_name, [(i, i ^ 1 << bit) for i in range(size)])]
    all_to_all x2, waiting for transfers between devices: 10 us -> 51.7 us  [per_device(): lax.all_to_all(context, 'tensor', split_axis=0, concat_axis=1, tiled=True)]
    ppermute x12 -> x6, waiting for transfers between devices: 33 us -> 0.02 us  [shift(): return lax.ppermute(x, 'tensor', moves)]
    ppermute x12 -> x6, starting transfers between devices: 49.4 us -> 17 us  [shift(): return lax.ppermute(x, 'tensor', moves)]
    dot_general x4 -> x0, matrix products: 27.3 us -> none  [the longest x2 18 us: dot_tn(): lax.dot_general(a, b, (((0,), (0,)), ((), ())), preferred_element_type=F32)]
    pallas_call x2 -> x4, Pallas kernels: 27.1 us -> 52 us  [the longest x2 30.7 us: weight_grad(): pl.pallas_call(functools.partial(weight_grad_kernel, packs, outs), grid_s...]
    dynamic_slice x25 -> x12, local copies, waits for them, and re-layouts: 22.8 us -> 7.21 us  [the longest x10 5.86 us: scatter_stages(): send = lax.dynamic_slice_in_dim(part, (1 - mine) * half, half, dim)]
    convert_element_type x17, other arithmetic: 10.7 us -> 22.2 us  [add_low(): return (a.astype(F32) + b.astype(F32)).astype(BF16)]
  transfers between devices with their start and end apart: 81 -> 75, of which waited for: 42 -> 27; matrix products, arithmetic and copies ran while one was open for 18% -> 16% of each run, Pallas kernels for 16% -> 24%
where the time goes in v2:
time: 866 us; the launch traced here: 859 us
  waiting for transfers between devices  389 us (45%)
  Pallas kernels  205 us (24%)
  other arithmetic  103 us (12%)
  starting transfers between devices  92.3 us (11%)
  local copies, waits for them, and re-layouts  40.2 us (5%)
  between operations  16.9 us (2%)
  matrix products  12.4 us (1%)
    all_gather x7, waiting for transfers between devices, gather_rows(): return lax.all_gather(x, 'tensor', axis=0, tiled=True)  146 us
    ppermute x52, waiting for transfers between devices, swap_bit(): return lax.ppermute(x, axis_name, [(i, i ^ 1 << bit) for i in range(size)])  108 us
    reduce_scatter x6, waiting for transfers between devices, scatter_rows(): return lax.psum_scatter(x, 'tensor', scatter_dimension=0, tiled=True)  76.2 us
    ppermute x52, starting transfers between devices, swap_bit(): return lax.ppermute(x, axis_name, [(i, i ^ 1 << bit) for i in range(size)])  58.6 us
    all_to_all x2, waiting for transfers between devices, per_device(): lax.all_to_all(context, 'tensor', split_axis=0, concat_axis=1, tiled=True)  51.7 us
    pallas_call x2, Pallas kernels, glu_backward(): pl.pallas_call(glu_backward_kernel, grid=(length // ROW_TILE,), in_specs=...  45.5 us
    pallas_call x2, Pallas kernels, attend_backward(): pl.pallas_call(attend_backward_kernel, grid=(length // ROW_TILE,), in_spe...  38.6 us
    pallas_call x2, Pallas kernels, attend_forward(): pl.pallas_call(attend_forward_kernel, grid=(length // ROW_TILE,), in_spec...  34.5 us
  transfers between devices with their start and end apart: 75, of which 27 were waited for; matrix products, arithmetic and copies ran while one was open for 16% of the time, Pallas kernels for 24%

profile of v2, /device:TPU:0, one launch (start us, length us, event | category | flops | bytes accessed | tf_op | source)
XLA Modules:
  0.0 858.5 jit_solution(6792793489680899654)
XLA Ops:
  12.2 5.0 fusion.33
  17.3 24.8 %all-gather.10.cloned.1.call-done = bf16[2048,512]{1,0:T(8,128)(2,1)} async-done(((bf16[256,512]{1,0:T(8,128)(2,1)}), bf16[2048,512]{1,0:T(8,128)(2,1)}) %all-gather.10.cloned.1.call-update) | async-done | bytes 2097168 | tf_op jit(solution)/shard_map/all_gather | solution.py:667
  49.5 7.9 collective-permute-done.2
  64.5 26.3 %all-gather.20.cloned.1.call-done = bf16[1,1024,2048]{2,1,0:T(8,128)(2,1)} async-done(((bf16[1,128,2048]{2,1,0:T(8,128)(2,1)}), bf16[1,1024,2048]{2,1,0:T(8,128)(2,1)}) %all-gather.20.cloned.1.call-update) | async-done | bytes 4194320 | tf_op jit(solution)/shard_map/all_gather | solution.py:667
  90.9 17.3 %attend_forward.2 = (bf16[6,1024,128]{2,1,0:T(8,128)(2,1)}, bf16[1024,256]{1,0:T(8,128)(2,1)}, f32[2,4,1,256]{3,2,1,0:T(1,128)}) custom-call(bf16[1024,2048]{1,0:T(8,128)(2,1)} %bitcast.220, bf16[3,2048,256]{2,1,0:T(8,128)(2,1)} %bitcast.224, f32[3,1,256]{2,1,0:T(1,128)} %broadcast_in_dim.8.b_ref, f32[1024,128]{1,0:T(8,128)} %get-tuple-element.393.cos_ref, ...), custom_call_target="tpu_custom_call" | custom-call | flops 199999995904 | bytes 1024 | tf_op jit(solution)/shard_map/attend_forward/pallas_call | solution.py:93
  114.3 4.1 all-to-all-start
  122.7 24.0 %all-to-all-done = bf16[8,128,256]{2,1,0:T(8,128)(2,1)} async-done(((bf16[8,128,256]{2,1,0:T(8,128)(2,1)}), bf16[8,128,256]{2,1,0:T(8,128)(2,1)}, u32[]{:S(2)}, u32[]{:S(2)}) %all-to-all-start) | async-done | bytes 524320 | tf_op jit(solution)/shard_map/all_to_all | solution.py:742
  147.9 3.9 broadcast_select_fusion.1
  157.8 17.3 %attend_forward.3 = (bf16[6,1024,128]{2,1,0:T(8,128)(2,1)}, bf16[1024,256]{1,0:T(8,128)(2,1)}, f32[2,4,1,256]{3,2,1,0:T(1,128)}) custom-call(bf16[1024,2048]{1,0:T(8,128)(2,1)} %bitcast.222, bf16[3,2048,256]{2,1,0:T(8,128)(2,1)} %bitcast.225, f32[3,1,256]{2,1,0:T(1,128)} %broadcast_in_dim.8.b_ref, f32[1024,128]{1,0:T(8,128)} %get-tuple-element.395.cos_ref, ...), custom_call_target="tpu_custom_call" | custom-call | flops 199999995904 | bytes 1024 | tf_op jit(solution)/shard_map/attend_forward/pallas_call | solution.py:93
  175.1 3.6 all-to-all-start.1
  180.6 27.7 %all-to-all-done.1 = bf16[8,128,256]{2,1,0:T(8,128)(2,1)S(1)} async-done(((bf16[8,128,256]{2,1,0:T(8,128)(2,1)}), bf16[8,128,256]{2,1,0:T(8,128)(2,1)S(1)}, u32[]{:S(2)}, u32[]{:S(2)}) %all-to-all-start.1) | async-done | bytes 524320 | tf_op jit(solution)/shard_map/all_to_all | solution.py:742
  208.4 4.7 fusion.55
  215.8 16.9 %glu_forward.2 = (bf16[688,1024]{1,0:T(8,128)(2,1)}, bf16[688,1024]{1,0:T(8,128)(2,1)}, bf16[688,1024]{1,0:T(8,128)(2,1)}, bf16[1024,2048]{1,0:T(8,128)(2,1)}) custom-call(s32[1]{0:T(128)} %bitcast.14.live_ref, bf16[1024,2048]{1,0:T(8,128)(2,1)} %all-gather.12.cloned.1.call-done.h_ref.refs_4_, bf16[688,2048]{1,0:T(8,128)(2,1)} %bitcast.228, ...), custom_call_target="tpu_custom_call" | custom-call | flops 199999995904 | bytes 1024 | tf_op jit(solution)/shard_map/glu_forward/pallas_call | solution.py:258
  233.0 29.8 %all-gather.14.cloned.1.call-done.h_ref.refs_5_ = bf16[1024,2048]{1,0:T(8,128)(2,1)} async-done(((bf16[128,2048]{1,0:T(8,128)(2,1)}), bf16[1024,2048]{1,0:T(8,128)(2,1)}) %all-gather.14.cloned.1.call-update) | async-done | bytes 4194320 | tf_op jit(solution)/shard_map/all_gather | solution.py:667
  262.8 17.0 %glu_forward.3 = (bf16[688,1024]{1,0:T(8,128)(2,1)}, bf16[688,1024]{1,0:T(8,128)(2,1)}, bf16[688,1024]{1,0:T(8,128)(2,1)}, bf16[1024,2048]{1,0:T(8,128)(2,1)}) custom-call(s32[1]{0:T(128)} %bitcast.14.live_ref, bf16[1024,2048]{1,0:T(8,128)(2,1)} %all-gather.14.cloned.1.call-done.h_ref.refs_5_, bf16[688,2048]{1,0:T(8,128)(2,1)} %bitcast.229, ...), custom_call_target="tpu_custom_call" | custom-call | flops 199999995904 | bytes 1024 | tf_op jit(solution)/shard_map/glu_forward/pallas_call | solution.py:258
  280.0 34.3 %reduce-scatter.7.cloned.1.call-done = bf16[128,2048]{1,0:T(8,128)(2,1)} async-done(((bf16[1024,2048]{1,0:T(8,128)(2,1)}), bf16[128,2048]{1,0:T(8,128)(2,1)}) %reduce-scatter.7.cloned.1.call-update) | async-done | bytes 524304 | tf_op jit(solution)/shard_map/reduce_scatter | solution.py:670
  323.5 41.9 %reduce-scatter.9.cloned.1.call-done = bf16[128,2048]{1,0:T(8,128)(2,1)} async-done(((bf16[1024,2048]{1,0:T(8,128)(2,1)}), bf16[128,2048]{1,0:T(8,128)(2,1)}) %reduce-scatter.9.cloned.1.call-update) | async-done | bytes 524304 | tf_op jit(solution)/shard_map/reduce_scatter | solution.py:670
  372.3 40.5 %all-gather.16.cloned.1.call-done.g_ref.refs_2_ = bf16[1024,2048]{1,0:T(8,128)(2,1)} async-done(((bf16[128,2048]{1,0:T(8,128)(2,1)}), bf16[1024,2048]{1,0:T(8,128)(2,1)}) %all-gather.16.cloned.1.call-update) | async-done | bytes 4194320 | tf_op jit(solution)/shard_map/all_gather | solution.py:667
  412.9 22.7 %glu_backward.2 = (bf16[688,1024]{1,0:T(8,128)(2,1)}, bf16[688,1024]{1,0:T(8,128)(2,1)}, f32[688,1]{1,0:T(8,128)}, f32[688,1]{1,0:T(8,128)}, bf16[1024,2048]{1,0:T(8,128)(2,1)}) custom-call(s32[1]{0:T(128)} %bitcast.14.live_ref, bf16[1024,2048]{1,0:T(8,128)(2,1)} %all-gather.16.cloned.1.call-done.g_ref.refs_2_, bf16[688,2048]{1,0:T(8,128)(2,1)} %bitcast.230, ...), custom_call_target="tpu_custom_call" | custom-call | flops 199999995904 | bytes 1024 | tf_op jit(solution)/shard_map/glu_backward/pallas_call | solution.py:321
  436.0 24.9 %all-gather.18.cloned.1.call-done.refs_3_.g_ref = bf16[1024,2048]{1,0:T(8,128)(2,1)} async-done(((bf16[128,2048]{1,0:T(8,128)(2,1)}), bf16[1024,2048]{1,0:T(8,128)(2,1)}) %all-gather.18.cloned.1.call-update) | async-done | bytes 4194320 | tf_op jit(solution)/shard_map/all_gather | solution.py:667
  460.9 11.5 %weight_grad.2 = (bf16[1,688,512]{2,1,0:T(8,128)(2,1)}, bf16[1,688,512]{2,1,0:T(8,128)(2,1)}, bf16[1,688,512]{2,1,0:T(8,128)(2,1)}, bf16[1,688,512]{2,1,0:T(8,128)(2,1)}) custom-call(s32[4]{0:T(128)} %pad_add_fusion.blocks_ref, bf16[688,1024]{1,0:T(8,128)(2,1)} %get-tuple-element.155.refs_0_, bf16[688,1024]{1,0:T(8,128)(2,1)} %get-tuple-element.156.refs_1_, ...), custom_call_target="tpu_custom_call" | custom-call | flops 199999995904 | bytes 1024 | tf_op jit(solution)/shard_map/weight_grad/pallas_call | solution.py:360
  475.4 22.8 %glu_backward.3 = (bf16[688,1024]{1,0:T(8,128)(2,1)}, bf16[688,1024]{1,0:T(8,128)(2,1)}, f32[688,1]{1,0:T(8,128)}, f32[688,1]{1,0:T(8,128)}, bf16[1024,2048]{1,0:T(8,128)(2,1)}) custom-call(s32[1]{0:T(128)} %bitcast.14.live_ref, bf16[1024,2048]{1,0:T(8,128)(2,1)} %all-gather.18.cloned.1.call-done.refs_3_.g_ref, bf16[688,2048]{1,0:T(8,128)(2,1)} %bitcast.231, ...), custom_call_target="tpu_custom_call" | custom-call | flops 199999995904 | bytes 1024 | tf_op jit(solution)/shard_map/glu_backward/pallas_call | solution.py:321
  506.0 19.2 %weight_grad.3 = (bf16[2,688,512]{2,1,0:T(8,128)(2,1)}, bf16[2,688,512]{2,1,0:T(8,128)(2,1)}, bf16[2,688,512]{2,1,0:T(8,128)(2,1)}, bf16[2,688,512]{2,1,0:T(8,128)(2,1)}) custom-call(s32[4]{0:T(128)} %pad_add_fusion.blocks_ref, bf16[688,1024]{1,0:T(8,128)(2,1)} %get-tuple-element.164.refs_0_, bf16[688,1024]{1,0:T(8,128)(2,1)} %get-tuple-element.165.refs_1_, ...), custom_call_target="tpu_custom_call" | custom-call | flops 199999995904 | bytes 1024 | tf_op jit(solution)/shard_map/weight_grad/pallas_call | solution.py:360
  534.8 3.1 convolution_convert_fusion.1
  538.7 3.5 all-to-all-start.2
  544.1 20.9 %collective-permute-done.7 = bf16[688,256]{1,0:T(8,128)(2,1)S(1)} collective-permute-done((bf16[688,256]{1,0:T(8,128)(2,1)S(1)}, bf16[688,256]{1,0:T(8,128)(2,1)S(1)}, u32[]{:S(2)}, u32[]{:S(2)}) %collective-permute-start.7) | collective-permute-done | bytes 352288 | tf_op jit(solution)/shard_map/ppermute | solution.py:455
  572.0 19.5 %attend_backward.2 = (bf16[3,1024,256]{2,1,0:T(8,128)(2,1)}, f32[3,1,256]{2,1,0:T(1,128)}, bf16[1024,2048]{1,0:T(8,128)(2,1)}) custom-call(bf16[6,1024,128]{2,1,0:T(8,128)(2,1)} %get-tuple-element.149.qkv_ref, bf16[1024,256]{1,0:T(8,128)(2,1)} %bitcast.186, f32[2,4,1,256]{3,2,1,0:T(1,128)} %get-tuple-element.173.lse_ref, s32[4,1,256]{2,1,0:T(1,128)} %bitcast.208, ...), custom_call_target="tpu_custom_call" | custom-call | flops 199999995904 | bytes 1024 | tf_op jit(solution)/shard_map/attend_backward/pallas_call | solution.py:198
  603.1 3.1 convolution_convert_fusion
  607.0 4.2 all-to-all-start.3
  621.3 8.5 row_grad.1
  629.8 5.6 all-to-all-done.3
  635.3 19.2 %attend_backward.3 = (bf16[3,1024,256]{2,1,0:T(8,128)(2,1)}, f32[3,1,256]{2,1,0:T(1,128)}, bf16[1024,2048]{1,0:T(8,128)(2,1)}) custom-call(bf16[6,1024,128]{2,1,0:T(8,128)(2,1)} %get-tuple-element.175.qkv_ref, bf16[1024,256]{1,0:T(8,128)(2,1)} %bitcast.43.grad_ref, f32[2,4,1,256]{3,2,1,0:T(1,128)} %get-tuple-element.185.lse_ref, s32[4,1,256]{2,1,0:T(1,128)} %bitcast.204, ...), custom_call_target="tpu_custom_call" | custom-call | flops 199999995904 | bytes 1024 | tf_op jit(solution)/shard_map/attend_backward/pallas_call | solution.py:198
  664.7 4.3 add_convert_fusion
  673.9 12.8 %slab_grad.1 = (bf16[3,512,256]{2,1,0:T(8,128)(2,1)}, bf16[3,512,256]{2,1,0:T(8,128)(2,1)}, bf16[3,512,256]{2,1,0:T(8,128)(2,1)}, bf16[3,512,256]{2,1,0:T(8,128)(2,1)}) custom-call(s32[4]{0:T(128)} %pad_add_fusion.blocks_ref, bf16[1024,2048]{1,0:T(8,128)(2,1)} %bitcast.221, bf16[1024,2048]{1,0:T(8,128)(2,1)} %bitcast.223, ...), custom_call_target="tpu_custom_call" | custom-call | flops 199999995904 | bytes 1024 | tf_op jit(solution)/shard_map/slab_grad/pallas_call | solution.py:395
  686.7 5.3 collective-permute-done.50
  703.1 5.3 slice_bitcast_fusion
  712.5 14.3 %collective-permute-done.16 = bf16[2048,256]{1,0:T(8,128)(2,1)} collective-permute-done((bf16[2048,256]{1,0:T(8,128)(2,1)}, bf16[2048,256]{1,0:T(8,128)(2,1)}, u32[]{:S(2)}, u32[]{:S(2)}) %collective-permute-start.16) | collective-permute-done | bytes 1048608 | tf_op jit(solution)/shard_map/ppermute | solution.py:455
  732.7 10.9 %collective-permute-done.29 = bf16[3,512,256]{2,1,0:T(8,128)(2,1)S(1)} collective-permute-done((bf16[3,512,256]{2,1,0:T(8,128)(2,1)}, bf16[3,512,256]{2,1,0:T(8,128)(2,1)S(1)}, u32[]{:S(2)}, u32[]{:S(2)}) %collective-permute-start.29) | collective-permute-done | bytes 786464 | tf_op jit(solution)/shard_map/ppermute | solution.py:455
  748.0 6.7 collective-permute-done.15
  760.7 3.9 collective-permute-start.19
  764.6 3.7 collective-permute-start.24
  769.7 5.5 collective-permute-start.22
  779.1 4.5 collective-permute-start.28
  785.3 6.3 collective-permute-done.31
  791.7 3.9 collective-permute-start.35
  802.0 14.2 %collective-permute-done.43 = bf16[256,128]{1,0:T(8,128)(2,1)S(1)} collective-permute-done((bf16[256,128]{1,0:T(8,128)(2,1)S(1)}, bf16[256,128]{1,0:T(8,128)(2,1)S(1)}, u32[]{:S(2)}, u32[]{:S(2)}) %collective-permute-start.43) | collective-permute-done | bytes 65568 | tf_op jit(solution)/shard_map/ppermute | solution.py:455
  822.5 9.3 %collective-permute-done.52 = f32[1376]{0:T(1024)S(1)} collective-permute-done((f32[1376]{0:T(1024)S(1)}, f32[1376]{0:T(1024)S(1)}, u32[]{:S(2)}, u32[]{:S(2)}) %collective-permute-start.52) | collective-permute-done | bytes 5536 | tf_op jit(solution)/shard_map/ppermute | solution.py:455
  844.8 2.9 convert_bitcast_fusion
  (556 shorter events, 192.2 us)
Async XLA Ops:
  7.2 34.8 %all-gather.10.cloned.1.call-start = ((), (), s32[]{:S(2)}) async-start(), calls=%async_computation.10 | async-start | bytes 2359296 | tf_op jit(solution)/shard_map/all_gather | solution.py:667
  9.7 81.2 %all-gather.20.cloned.1.call-start = ((), (), s32[]{:S(2)}) async-start(), calls=%async_computation.21 | async-start | bytes 4718592 | tf_op jit(solution)/shard_map/all_gather | solution.py:667
  10.8 147.0 %all-gather.22.cloned.1.call-start = ((), (), s32[]{:S(2)}) async-start(), calls=%async_computation.22 | async-start | bytes 4718592 | tf_op jit(solution)/shard_map/all_gather | solution.py:667
  58.8 49.4 %collective-permute-start.3 = (bf16[2048,256]{1,0:T(8,128)(2,1)}, bf16[2048,256]{1,0:T(8,128)(2,1)}, u32[]{:S(2)}, u32[]{:S(2)}) collective-permute-start(bf16[2048,256]{1,0:T(8,128)(2,1)} %pad_maximum_fusion.6), channel_id=1, source_target_pairs={{0,16},{8,24},{16,0},{24,8},{1,17},{9,25},{17,1},{25,9},{2,18},{10... | collective-permute-start | bytes 3145736 | tf_op jit(solution)/shard_map/ppermute | solution.py:455
  64.5 45.5 %collective-permute-start.1 = (bf16[2048,256]{1,0:T(8,128)(2,1)}, bf16[2048,256]{1,0:T(8,128)(2,1)}, u32[]{:S(2)}, u32[]{:S(2)}) collective-permute-start(bf16[2048,256]{1,0:T(8,128)(2,1)} %pad_maximum_fusion.5), channel_id=1, source_target_pairs={{0,8},{8,0},{16,24},{24,16},{1,9},{9,1},{17,25},{25,17},{2,10},{10... | collective-permute-start | bytes 3145736 | tf_op jit(solution)/shard_map/ppermute | solution.py:455
  114.1 33.8 %collective-permute-start.4 = (bf16[2048,1024]{1,0:T(8,128)(2,1)}, bf16[2048,1024]{1,0:T(8,128)(2,1)}, u32[]{:S(2)}, u32[]{:S(2)}) collective-permute-start(bf16[2048,1024]{1,0:T(8,128)(2,1)} %pad_maximum_fusion.1), channel_id=1, source_target_pairs={{0,1},{1,0},{2,3},{3,2},{4,5},{5,4},{6,7},{7,6},{8,9},{9,8},{10,11... | collective-permute-start | bytes 12582920 | tf_op jit(solution)/shard_map/ppermute | solution.py:455
  114.3 32.5 %all-to-all-start = ((bf16[8,128,256]{2,1,0:T(8,128)(2,1)}), bf16[8,128,256]{2,1,0:T(8,128)(2,1)}, u32[]{:S(2)}, u32[]{:S(2)}) async-start(bf16[8,128,256]{2,1,0:T(8,128)(2,1)} %bitcast.187), calls=%async_computation | async-start | bytes 1048576 | tf_op jit(solution)/shard_map/all_to_all | solution.py:742
  118.4 97.3 %all-gather.12.cloned.1.call-start = ((), (), s32[]{:S(2)}) async-start(), calls=%async_computation.11 | async-start | bytes 4718592 | tf_op jit(solution)/shard_map/all_gather | solution.py:667
  175.1 33.2 %all-to-all-start.1 = ((bf16[8,128,256]{2,1,0:T(8,128)(2,1)}), bf16[8,128,256]{2,1,0:T(8,128)(2,1)S(1)}, u32[]{:S(2)}, u32[]{:S(2)}) async-start(bf16[8,128,256]{2,1,0:T(8,128)(2,1)} %bitcast.188), calls=%async_computation.1 | async-start | bytes 1048576 | tf_op jit(solution)/shard_map/all_to_all | solution.py:742
  178.8 84.1 %all-gather.14.cloned.1.call-start = ((), (), s32[]{:S(2)}) async-start(), calls=%async_computation.13 | async-start | bytes 4718592 | tf_op jit(solution)/shard_map/all_gather | solution.py:667
  215.7 98.6 %reduce-scatter.7.cloned.1.call-start = ((), (), s32[]{:S(2)}) async-start(), calls=%async_computation.12 | async-start | bytes 4718592 | tf_op jit(solution)/shard_map/reduce_scatter | solution.py:670
  232.7 132.6 %reduce-scatter.9.cloned.1.call-start = ((), (), s32[]{:S(2)}) async-start(), calls=%async_computation.14 | async-start | bytes 4718592 | tf_op jit(solution)/shard_map/reduce_scatter | solution.py:670
  279.9 132.9 %all-gather.16.cloned.1.call-start = ((), (), s32[]{:S(2)}) async-start(), calls=%async_computation.15 | async-start | bytes 4718592 | tf_op jit(solution)/shard_map/all_gather | solution.py:667
  319.3 141.7 %all-gather.18.cloned.1.call-start = ((), (), s32[]{:S(2)}) async-start(), calls=%async_computation.17 | async-start | bytes 4718592 | tf_op jit(solution)/shard_map/all_gather | solution.py:667
  371.2 158.5 %reduce-scatter.11.cloned.1.call-start = ((), (), s32[]{:S(2)}) async-start(), calls=%async_computation.16 | async-start | bytes 4718592 | tf_op jit(solution)/shard_map/reduce_scatter | solution.py:670
  435.5 162.8 %reduce-scatter.15.cloned.1.call-start = ((), (), s32[]{:S(2)}) async-start(), calls=%async_computation.19 | async-start | bytes 4718592 | tf_op jit(solution)/shard_map/reduce_scatter | solution.py:670
  472.5 28.0 %collective-permute-start.5 = (bf16[688,512]{1,0:T(8,128)(2,1)}, bf16[688,512]{1,0:T(8,128)(2,1)}, u32[]{:S(2)}, u32[]{:S(2)}) collective-permute-start(bf16[688,512]{1,0:T(8,128)(2,1)} %bitcast.237), channel_id=1, source_target_pairs={{0,8},{8,0},{16,24},{24,16},{1,9},{9,1},{17,25},{25,17},{2,10},{10... | collective-permute-start | bytes 2113544 | tf_op jit(solution)/shard_map/ppermute | solution.py:455
  473.9 29.2 %collective-permute-start.54 = (bf16[688,512]{1,0:T(8,128)(2,1)}, bf16[688,512]{1,0:T(8,128)(2,1)}, u32[]{:S(2)}, u32[]{:S(2)}) collective-permute-start(bf16[688,512]{1,0:T(8,128)(2,1)} %bitcast.236), channel_id=1, source_target_pairs={{0,16},{8,24},{16,0},{24,8},{1,17},{9,25},{17,1},{25,9},{2,18},{10... | collective-permute-start | bytes 2113544 | tf_op jit(solution)/shard_map/ppermute | solution.py:455
  502.6 25.5 %collective-permute-start.6 = (bf16[688,256]{1,0:T(8,128)(2,1)}, bf16[688,256]{1,0:T(8,128)(2,1)}, u32[]{:S(2)}, u32[]{:S(2)}) collective-permute-start(bf16[688,256]{1,0:T(8,128)(2,1)} %constant_dynamic-slice_fusion.11), channel_id=1, source_target_pairs={{0,16},{8,24},{16,0},{24,8},{1,17},{9,25},{17,1},{25,9},{2,18},{10... | collective-permute-start | bytes 1056776 | tf_op jit(solution)/shard_map/ppermute | solution.py:455
  505.3 24.4 %collective-permute-start.55 = (bf16[688,256]{1,0:T(8,128)(2,1)}, bf16[688,256]{1,0:T(8,128)(2,1)}, u32[]{:S(2)}, u32[]{:S(2)}) collective-permute-start(bf16[688,256]{1,0:T(8,128)(2,1)} %constant_dynamic-slice_fusion.1), channel_id=1, source_target_pairs={{0,8},{8,0},{16,24},{24,16},{1,9},{9,1},{17,25},{25,17},{2,10},{10... | collective-permute-start | bytes 1056776 | tf_op jit(solution)/shard_map/ppermute | solution.py:455
  525.2 66.3 %collective-permute-start.47 = (bf16[2,688,512]{2,1,0:T(8,128)(2,1)}, bf16[2,688,512]{2,1,0:T(8,128)(2,1)}, u32[]{:S(2)}, u32[]{:S(2)}) collective-permute-start(bf16[2,688,512]{2,1,0:T(8,128)(2,1)} %get-tuple-element.236), channel_id=1, source_target_pairs={{0,16},{8,24},{16,0},{24,8},{1,17},{9,25},{17,1},{25,9},{2,18},{10... | collective-permute-start | bytes 4227080 | tf_op jit(solution)/shard_map/ppermute | solution.py:455
  526.6 64.9 %collective-permute-start.8 = (bf16[2,688,512]{2,1,0:T(8,128)(2,1)}, bf16[2,688,512]{2,1,0:T(8,128)(2,1)}, u32[]{:S(2)}, u32[]{:S(2)}) collective-permute-start(bf16[2,688,512]{2,1,0:T(8,128)(2,1)} %get-tuple-element.168), channel_id=1, source_target_pairs={{0,8},{8,0},{16,24},{24,16},{1,9},{9,1},{17,25},{25,17},{2,10},{10... | collective-permute-start | bytes 4227080 | tf_op jit(solution)/shard_map/ppermute | solution.py:455
  529.2 35.7 %collective-permute-start.7 = (bf16[688,256]{1,0:T(8,128)(2,1)S(1)}, bf16[688,256]{1,0:T(8,128)(2,1)S(1)}, u32[]{:S(2)}, u32[]{:S(2)}) collective-permute-start(bf16[688,256]{1,0:T(8,128)(2,1)S(1)} %add_convert_fusion.16), channel_id=1, source_target_pairs={{0,16},{8,24},{16,0},{24,8},{1,17},{9,25},{17,1},{25,9},{2,18},{10... | collective-permute-start | bytes 1056776 | tf_op jit(solution)/shard_map/ppermute | solution.py:455
  538.7 32.6 %all-to-all-start.2 = ((bf16[128,8,256]{2,0,1:T(8,128)(2,1)}), bf16[128,8,256]{2,0,1:T(8,128)(2,1)S(1)}, u32[]{:S(2)}, u32[]{:S(2)}) async-start(bf16[128,8,256]{2,0,1:T(8,128)(2,1)} %bitcast.168), calls=%async_computation.5 | async-start | bytes 1048576 | tf_op jit(solution)/shard_map/all_to_all | solution.py:834
  542.2 305.5 %reduce-scatter.13.cloned.1.call-start = ((), (), s32[]{:S(2)}) async-start(), calls=%async_computation.18 | async-start | bytes 4718592 | tf_op jit(solution)/shard_map/reduce_scatter | solution.py:670
  543.3 24.8 %collective-permute-start.56 = (bf16[688,256]{1,0:T(8,128)(2,1)S(1)}, bf16[688,256]{1,0:T(8,128)(2,1)S(1)}, u32[]{:S(2)}, u32[]{:S(2)}) collective-permute-start(bf16[688,256]{1,0:T(8,128)(2,1)S(1)} %add_convert_fusion.15), channel_id=1, source_target_pairs={{0,8},{8,0},{16,24},{24,16},{1,9},{9,1},{17,25},{25,17},{2,10},{10... | collective-permute-start | bytes 1056776 | tf_op jit(solution)/shard_map/ppermute | solution.py:455
  566.6 143.5 %collective-permute-start.53 = (bf16[688,512]{1,0:T(8,128)(2,1)}, bf16[688,512]{1,0:T(8,128)(2,1)}, u32[]{:S(2)}, u32[]{:S(2)}) collective-permute-start(bf16[688,512]{1,0:T(8,128)(2,1)} %pad_maximum_fusion.13), channel_id=1, source_target_pairs={{0,8},{8,0},{16,24},{24,16},{1,9},{9,1},{17,25},{25,17},{2,10},{10... | collective-permute-start | bytes 2113544 | tf_op jit(solution)/shard_map/ppermute | solution.py:455
  569.8 138.6 %collective-permute-start.57 = (bf16[688,512]{1,0:T(8,128)(2,1)}, bf16[688,512]{1,0:T(8,128)(2,1)}, u32[]{:S(2)}, u32[]{:S(2)}) collective-permute-start(bf16[688,512]{1,0:T(8,128)(2,1)} %pad_maximum_fusion.14), channel_id=1, source_target_pairs={{0,16},{8,24},{16,0},{24,8},{1,17},{9,25},{17,1},{25,9},{2,18},{10... | collective-permute-start | bytes 2113544 | tf_op jit(solution)/shard_map/ppermute | solution.py:455
  597.7 20.0 %collective-permute-start.9 = (bf16[2,688,256]{2,1,0:T(8,128)(2,1)}, bf16[2,688,256]{2,1,0:T(8,128)(2,1)}, u32[]{:S(2)}, u32[]{:S(2)}) collective-permute-start(bf16[2,688,256]{2,1,0:T(8,128)(2,1)} %constant_dynamic-slice_fusion.10), channel_id=1, source_target_pairs={{0,16},{8,24},{16,0},{24,8},{1,17},{9,25},{17,1},{25,9},{2,18},{10... | collective-permute-start | bytes 2113544 | tf_op jit(solution)/shard_map/ppermute | solution.py:455
  607.0 28.3 %all-to-all-start.3 = ((bf16[128,8,256]{2,0,1:T(8,128)(2,1)}), bf16[128,8,256]{2,0,1:T(8,128)(2,1)}, u32[]{:S(2)}, u32[]{:S(2)}) async-start(bf16[128,8,256]{2,0,1:T(8,128)(2,1)} %bitcast.180), calls=%async_computation.8 | async-start | bytes 1048576 | tf_op jit(solution)/shard_map/all_to_all | solution.py:834
  611.2 237.8 %reduce-scatter.17.cloned.1.call-start = ((), (), s32[]{:S(2)}) async-start(), calls=%async_computation.20 | async-start | bytes 4718592 | tf_op jit(solution)/shard_map/reduce_scatter | solution.py:670
  616.3 40.1 %collective-permute-start.49 = (bf16[2,688,256]{2,1,0:T(8,128)(2,1)}, bf16[2,688,256]{2,1,0:T(8,128)(2,1)}, u32[]{:S(2)}, u32[]{:S(2)}) collective-permute-start(bf16[2,688,256]{2,1,0:T(8,128)(2,1)} %add_convert_fusion.7), channel_id=1, source_target_pairs={{0,8},{8,0},{16,24},{24,16},{1,9},{9,1},{17,25},{25,17},{2,10},{10... | collective-permute-start | bytes 2113544 | tf_op jit(solution)/shard_map/ppermute | solution.py:455
  620.0 36.5 %collective-permute-start.11 = (bf16[2,688,256]{2,1,0:T(8,128)(2,1)}, bf16[2,688,256]{2,1,0:T(8,128)(2,1)}, u32[]{:S(2)}, u32[]{:S(2)}) collective-permute-start(bf16[2,688,256]{2,1,0:T(8,128)(2,1)} %add_convert_fusion.8), channel_id=1, source_target_pairs={{0,16},{8,24},{16,0},{24,8},{1,17},{9,25},{17,1},{25,9},{2,18},{10... | collective-permute-start | bytes 2113544 | tf_op jit(solution)/shard_map/ppermute | solution.py:455
  629.8 35.0 %collective-permute-start.10 = (bf16[2048,1024]{1,0:T(8,128)(2,1)}, bf16[2048,1024]{1,0:T(8,128)(2,1)}, u32[]{:S(2)}, u32[]{:S(2)}) collective-permute-start(bf16[2048,1024]{1,0:T(8,128)(2,1)} %get-tuple-element.183), channel_id=1, source_target_pairs={{0,1},{1,0},{2,3},{3,2},{4,5},{5,4},{6,7},{7,6},{8,9},{9,8},{10,11... | collective-permute-start | bytes 12582920 | tf_op jit(solution)/shard_map/ppermute | solution.py:455
  659.2 32.8 %collective-permute-start.50 = (bf16[2,688,512]{2,1,0:T(8,128)(2,1)}, bf16[2,688,512]{2,1,0:T(8,128)(2,1)}, u32[]{:S(2)}, u32[]{:S(2)}) collective-permute-start(bf16[2,688,512]{2,1,0:T(8,128)(2,1)} %pad_maximum_fusion.4), channel_id=1, source_target_pairs={{0,16},{8,24},{16,0},{24,8},{1,17},{9,25},{17,1},{25,9},{2,18},{10... | collective-permute-start | bytes 4227080 | tf_op jit(solution)/shard_map/ppermute | solution.py:455
  663.3 34.1 %collective-permute-start.46 = (bf16[2,688,512]{2,1,0:T(8,128)(2,1)}, bf16[2,688,512]{2,1,0:T(8,128)(2,1)}, u32[]{:S(2)}, u32[]{:S(2)}) collective-permute-start(bf16[2,688,512]{2,1,0:T(8,128)(2,1)} %pad_maximum_fusion.3), channel_id=1, source_target_pairs={{0,8},{8,0},{16,24},{24,16},{1,9},{9,1},{17,25},{25,17},{2,10},{10... | collective-permute-start | bytes 4227080 | tf_op jit(solution)/shard_map/ppermute | solution.py:455
  673.0 56.9 %collective-permute-start.13 = (bf16[2048,256]{1,0:T(8,128)(2,1)}, bf16[2048,256]{1,0:T(8,128)(2,1)}, u32[]{:S(2)}, u32[]{:S(2)}) collective-permute-start(bf16[2048,256]{1,0:T(8,128)(2,1)} %constant_dynamic-slice_fusion.9), channel_id=1, source_target_pairs={{0,8},{8,0},{16,24},{24,16},{1,9},{9,1},{17,25},{25,17},{2,10},{10... | collective-permute-start | bytes 3145736 | tf_op jit(solution)/shard_map/ppermute | solution.py:455
  692.0 51.5 %collective-permute-start.12 = (bf16[3,512,256]{2,1,0:T(8,128)(2,1)}, bf16[3,512,256]{2,1,0:T(8,128)(2,1)}, u32[]{:S(2)}, u32[]{:S(2)}) collective-permute-start(bf16[3,512,256]{2,1,0:T(8,128)(2,1)} %get-tuple-element.194), channel_id=1, source_target_pairs={{0,8},{8,0},{16,24},{24,16},{1,9},{9,1},{17,25},{25,17},{2,10},{10... | collective-permute-start | bytes 2359304 | tf_op jit(solution)/shard_map/ppermute | solution.py:455
  700.4 26.4 %collective-permute-start.16 = (bf16[2048,256]{1,0:T(8,128)(2,1)}, bf16[2048,256]{1,0:T(8,128)(2,1)}, u32[]{:S(2)}, u32[]{:S(2)}) collective-permute-start(bf16[2048,256]{1,0:T(8,128)(2,1)} %constant_dynamic-slice_fusion.6), channel_id=1, source_target_pairs={{0,16},{8,24},{16,0},{24,8},{1,17},{9,25},{17,1},{25,9},{2,18},{10... | collective-permute-start | bytes 3145736 | tf_op jit(solution)/shard_map/ppermute | solution.py:455
  710.2 33.4 %collective-permute-start.29 = (bf16[3,512,256]{2,1,0:T(8,128)(2,1)}, bf16[3,512,256]{2,1,0:T(8,128)(2,1)S(1)}, u32[]{:S(2)}, u32[]{:S(2)}) collective-permute-start(bf16[3,512,256]{2,1,0:T(8,128)(2,1)} %get-tuple-element.214), channel_id=1, source_target_pairs={{0,16},{8,24},{16,0},{24,8},{1,17},{9,25},{17,1},{25,9},{2,18},{10... | collective-permute-start | bytes 2359304 | tf_op jit(solution)/shard_map/ppermute | solution.py:455
  731.5 23.3 %collective-permute-start.15 = (bf16[2048,128]{1,0:T(8,128)(2,1)S(1)}, bf16[2048,128]{1,0:T(8,128)(2,1)S(1)}, u32[]{:S(2)}, u32[]{:S(2)}) collective-permute-start(bf16[2048,128]{1,0:T(8,128)(2,1)S(1)} %constant_dynamic-slice_fusion.8), channel_id=1, source_target_pairs={{0,16},{8,24},{16,0},{24,8},{1,17},{9,25},{17,1},{25,9},{2,18},{10... | collective-permute-start | bytes 1572872 | tf_op jit(solution)/shard_map/ppermute | solution.py:455
  746.4 21.9 %collective-permute-start.30 = (bf16[3,256,256]{2,1,0:T(8,128)(2,1)S(1)}, bf16[3,256,256]{2,1,0:T(8,128)(2,1)S(1)}, u32[]{:S(2)}, u32[]{:S(2)}) collective-permute-start(bf16[3,256,256]{2,1,0:T(8,128)(2,1)S(1)} %constant_dynamic-slice_fusion.3), channel_id=1, source_target_pairs={{0,8},{8,0},{16,24},{24,16},{1,9},{9,1},{17,25},{25,17},{2,10},{10... | collective-permute-start | bytes 1179656 | tf_op jit(solution)/shard_map/ppermute | solution.py:455
  760.7 22.9 %collective-permute-start.19 = (bf16[512,256]{1,0:T(8,128)(2,1)S(1)}, bf16[512,256]{1,0:T(8,128)(2,1)S(1)}, u32[]{:S(2)}, u32[]{:S(2)}) collective-permute-start(bf16[512,256]{1,0:T(8,128)(2,1)S(1)} %get-tuple-element.323), channel_id=1, source_target_pairs={{0,2},{1,3},{2,4},{3,5},{4,6},{5,7},{8,10},{9,11},{10,12},{11,13},... | collective-permute-start | bytes 786440 | tf_op jit(solution)/shard_map/ppermute | solution.py:659
  776.6 41.1 %collective-permute-start.51 = (f32[1376]{0:T(1024)S(1)}, f32[1376]{0:T(1024)S(1)}, u32[]{:S(2)}, u32[]{:S(2)}) collective-permute-start(f32[1376]{0:T(1024)S(1)} %copy-done.109), channel_id=1, source_target_pairs={{0,8},{8,0},{16,24},{24,16},{1,9},{9,1},{17,25},{25,17},{2,10},{10... | collective-permute-start | bytes 16520 | tf_op jit(solution)/shard_map/ppermute | solution.py:455
  777.9 40.4 %collective-permute-start.33 = (f32[3,256]{1,0:T(4,128)S(1)}, f32[3,256]{1,0:T(4,128)S(1)}, u32[]{:S(2)}, u32[]{:S(2)}) collective-permute-start(f32[3,256]{1,0:T(4,128)S(1)} %bitcast.217), channel_id=1, source_target_pairs={{0,8},{8,0},{16,24},{24,16},{1,9},{9,1},{17,25},{25,17},{2,10},{10... | collective-permute-start | bytes 9224 | tf_op jit(solution)/shard_map/ppermute | solution.py:455
  798.2 46.0 %collective-permute-start.26 = (bf16[3,512,256]{2,1,0:T(8,128)(2,1)S(1)}, bf16[3,512,256]{2,1,0:T(8,128)(2,1)S(1)}, u32[]{:S(2)}, u32[]{:S(2)}) collective-permute-start(bf16[3,512,256]{2,1,0:T(8,128)(2,1)S(1)} %pad_maximum_fusion.11), channel_id=1, source_target_pairs={{0,8},{8,0},{16,24},{24,16},{1,9},{9,1},{17,25},{25,17},{2,10},{10... | collective-permute-start | bytes 2359304 | tf_op jit(solution)/shard_map/ppermute | solution.py:455
  816.2 27.9 %collective-permute-start.32 = (bf16[3,512,256]{2,1,0:T(8,128)(2,1)S(1)}, bf16[3,512,256]{2,1,0:T(8,128)(2,1)S(1)}, u32[]{:S(2)}, u32[]{:S(2)}) collective-permute-start(bf16[3,512,256]{2,1,0:T(8,128)(2,1)S(1)} %pad_maximum_fusion.12), channel_id=1, source_target_pairs={{0,16},{8,24},{16,0},{24,8},{1,17},{9,25},{17,1},{25,9},{2,18},{10... | collective-permute-start | bytes 2359304 | tf_op jit(solution)/shard_map/ppermute | solution.py:455
  817.7 23.3 %collective-permute-start.38 = (bf16[256,256]{1,0:T(8,128)(2,1)S(1)}, bf16[256,256]{1,0:T(8,128)(2,1)S(1)}, u32[]{:S(2)}, u32[]{:S(2)}) collective-permute-start(bf16[256,256]{1,0:T(8,128)(2,1)S(1)} %pad_maximum_fusion.20), channel_id=1, source_target_pairs={{0,8},{8,0},{16,24},{24,16},{1,9},{9,1},{17,25},{25,17},{2,10},{10... | collective-permute-start | bytes 393224 | tf_op jit(solution)/shard_map/ppermute | solution.py:455
  (151 other events, 1693.9 us)
Sparse Core Ops, SparseCore 0:
  10.2 31.7 all-gather.9
  44.2 46.6 all-gather.19
  93.1 56.9 all-gather.21
  157.9 57.0 all-gather.11
  217.0 45.7 all-gather.13
  265.6 48.7 reduce-scatter.6
  317.2 48.1 reduce-scatter.8
  367.5 45.2 all-gather.15
  415.0 45.8 all-gather.17
  463.6 48.6 reduce-scatter.10
  515.2 56.5 reduce-scatter.14
  598.4 56.8 reduce-scatter.12
  657.6 50.7 reduce-scatter.16

commit v3 on v2

--- a/solution.py
+++ b/solution.py
@@ -22,6 +22,7 @@
 ROW_TILE = 256
 VMEM_LIMIT = 56 * 1024 * 1024
 LONG = pl.CostEstimate(flops=200_000_000_000, bytes_accessed=1024, transcendentals=0)
+SHORT = pl.CostEstimate(flops=1024, bytes_accessed=1024, transcendentals=0)
 BF16 = jnp.bfloat16
 F32 = jnp.float32
 
@@ -189,7 +190,7 @@
     x_grad_ref[...] = total.astype(BF16)
 
 
-def attend_backward(qkv, grad, lse, lo, hi, cosine, sine, w):
+def attend_backward(qkv, grad, lse, lo, hi, cosine, sine, w, cost):
     width, head_width = w.shape[1:]
     length = grad.shape[0]
     heads = head_width // HEAD_DIM
@@ -223,7 +224,7 @@
             pltpu.VMEM((length, HEAD_DIM), F32),
         ],
         compiler_params=pltpu.CompilerParams(vmem_limit_bytes=VMEM_LIMIT),
-        cost_estimate=LONG,
+        cost_estimate=cost,
         name="attend_backward",
     )(qkv, grad, lse, lo, hi, cosine, sine, w)
 
@@ -403,43 +404,72 @@
         ),
         out_shape=[jax.ShapeDtypeStruct((3, tile, columns), BF16)] * count,
         compiler_params=pltpu.CompilerParams(vmem_limit_bytes=VMEM_LIMIT),
-        cost_estimate=LONG,
+        cost_estimate=SHORT,
         name="slab_grad",
     )(blocks, *lefts, *rights)
 
 
-def row_grad_kernel(blocks_ref, left_ref, right_ref, *results):
-    depth = left_ref.shape[1]
+def row_grad_kernel(sides_ref, left_ref, right_ref, *results):
+    columns = left_ref.shape[1]
     for index, result in enumerate(results):
 
         @pl.when(pl.program_id(0) == index)
         def _():
-            for first in range(0, depth, 512):
-                result[first : first + 512, :] = dot_tn(
-                    left_ref[:, first : first + 512], right_ref[...]
-                ).astype(BF16)
-
-
-def row_grad(left, right, blocks):
+            rows = pl.ds(pl.multiple_of(pl.program_id(1) * columns, columns), columns)
+            result[rows, :] = dot_tn(left_ref[...], right_ref[...]).astype(BF16)
+
+
+def row_grad(left, right, sides, columns):
     rows, depth = left.shape
-    count = blocks.shape[0]
-    tile = right.shape[1] // count
+    width = right.shape[1]
+    count = sides.shape[0]
+    steps = depth // columns // count
     return pl.pallas_call(
         row_grad_kernel,
         grid_spec=pltpu.PrefetchScalarGridSpec(
             num_scalar_prefetch=1,
+            grid=(count, steps),
+            in_specs=[
+                pl.BlockSpec((rows, columns), lambda i, j, at: (0, count * j + at[i])),
+                pl.BlockSpec((rows, width), lambda i, j, at: (0, 0)),
+            ],
+            out_specs=[pl.BlockSpec((depth // count, width), lambda i, j, at: (0, 0))] * count,
+        ),
+        out_shape=[jax.ShapeDtypeStruct((depth // count, width), BF16)] * count,
+        compiler_params=pltpu.CompilerParams(vmem_limit_bytes=VMEM_LIMIT),
+        cost_estimate=SHORT,
+        name="row_grad",
+    )(sides, left, right)
+
+
+def assemble_kernel(dim, sources_ref, *refs):
+    pieces, result = refs[:-1], refs[-1]
+    for index, piece in enumerate(pieces):
+
+        @pl.when(sources_ref[pl.program_id(0)] == index)
+        def _():
+            result[...] = piece[...].astype(F32)
+
+
+def assemble(pieces, sources, dim, cost):
+    shape = pieces[0].shape
+    count = len(pieces)
+    whole = shape[:dim] + (shape[dim] * count,) + shape[dim + 1 :]
+    zeros = (0,) * len(shape)
+    place = lambda i, at: zeros[:dim] + (i,) + zeros[dim + 1 :]
+    return pl.pallas_call(
+        functools.partial(assemble_kernel, dim),
+        grid_spec=pltpu.PrefetchScalarGridSpec(
+            num_scalar_prefetch=1,
             grid=(count,),
-            in_specs=[
-                pl.BlockSpec((rows, depth), lambda i, at: (0, 0)),
-                pl.BlockSpec((rows, tile), lambda i, at: (0, at[i])),
-            ],
-            out_specs=[pl.BlockSpec((depth, tile), lambda i, at: (0, 0))] * count,
+            in_specs=[pl.BlockSpec(shape, lambda i, at: zeros)] * count,
+            out_specs=pl.BlockSpec(shape, place),
         ),
-        out_shape=[jax.ShapeDtypeStruct((depth, tile), BF16)] * count,
+        out_shape=jax.ShapeDtypeStruct(whole, F32),
         compiler_params=pltpu.CompilerParams(vmem_limit_bytes=VMEM_LIMIT),
-        cost_estimate=LONG,
-        name="row_grad",
-    )(blocks, left, right)
+        cost_estimate=cost,
+        name="assemble",
+    )(sources, *pieces)
 
 
 def add_low(a, b):
@@ -447,7 +477,14 @@
 
 
 def after(x, *earlier):
-    return lax.optimization_barrier((x, *earlier))[0]
+    return lax.optimization_barrier((x, *jax.tree.leaves(earlier)))[0]
+
+
+def all_after(xs, earlier):
+    earlier = jax.tree.leaves(earlier)
+    if not earlier:
+        return list(xs)
+    return list(lax.optimization_barrier((*xs, *earlier))[: len(xs)])
 
 
 def swap_bit(x, axis_name, bit):
@@ -465,17 +502,19 @@
         try:
             if self.moving is None:
                 sends = next(self.chain)
-                if earlier:
-                    sends = [(after(x, *earlier), move) for x, move in sends]
+                self.sent = all_after([x for x, _ in sends], earlier)
             else:
-                got = [after(x, *earlier) for x in self.moving] if earlier else self.moving
-                sends = self.chain.send(got)
-            self.sent = sends[0][0]
-            self.moving = [move(x) for x, move in sends]
+                sends = self.chain.send(all_after(self.moving, earlier))
+                self.sent = [x for x, _ in sends]
+            self.moving = [move(x) for x, (_, move) in zip(self.sent, sends)]
         except StopIteration as end:
             self.moving = None
             self.result = end.value
         return self
+
+    def settle(self, *earlier):
+        self.moving = all_after(self.moving, earlier)
+        return self.moving
 
     def finish(self, *earlier):
         while self.result is None:
@@ -495,7 +534,7 @@
     return jnp.stack(sends + keeps).astype(jnp.int32)
 
 
-def scatter_stages(parts, rank, orders, dim, blocks=None):
+def scatter_stages(parts, rank, orders, dim, blocks=None, axis_name="batch", first_bit=0):
     if blocks is not None:
         count = len(orders)
         got = yield [
@@ -509,7 +548,7 @@
             mine = (rank >> order[place]) & 1
             send = lax.dynamic_slice_in_dim(part, (1 - mine) * half, half, dim)
             keeps.append(lax.dynamic_slice_in_dim(part, mine * half, half, dim))
-            sends.append((send, by_bit(order[place])))
+            sends.append((send, by_bit(order[place] + first_bit, axis_name)))
         parts = [add_low(keep, got) for keep, got in zip(keeps, (yield sends))]
     return parts
 
@@ -540,23 +579,41 @@
     return [lax.slice_in_dim(x, k * size, (k + 1) * size, axis=dim) for k in range(count)]
 
 
-def sum_stages(blocks, rank, orders, dim):
+def sum_stages(blocks, rank, orders, dim, cost):
     parts = yield from scatter_stages(None, rank, orders, dim, blocks)
-    parts = yield from gather_stages(parts, rank, orders, dim)
-    return jnp.concatenate(parts, axis=dim).astype(F32)
-
-
-def line_scatter_stages(x, rank, size, shift):
-    sends = []
-    for away in range(1, size):
-        for step in (away, -away):
-            target = jnp.clip(rank + step, 0, size - 1)
-            block = lax.dynamic_index_in_dim(x, target, 0, keepdims=False)
-            sends.append((block, functools.partial(shift, step=step)))
-    total = lax.dynamic_index_in_dim(x, rank, 0, keepdims=False).astype(F32)
-    for block in (yield sends):
-        total = total + block.astype(F32)
-    return total.astype(BF16)
+    parts = yield from gather_stages(parts, rank, [order[1:] for order in orders], dim)
+    others = yield [(part, by_bit(order[0])) for part, order in zip(parts, orders)]
+    sources = []
+    for index, order in enumerate(orders):
+        bit = (rank >> order[0]) & 1
+        sources += [bit * len(orders) + index, (1 - bit) * len(orders) + index]
+    return assemble(parts + others, jnp.stack(sources).astype(jnp.int32), dim, cost)
+
+
+def to_peer(mask):
+    def move(x):
+        size = lax.axis_size("batch")
+        return lax.ppermute(x, "batch", [(i, i ^ mask) for i in range(size)])
+
+    return move
+
+
+def peer_blocks(rank, size):
+    return jnp.stack([rank ^ mask for mask in range(size)]).astype(jnp.int32)
+
+
+def direct_gather_stages(piece, rank, size, dim):
+    others = yield [(piece, to_peer(mask)) for mask in range(1, size)]
+    return assemble([piece, *others], peer_blocks(rank, size), dim, LONG)
+
+
+def direct_sum_stages(blocks, rank, size, dim):
+    got = yield [(blocks[mask], to_peer(mask)) for mask in range(1, size)]
+    total = blocks[0].astype(F32)
+    for other in got:
+        total = total + other.astype(F32)
+    result = yield from direct_gather_stages(total.astype(BF16), rank, size, dim)
+    return result
 
 
 def small_stages(everywhere, over_batch, batch_bits, tensor_bits):
@@ -564,6 +621,8 @@
         (other,) = yield [(everywhere, by_bit(bit, "tensor"))]
         everywhere = everywhere + other
     values = [everywhere, *over_batch]
+    if callable(values[-1]):
+        values = values[:-1] + [values[-1]()]
     for bit in range(batch_bits):
         others = yield [(value, by_bit(bit)) for value in values]
         values = [value + other for value, other in zip(values, others)]
@@ -649,15 +708,6 @@
     scale_value = residual_scale[0]
     across = by_bit(0, "tensor")
 
-    def shift(x, step):
-        moves = [
-            (chip * 2 + side, (chip + step) * 2 + side)
-            for chip in range(chips)
-            for side in range(2)
-            if 0 <= chip + step < chips
-        ]
-        return lax.ppermute(x, "tensor", moves)
-
     def by_core(mine, other, axis):
         return jnp.concatenate(
             [jnp.where(first_core, mine, other), jnp.where(first_core, other, mine)], axis=axis
@@ -700,19 +750,15 @@
     def out_scatter_stages(send, keep):
         (other,) = yield [(send, across)]
         total = add_low(keep, other)
-        parts = yield from scatter_stages(cut(total, len(orders), 1), batch_rank, orders, 1)
+        parts = yield from scatter_stages(
+            cut(total, len(orders), 1), batch_rank, orders, 1
+        )
         total = jnp.concatenate(parts, axis=1)
-        total = yield from line_scatter_stages(
-            total.reshape(chips, -1, total.shape[1]), chip_rank, chips, shift
-        )
-        rows = total.shape[0] // 2
-        mine = lax.dynamic_slice_in_dim(total, core * rows, rows, 0)
-        (other,) = yield [
-            (lax.dynamic_slice_in_dim(total, (1 - core) * rows, rows, 0), across)
-        ]
-        sides = [jnp.where(first_core, mine, other), jnp.where(first_core, other, mine)]
-        parts = [part for side in sides for part in cut(side, len(orders), 1)]
-        parts = yield from gather_stages(parts, batch_rank, orders * 2, 1)
+        chip_bits = list(reversed(range(chips.bit_length() - 1)))
+        (total,) = yield from scatter_stages(
+            [total], chip_rank, [chip_bits], 0, axis_name="tensor", first_bit=1
+        )
+        parts = yield from gather_stages(cut(total, len(orders), 1), batch_rank, orders, 1)
         return jnp.concatenate(parts, axis=1).astype(F32)
 
     tables = [rotary_tables(rotary_positions[p]) for p in range(packs)]
@@ -726,9 +772,8 @@
     for p in range(packs):
         whole_tokens.append(gather_rows(tokens[p]))
     out_flow = Flow(out_gather_stages(out_piece))
-    for _ in range(len(orders[0])):
-        out_flow.step()
-    last = out_flow.sent
+    whole_out = out_flow.finish()
+    last = whole_out
 
     qkvs, log_sums, context_rows = [], [], []
     normed, normal_one, inverse_one, hidden = [], [], [], []
@@ -741,9 +786,6 @@
         context_rows.append(
             lax.all_to_all(context, "tensor", split_axis=0, concat_axis=1, tiled=True)
         )
-        if p == 0:
-            out_flow.step(context)
-            whole_out = out_flow.finish()
         attended = dot_nn(context_rows[p], whole_out) + out_bias
         value, normal, inverse = norm_forward(
             scale_value * tokens[p].astype(F32) + attended, norm_gain, norm_shift
@@ -794,7 +836,7 @@
                 [[after(act, last)] for act in activated], branch_grads, blocks
             )
             down_flow = Flow(
-                sum_stages([block[0] for block in down_blocks], batch_rank, orders, 1)
+                sum_stages([block[0] for block in down_blocks], batch_rank, orders, 1, LONG)
             ).step()
             last = down_flow.sent
         gate_low, up_low, gate_sum, up_sum, normed_part = glu_backward(
@@ -811,7 +853,7 @@
     glu_blocks = weight_grad(
         [[after(gate, last), up] for gate, up in zip(gate_lows, up_lows)], hidden, blocks
     )
-    glu_flow = Flow(sum_stages(glu_blocks, batch_rank, orders, 2)).step()
+    glu_flow = Flow(sum_stages(glu_blocks, batch_rank, orders, 2, SHORT)).step()
     down_flow.step(glu_flow.sent)
     last = down_flow.sent
 
@@ -835,14 +877,16 @@
             context_grad, "tensor", split_axis=1, concat_axis=0, tiled=True
         )
         if p == packs - 1:
-            glu_flow.step(last)
+            last = glu_flow.step(last).sent
+            last = down_flow.step(last).result
             send, keep = row_grad(
-                after(jnp.concatenate(context_rows, axis=0), glu_flow.sent),
+                after(jnp.concatenate(context_rows, axis=0), last),
                 jnp.concatenate(attended_lows, axis=0),
                 jnp.stack([1 - core, core]).astype(jnp.int32),
+                out_weight.shape[0],
             )
             out_flow = Flow(out_scatter_stages(send, keep)).step()
-            last = out_flow.sent
+            last = send
             shared = jnp.stack(
                 [
                     out_bias_part,
@@ -853,10 +897,21 @@
                     final_shift_part,
                 ]
             )
+            glu_bias = jnp.concatenate([gate_bias_part[:, 0], up_bias_part[:, 0]])
+            small_flow = Flow(
+                small_stages(
+                    shared,
+                    (glu_bias, lambda: qkv_bias_part[:, 0, :]),
+                    batch_size.bit_length() - 1,
+                    tensor_size.bit_length() - 1,
+                )
+            ).step(send)
         else:
-            last = down_flow.step(last).sent
+            down_flow.step(last)
+            last = glu_flow.step(down_flow.sent, context_grad).sent
         low, bias_sum, input_part = attend_backward(
-            qkvs[p], after(context_grad, last), log_sums[p], *ranges[p], *tables[p], qkv_slabs
+            qkvs[p], after(context_grad, last), log_sums[p], *ranges[p], *tables[p], qkv_slabs,
+            LONG if p < packs - 1 else SHORT,
         )
         last = low
         lows.append(low)
@@ -864,30 +919,24 @@
         input_grads.append(
             scatter_rows(input_part).astype(F32) + scale_value * grads_one[p]
         )
-        glu_flow.step(last)
-        last = glu_flow.sent
         if p == packs - 1:
-            last = out_flow.step(last).sent
-    qkv_blocks = slab_grad(whole_tokens, [after(low, last) for low in lows], blocks)
-    qkv_flow = Flow(sum_stages(qkv_blocks, batch_rank, orders, 1)).step()
+            last = [out_flow.step(low).sent, small_flow.step(low).sent, glu_flow.settle(low)]
+        else:
+            last = glu_flow.step(last).sent
+    qkv_blocks = slab_grad(
+        whole_tokens, [after(low, last) for low in lows], peer_blocks(batch_rank, batch_size)
+    )
+    qkv_flow = Flow(direct_sum_stages(qkv_blocks, batch_rank, batch_size, 1)).step()
     last = qkv_flow.sent
-    glu_bias = jnp.concatenate([gate_bias_part[:, 0], up_bias_part[:, 0]])
-    small_flow = Flow(
-        small_stages(
-            shared,
-            (glu_bias, qkv_bias_part[:, 0, :]),
-            batch_size.bit_length() - 1,
-            tensor_size.bit_length() - 1,
-        )
-    )
-    flows = [down_flow, glu_flow, out_flow, qkv_flow, small_flow]
+    flows = [down_flow, glu_flow, small_flow, out_flow, qkv_flow]
+    last = glu_flow.step(last).result
     while any(flow.result is None for flow in flows):
-        for flow in flows:
+        for flow in (out_flow, small_flow, qkv_flow, glu_flow, down_flow):
             if flow.result is None:
                 flow.step(last)
                 if flow.result is None:
                     last = flow.sent
-    down_grad, glu_grad, out_grad, qkv_grad, (shared, glu_bias, qkv_bias_grad) = [
+    down_grad, glu_grad, (shared, glu_bias, qkv_bias_grad), out_grad, qkv_grad = [
         flow.result for flow in flows
     ]
     return (

time: 866 us -> 842 us (0.972)
  starting transfers between devices: 92.3 us -> 63.8 us
  Pallas kernels: 205 us -> 226 us
  other arithmetic: 103 us -> 91.2 us
    ppermute x6, waiting for transfers between devices: 0.02 us -> 22.8 us  [move(): return lax.ppermute(x, 'batch', [(i, i ^ mask) for i in range(size)])]
    all_gather x7, waiting for transfers between devices: 146 us -> 126 us  [gather_rows(): return lax.all_gather(x, 'tensor', axis=0, tiled=True)]
    pallas_call x0 -> x3, Pallas kernels: none -> 19.2 us  [assemble(): pl.pallas_call(functools.partial(assemble_kernel, dim), grid_spec=pltpu.P...]
    ppermute x52 -> x41, waiting for transfers between devices: 108 us -> 89 us  [swap_bit(): return lax.ppermute(x, axis_name, [(i, i ^ 1 << bit) for i in range(size)])]
    ppermute x52 -> x41, starting transfers between devices: 58.6 us -> 40.2 us  [swap_bit(): return lax.ppermute(x, axis_name, [(i, i ^ 1 << bit) for i in range(size)])]
    ppermute x6, starting transfers between devices: 17 us -> 7.15 us  [move(): return lax.ppermute(x, 'batch', [(i, i ^ mask) for i in range(size)])]
    select_n x18 -> x11, other arithmetic: 14.2 us -> 5.18 us  [gather_stages(): jnp.where(mine, other, part)]
    convert_element_type x17 -> x15, other arithmetic: 22.2 us -> 21 us  [add_low(): return (a.astype(F32) + b.astype(F32)).astype(BF16)]
  transfers between devices with their start and end apart: 75 -> 64, of which waited for: 27 -> 27; matrix products, arithmetic and copies ran while one was open for 16% -> 15% of each run, Pallas kernels for 24% -> 27%
where the time goes in v3:
time: 842 us; the launch traced here: 835 us
  waiting for transfers between devices  381 us (45%)
  Pallas kernels  226 us (27%)
  other arithmetic  91.2 us (11%)
  starting transfers between devices  63.8 us (8%)
  local copies, waits for them, and re-layouts  43.5 us (5%)
  between operations  16.5 us (2%)
  matrix products  13.1 us (2%)
    all_gather x7, waiting for transfers between devices, gather_rows(): return lax.all_gather(x, 'tensor', axis=0, tiled=True)  126 us
    ppermute x41, waiting for transfers between devices, swap_bit(): return lax.ppermute(x, axis_name, [(i, i ^ 1 << bit) for i in range(size)])  89 us
    reduce_scatter x6, waiting for transfers between devices, scatter_rows(): return lax.psum_scatter(x, 'tensor', scatter_dimension=0, tiled=True)  76.7 us
    all_to_all x2, waiting for transfers between devices, per_device(): lax.all_to_all(context, 'tensor', split_axis=0, concat_axis=1, tiled=True)  52.7 us
    pallas_call x2, Pallas kernels, glu_backward(): pl.pallas_call(glu_backward_kernel, grid=(length // ROW_TILE,), in_specs=...  45.5 us
    ppermute x41, starting transfers between devices, swap_bit(): return lax.ppermute(x, axis_name, [(i, i ^ 1 << bit) for i in range(size)])  40.2 us
    pallas_call x2, Pallas kernels, attend_backward(): pl.pallas_call(attend_backward_kernel, grid=(length // ROW_TILE,), in_spe...  38.9 us
    pallas_call x2, Pallas kernels, attend_forward(): pl.pallas_call(attend_forward_kernel, grid=(length // ROW_TILE,), in_spec...  34.5 us
  transfers between devices with their start and end apart: 64, of which 27 were waited for; matrix products, arithmetic and copies ran while one was open for 15% of the time, Pallas kernels for 27%

profile of v3, /device:TPU:0, one launch (start us, length us, event | category | flops | bytes accessed | tf_op | source)
XLA Modules:
  0.0 835.0 jit_solution(6306154113131421767)
XLA Ops:
  12.2 29.8 %all-gather.10.cloned.1.call-done = bf16[2048,512]{1,0:T(8,128)(2,1)} async-done(((bf16[256,512]{1,0:T(8,128)(2,1)}), bf16[2048,512]{1,0:T(8,128)(2,1)}) %all-gather.10.cloned.1.call-update) | async-done | bytes 2097168 | tf_op jit(solution)/shard_map/all_gather | solution.py:717
  44.9 5.0 fusion.29
  51.3 6.1 collective-permute-done
  59.2 5.5 collective-permute-done.2
  68.8 17.4 %collective-permute-done.1 = bf16[2048,256]{1,0:T(8,128)(2,1)S(1)} collective-permute-done((bf16[2048,256]{1,0:T(8,128)(2,1)S(1)}, bf16[2048,256]{1,0:T(8,128)(2,1)S(1)}, u32[]{:S(2)}, u32[]{:S(2)}) %collective-permute-start.1) | collective-permute-done | bytes 1048608 | tf_op jit(solution)/shard_map/ppermute | solution.py:492
  88.6 2.7 pad_maximum_fusion.1
  91.5 17.2 %attend_forward.2 = (bf16[6,1024,128]{2,1,0:T(8,128)(2,1)}, bf16[1024,256]{1,0:T(8,128)(2,1)}, f32[2,4,1,256]{3,2,1,0:T(1,128)}) custom-call(bf16[1024,2048]{1,0:T(8,128)(2,1)} %bitcast.169, bf16[3,2048,256]{2,1,0:T(8,128)(2,1)} %bitcast.173, f32[3,1,256]{2,1,0:T(1,128)} %broadcast_in_dim.8.b_ref, f32[1024,128]{1,0:T(8,128)} %get-tuple-element.337.cos_ref, ...), custom_call_target="tpu_custom_call" | custom-call | flops 199999995904 | bytes 1024 | tf_op jit(solution)/shard_map/attend_forward/pallas_call | solution.py:94
  108.7 4.4 all-to-all-start
  114.0 2.9 pad_maximum_fusion.14
  117.5 25.4 %all-to-all-done = bf16[8,128,256]{2,1,0:T(8,128)(2,1)} async-done(((bf16[8,128,256]{2,1,0:T(8,128)(2,1)}), bf16[8,128,256]{2,1,0:T(8,128)(2,1)}, u32[]{:S(2)}, u32[]{:S(2)}) %all-to-all-start) | async-done | bytes 524320 | tf_op jit(solution)/shard_map/all_to_all | solution.py:787
  144.0 4.0 broadcast_select_fusion.1
  154.1 17.3 %attend_forward.3 = (bf16[6,1024,128]{2,1,0:T(8,128)(2,1)}, bf16[1024,256]{1,0:T(8,128)(2,1)}, f32[2,4,1,256]{3,2,1,0:T(1,128)}) custom-call(bf16[1024,2048]{1,0:T(8,128)(2,1)} %bitcast.171, bf16[3,2048,256]{2,1,0:T(8,128)(2,1)} %bitcast.174, f32[3,1,256]{2,1,0:T(1,128)} %broadcast_in_dim.8.b_ref, f32[1024,128]{1,0:T(8,128)} %get-tuple-element.339.cos_ref, ...), custom_call_target="tpu_custom_call" | custom-call | flops 199999995904 | bytes 1024 | tf_op jit(solution)/shard_map/attend_forward/pallas_call | solution.py:94
  171.4 3.6 all-to-all-start.1
  176.8 27.3 %all-to-all-done.1 = bf16[8,128,256]{2,1,0:T(8,128)(2,1)S(1)} async-done(((bf16[8,128,256]{2,1,0:T(8,128)(2,1)}), bf16[8,128,256]{2,1,0:T(8,128)(2,1)S(1)}, u32[]{:S(2)}, u32[]{:S(2)}) %all-to-all-start.1) | async-done | bytes 524320 | tf_op jit(solution)/shard_map/all_to_all | solution.py:787
  204.2 4.7 fusion.50
  211.6 16.9 %glu_forward.2 = (bf16[688,1024]{1,0:T(8,128)(2,1)}, bf16[688,1024]{1,0:T(8,128)(2,1)}, bf16[688,1024]{1,0:T(8,128)(2,1)}, bf16[1024,2048]{1,0:T(8,128)(2,1)}) custom-call(s32[1]{0:T(128)} %bitcast.14.live_ref, bf16[1024,2048]{1,0:T(8,128)(2,1)} %all-gather.12.cloned.1.call-done.h_ref.refs_4_, bf16[688,2048]{1,0:T(8,128)(2,1)} %bitcast.217, ...), custom_call_target="tpu_custom_call" | custom-call | flops 199999995904 | bytes 1024 | tf_op jit(solution)/shard_map/glu_forward/pallas_call | solution.py:259
  228.9 29.7 %all-gather.14.cloned.1.call-done.h_ref.refs_5_ = bf16[1024,2048]{1,0:T(8,128)(2,1)} async-done(((bf16[128,2048]{1,0:T(8,128)(2,1)}), bf16[1024,2048]{1,0:T(8,128)(2,1)}) %all-gather.14.cloned.1.call-update) | async-done | bytes 4194320 | tf_op jit(solution)/shard_map/all_gather | solution.py:717
  258.6 17.1 %glu_forward.3 = (bf16[688,1024]{1,0:T(8,128)(2,1)}, bf16[688,1024]{1,0:T(8,128)(2,1)}, bf16[688,1024]{1,0:T(8,128)(2,1)}, bf16[1024,2048]{1,0:T(8,128)(2,1)}) custom-call(s32[1]{0:T(128)} %bitcast.14.live_ref, bf16[1024,2048]{1,0:T(8,128)(2,1)} %all-gather.14.cloned.1.call-done.h_ref.refs_5_, bf16[688,2048]{1,0:T(8,128)(2,1)} %bitcast.218, ...), custom_call_target="tpu_custom_call" | custom-call | flops 199999995904 | bytes 1024 | tf_op jit(solution)/shard_map/glu_forward/pallas_call | solution.py:259
  275.8 34.3 %reduce-scatter.7.cloned.1.call-done = bf16[128,2048]{1,0:T(8,128)(2,1)} async-done(((bf16[1024,2048]{1,0:T(8,128)(2,1)}), bf16[128,2048]{1,0:T(8,128)(2,1)}) %reduce-scatter.7.cloned.1.call-update) | async-done | bytes 524304 | tf_op jit(solution)/shard_map/reduce_scatter | solution.py:720
  318.6 42.4 %reduce-scatter.9.cloned.1.call-done = bf16[128,2048]{1,0:T(8,128)(2,1)} async-done(((bf16[1024,2048]{1,0:T(8,128)(2,1)}), bf16[128,2048]{1,0:T(8,128)(2,1)}) %reduce-scatter.9.cloned.1.call-update) | async-done | bytes 524304 | tf_op jit(solution)/shard_map/reduce_scatter | solution.py:720
  368.1 40.5 %all-gather.16.cloned.1.call-done.g_ref.refs_2_ = bf16[1024,2048]{1,0:T(8,128)(2,1)} async-done(((bf16[128,2048]{1,0:T(8,128)(2,1)}), bf16[1024,2048]{1,0:T(8,128)(2,1)}) %all-gather.16.cloned.1.call-update) | async-done | bytes 4194320 | tf_op jit(solution)/shard_map/all_gather | solution.py:717
  408.6 22.6 %glu_backward.2 = (bf16[688,1024]{1,0:T(8,128)(2,1)}, bf16[688,1024]{1,0:T(8,128)(2,1)}, f32[688,1]{1,0:T(8,128)}, f32[688,1]{1,0:T(8,128)}, bf16[1024,2048]{1,0:T(8,128)(2,1)}) custom-call(s32[1]{0:T(128)} %bitcast.14.live_ref, bf16[1024,2048]{1,0:T(8,128)(2,1)} %all-gather.16.cloned.1.call-done.g_ref.refs_2_, bf16[688,2048]{1,0:T(8,128)(2,1)} %bitcast.219, ...), custom_call_target="tpu_custom_call" | custom-call | flops 199999995904 | bytes 1024 | tf_op jit(solution)/shard_map/glu_backward/pallas_call | solution.py:322
  431.2 25.4 %all-gather.18.cloned.1.call-done.refs_3_.g_ref = bf16[1024,2048]{1,0:T(8,128)(2,1)} async-done(((bf16[128,2048]{1,0:T(8,128)(2,1)}), bf16[1024,2048]{1,0:T(8,128)(2,1)}) %all-gather.18.cloned.1.call-update) | async-done | bytes 4194320 | tf_op jit(solution)/shard_map/all_gather | solution.py:717
  456.7 11.5 %weight_grad.2 = (bf16[1,688,512]{2,1,0:T(8,128)(2,1)}, bf16[1,688,512]{2,1,0:T(8,128)(2,1)}, bf16[1,688,512]{2,1,0:T(8,128)(2,1)}, bf16[1,688,512]{2,1,0:T(8,128)(2,1)}) custom-call(s32[4]{0:T(128)} %pad_add_fusion.blocks_ref, bf16[688,1024]{1,0:T(8,128)(2,1)} %get-tuple-element.142.refs_0_, bf16[688,1024]{1,0:T(8,128)(2,1)} %get-tuple-element.143.refs_1_, ...), custom_call_target="tpu_custom_call" | custom-call | flops 199999995904 | bytes 1024 | tf_op jit(solution)/shard_map/weight_grad/pallas_call | solution.py:361
  471.1 22.9 %glu_backward.3 = (bf16[688,1024]{1,0:T(8,128)(2,1)}, bf16[688,1024]{1,0:T(8,128)(2,1)}, f32[688,1]{1,0:T(8,128)}, f32[688,1]{1,0:T(8,128)}, bf16[1024,2048]{1,0:T(8,128)(2,1)}) custom-call(s32[1]{0:T(128)} %bitcast.14.live_ref, bf16[1024,2048]{1,0:T(8,128)(2,1)} %all-gather.18.cloned.1.call-done.refs_3_.g_ref, bf16[688,2048]{1,0:T(8,128)(2,1)} %bitcast.220, ...), custom_call_target="tpu_custom_call" | custom-call | flops 199999995904 | bytes 1024 | tf_op jit(solution)/shard_map/glu_backward/pallas_call | solution.py:322
  500.5 19.2 %weight_grad.3 = (bf16[2,688,512]{2,1,0:T(8,128)(2,1)}, bf16[2,688,512]{2,1,0:T(8,128)(2,1)}, bf16[2,688,512]{2,1,0:T(8,128)(2,1)}, bf16[2,688,512]{2,1,0:T(8,128)(2,1)}) custom-call(s32[4]{0:T(128)} %pad_add_fusion.blocks_ref, bf16[688,1024]{1,0:T(8,128)(2,1)} %get-tuple-element.154.refs_0_, bf16[688,1024]{1,0:T(8,128)(2,1)} %get-tuple-element.155.refs_1_, ...), custom_call_target="tpu_custom_call" | custom-call | flops 199999995904 | bytes 1024 | tf_op jit(solution)/shard_map/weight_grad/pallas_call | solution.py:361
  531.1 3.1 convolution_convert_fusion.1
  535.0 3.5 all-to-all-start.2
  539.7 20.9 %collective-permute-done.11 = bf16[688,256]{1,0:T(8,128)(2,1)S(1)} collective-permute-done((bf16[688,256]{1,0:T(8,128)(2,1)S(1)}, bf16[688,256]{1,0:T(8,128)(2,1)S(1)}, u32[]{:S(2)}, u32[]{:S(2)}) %collective-permute-start.11) | collective-permute-done | bytes 352288 | tf_op jit(solution)/shard_map/ppermute | solution.py:492
  572.8 19.4 %attend_backward.2 = (bf16[3,1024,256]{2,1,0:T(8,128)(2,1)}, f32[3,1,256]{2,1,0:T(1,128)}, bf16[1024,2048]{1,0:T(8,128)(2,1)}) custom-call(bf16[6,1024,128]{2,1,0:T(8,128)(2,1)} %get-tuple-element.136.qkv_ref, bf16[1024,256]{1,0:T(8,128)(2,1)} %bitcast.183, f32[2,4,1,256]{3,2,1,0:T(1,128)} %get-tuple-element.170.lse_ref, s32[4,1,256]{2,1,0:T(1,128)} %bitcast.205, ...), custom_call_target="tpu_custom_call" | custom-call | flops 199999995904 | bytes 1024 | tf_op jit(solution)/shard_map/attend_backward/pallas_call | solution.py:199
  606.2 3.8 convolution_convert_fusion
  610.0 4.3 collective-permute-done.17
  620.1 5.4 assemble.3
  625.5 10.6 %row_grad.1 = (bf16[1024,2048]{1,0:T(8,128)(2,1)}, bf16[1024,2048]{1,0:T(8,128)(2,1)}) custom-call(s32[2]{0:T(128)} %pad_add_fusion.1.sides_ref, bf16[256,2048]{1,0:T(8,128)(2,1)} %pad_maximum_fusion.8.left_ref, bf16[256,2048]{1,0:T(8,128)(2,1)} %pad_maximum_fusion.9.right_ref), custom_call_target="tpu_custom_call" | custom-call | flops 1024 | bytes 1024 | tf_op jit(solution)/shard_map/row_grad/pallas_call | solution.py:427
  636.9 3.5 all-to-all-start.3
  642.6 13.1 %all-to-all-done.3 = bf16[128,8,256]{2,0,1:T(8,128)(2,1)S(1)} async-done(((bf16[128,8,256]{2,0,1:T(8,128)(2,1)}), bf16[128,8,256]{2,0,1:T(8,128)(2,1)S(1)}, u32[]{:S(2)}, u32[]{:S(2)}) %all-to-all-start.3) | async-done | bytes 524320 | tf_op jit(solution)/shard_map/all_to_all | solution.py:876
  656.5 19.5 %attend_backward.3 = (bf16[3,1024,256]{2,1,0:T(8,128)(2,1)}, f32[3,1,256]{2,1,0:T(1,128)}, bf16[1024,2048]{1,0:T(8,128)(2,1)}) custom-call(bf16[6,1024,128]{2,1,0:T(8,128)(2,1)} %get-tuple-element.172.qkv_ref, bf16[1024,256]{1,0:T(8,128)(2,1)} %bitcast.177, f32[2,4,1,256]{3,2,1,0:T(1,128)} %get-tuple-element.185.lse_ref, s32[4,1,256]{2,1,0:T(1,128)} %bitcast.189, ...), custom_call_target="tpu_custom_call" | custom-call | flops 1024 | bytes 1024 | tf_op jit(solution)/shard_map/attend_backward/pallas_call | solution.py:199
  676.0 4.1 add_convert_fusion
  691.1 12.9 %slab_grad.1 = (bf16[3,512,256]{2,1,0:T(8,128)(2,1)}, bf16[3,512,256]{2,1,0:T(8,128)(2,1)}, bf16[3,512,256]{2,1,0:T(8,128)(2,1)}, bf16[3,512,256]{2,1,0:T(8,128)(2,1)}) custom-call(s32[4]{0:T(128)} %pad_add_fusion.3.blocks_ref.sources_ref, bf16[1024,2048]{1,0:T(8,128)(2,1)} %bitcast.170, bf16[1024,2048]{1,0:T(8,128)(2,1)} %bitcast.172, ...), custom_call_target="tpu_custom_call" | custom-call | flops 1024 | bytes 1024 | tf_op jit(solution)/shard_map/slab_grad/pallas_call | solution.py:396
  705.7 8.0 assemble.4
  726.3 18.7 %collective-permute-done.24 = bf16[3,512,256]{2,1,0:T(8,128)(2,1)} collective-permute-done((bf16[3,512,256]{2,1,0:T(8,128)(2,1)}, bf16[3,512,256]{2,1,0:T(8,128)(2,1)}, u32[]{:S(2)}, u32[]{:S(2)}) %collective-permute-start.24) | collective-permute-done | bytes 786464 | tf_op jit(solution)/shard_map/ppermute | solution.py:596
  749.8 3.8 collective-permute-done.34
  754.4 18.5 %collective-permute-done.33 = bf16[1024,256]{1,0:T(8,128)(2,1)S(1)} collective-permute-done((bf16[1024,256]{1,0:T(8,128)(2,1)}, bf16[1024,256]{1,0:T(8,128)(2,1)S(1)}, u32[]{:S(2)}, u32[]{:S(2)}) %collective-permute-start.33) | collective-permute-done | bytes 524320 | tf_op jit(solution)/shard_map/ppermute | solution.py:492
  773.4 10.5 %slice_bitcast_fusion = (f32[2048,688]{0,1:T(8,128)}, f32[2048,688]{0,1:T(8,128)}) fusion(f32[2,688,2048]{2,1,0:T(8,128)} %assemble.4), kind=kLoop, calls=%fused_computation.2 | loop fusion | bytes 22544384 | tf_op jit(solution)/shard_map/transpose | solution.py:953
  789.4 4.4 collective-permute-done.38
  794.7 2.4 collective-permute-start.41
  803.4 2.8 collective-permute-start.43
  806.2 5.7 assemble.5
  (488 shorter events, 163.8 us)
Async XLA Ops:
  7.2 34.8 %all-gather.10.cloned.1.call-start = ((), (), s32[]{:S(2)}) async-start(), calls=%async_computation.10 | async-start | bytes 2359296 | tf_op jit(solution)/shard_map/all_gather | solution.py:717
  9.7 81.8 %all-gather.20.cloned.1.call-start = ((), (), s32[]{:S(2)}) async-start(), calls=%async_computation.21 | async-start | bytes 4718592 | tf_op jit(solution)/shard_map/all_gather | solution.py:717
  10.8 143.3 %all-gather.22.cloned.1.call-start = ((), (), s32[]{:S(2)}) async-start(), calls=%async_computation.22 | async-start | bytes 4718592 | tf_op jit(solution)/shard_map/all_gather | solution.py:717
  57.7 28.5 %collective-permute-start.1 = (bf16[2048,256]{1,0:T(8,128)(2,1)S(1)}, bf16[2048,256]{1,0:T(8,128)(2,1)S(1)}, u32[]{:S(2)}, u32[]{:S(2)}) collective-permute-start(bf16[2048,256]{1,0:T(8,128)(2,1)S(1)} %pad_maximum_fusion.5), channel_id=1, source_target_pairs={{0,8},{8,0},{16,24},{24,16},{1,9},{9,1},{17,25},{25,17},{2,10},{10... | collective-permute-start | bytes 3145736 | tf_op jit(solution)/shard_map/ppermute | solution.py:492
  64.9 23.3 %collective-permute-start.3 = (bf16[2048,256]{1,0:T(8,128)(2,1)S(1)}, bf16[2048,256]{1,0:T(8,128)(2,1)S(1)}, u32[]{:S(2)}, u32[]{:S(2)}) collective-permute-start(bf16[2048,256]{1,0:T(8,128)(2,1)S(1)} %pad_maximum_fusion.6), channel_id=1, source_target_pairs={{0,16},{8,24},{16,0},{24,8},{1,17},{9,25},{17,1},{25,9},{2,18},{10... | collective-permute-start | bytes 3145736 | tf_op jit(solution)/shard_map/ppermute | solution.py:492
  91.4 52.6 %collective-permute-start.4 = (bf16[2048,1024]{1,0:T(8,128)(2,1)}, bf16[2048,1024]{1,0:T(8,128)(2,1)}, u32[]{:S(2)}, u32[]{:S(2)}) collective-permute-start(bf16[2048,1024]{1,0:T(8,128)(2,1)} %pad_maximum_fusion.1), channel_id=1, source_target_pairs={{0,1},{1,0},{2,3},{3,2},{4,5},{5,4},{6,7},{7,6},{8,9},{9,8},{10,11... | collective-permute-start | bytes 12582920 | tf_op jit(solution)/shard_map/ppermute | solution.py:492
  108.7 34.2 %all-to-all-start = ((bf16[8,128,256]{2,1,0:T(8,128)(2,1)}), bf16[8,128,256]{2,1,0:T(8,128)(2,1)}, u32[]{:S(2)}, u32[]{:S(2)}) async-start(bf16[8,128,256]{2,1,0:T(8,128)(2,1)} %bitcast.185), calls=%async_computation | async-start | bytes 1048576 | tf_op jit(solution)/shard_map/all_to_all | solution.py:787
  113.1 98.5 %all-gather.12.cloned.1.call-start = ((), (), s32[]{:S(2)}) async-start(), calls=%async_computation.11 | async-start | bytes 4718592 | tf_op jit(solution)/shard_map/all_gather | solution.py:717
  171.4 32.7 %all-to-all-start.1 = ((bf16[8,128,256]{2,1,0:T(8,128)(2,1)}), bf16[8,128,256]{2,1,0:T(8,128)(2,1)S(1)}, u32[]{:S(2)}, u32[]{:S(2)}) async-start(bf16[8,128,256]{2,1,0:T(8,128)(2,1)} %bitcast.186), calls=%async_computation.1 | async-start | bytes 1048576 | tf_op jit(solution)/shard_map/all_to_all | solution.py:787
  175.0 83.6 %all-gather.14.cloned.1.call-start = ((), (), s32[]{:S(2)}) async-start(), calls=%async_computation.13 | async-start | bytes 4718592 | tf_op jit(solution)/shard_map/all_gather | solution.py:717
  211.6 98.5 %reduce-scatter.7.cloned.1.call-start = ((), (), s32[]{:S(2)}) async-start(), calls=%async_computation.12 | async-start | bytes 4718592 | tf_op jit(solution)/shard_map/reduce_scatter | solution.py:720
  228.6 132.5 %reduce-scatter.9.cloned.1.call-start = ((), (), s32[]{:S(2)}) async-start(), calls=%async_computation.14 | async-start | bytes 4718592 | tf_op jit(solution)/shard_map/reduce_scatter | solution.py:720
  275.7 132.8 %all-gather.16.cloned.1.call-start = ((), (), s32[]{:S(2)}) async-start(), calls=%async_computation.15 | async-start | bytes 4718592 | tf_op jit(solution)/shard_map/all_gather | solution.py:717
  316.7 139.9 %all-gather.18.cloned.1.call-start = ((), (), s32[]{:S(2)}) async-start(), calls=%async_computation.17 | async-start | bytes 4718592 | tf_op jit(solution)/shard_map/all_gather | solution.py:717
  367.6 158.5 %reduce-scatter.11.cloned.1.call-start = ((), (), s32[]{:S(2)}) async-start(), calls=%async_computation.16 | async-start | bytes 4718592 | tf_op jit(solution)/shard_map/reduce_scatter | solution.py:720
  468.2 25.8 %collective-permute-start.5 = (bf16[688,512]{1,0:T(8,128)(2,1)}, bf16[688,512]{1,0:T(8,128)(2,1)}, u32[]{:S(2)}, u32[]{:S(2)}) collective-permute-start(bf16[688,512]{1,0:T(8,128)(2,1)} %bitcast.226), channel_id=1, source_target_pairs={{0,8},{8,0},{16,24},{24,16},{1,9},{9,1},{17,25},{25,17},{2,10},{10... | collective-permute-start | bytes 2113544 | tf_op jit(solution)/shard_map/ppermute | solution.py:492
  469.6 24.4 %collective-permute-start.6 = (bf16[688,512]{1,0:T(8,128)(2,1)}, bf16[688,512]{1,0:T(8,128)(2,1)}, u32[]{:S(2)}, u32[]{:S(2)}) collective-permute-start(bf16[688,512]{1,0:T(8,128)(2,1)} %bitcast.225), channel_id=1, source_target_pairs={{0,16},{8,24},{16,0},{24,8},{1,17},{9,25},{17,1},{25,9},{2,18},{10... | collective-permute-start | bytes 2113544 | tf_op jit(solution)/shard_map/ppermute | solution.py:492
  499.2 23.4 %collective-permute-start.7 = (bf16[688,256]{1,0:T(8,128)(2,1)}, bf16[688,256]{1,0:T(8,128)(2,1)}, u32[]{:S(2)}, u32[]{:S(2)}) collective-permute-start(bf16[688,256]{1,0:T(8,128)(2,1)} %constant_dynamic-slice_fusion.8), channel_id=1, source_target_pairs={{0,16},{8,24},{16,0},{24,8},{1,17},{9,25},{17,1},{25,9},{2,18},{10... | collective-permute-start | bytes 1056776 | tf_op jit(solution)/shard_map/ppermute | solution.py:492
  499.8 22.9 %collective-permute-start.8 = (bf16[688,256]{1,0:T(8,128)(2,1)}, bf16[688,256]{1,0:T(8,128)(2,1)}, u32[]{:S(2)}, u32[]{:S(2)}) collective-permute-start(bf16[688,256]{1,0:T(8,128)(2,1)} %constant_dynamic-slice_fusion.7), channel_id=1, source_target_pairs={{0,8},{8,0},{16,24},{24,16},{1,9},{9,1},{17,25},{25,17},{2,10},{10... | collective-permute-start | bytes 1056776 | tf_op jit(solution)/shard_map/ppermute | solution.py:492
  519.7 45.0 %collective-permute-start.9 = (bf16[2,688,512]{2,1,0:T(8,128)(2,1)}, bf16[2,688,512]{2,1,0:T(8,128)(2,1)}, u32[]{:S(2)}, u32[]{:S(2)}) collective-permute-start(bf16[2,688,512]{2,1,0:T(8,128)(2,1)} %get-tuple-element.158), channel_id=1, source_target_pairs={{0,8},{8,0},{16,24},{24,16},{1,9},{9,1},{17,25},{25,17},{2,10},{10... | collective-permute-start | bytes 4227080 | tf_op jit(solution)/shard_map/ppermute | solution.py:492
  521.1 43.6 %collective-permute-start.10 = (bf16[2,688,512]{2,1,0:T(8,128)(2,1)}, bf16[2,688,512]{2,1,0:T(8,128)(2,1)}, u32[]{:S(2)}, u32[]{:S(2)}) collective-permute-start(bf16[2,688,512]{2,1,0:T(8,128)(2,1)} %get-tuple-element.159), channel_id=1, source_target_pairs={{0,16},{8,24},{16,0},{24,8},{1,17},{9,25},{17,1},{25,9},{2,18},{10... | collective-permute-start | bytes 4227080 | tf_op jit(solution)/shard_map/ppermute | solution.py:492
  523.7 36.9 %collective-permute-start.11 = (bf16[688,256]{1,0:T(8,128)(2,1)S(1)}, bf16[688,256]{1,0:T(8,128)(2,1)S(1)}, u32[]{:S(2)}, u32[]{:S(2)}) collective-permute-start(bf16[688,256]{1,0:T(8,128)(2,1)S(1)} %add_convert_fusion.14), channel_id=1, source_target_pairs={{0,16},{8,24},{16,0},{24,8},{1,17},{9,25},{17,1},{25,9},{2,18},{10... | collective-permute-start | bytes 1056776 | tf_op jit(solution)/shard_map/ppermute | solution.py:492
  525.4 35.2 %collective-permute-start.12 = (bf16[688,256]{1,0:T(8,128)(2,1)S(1)}, bf16[688,256]{1,0:T(8,128)(2,1)S(1)}, u32[]{:S(2)}, u32[]{:S(2)}) collective-permute-start(bf16[688,256]{1,0:T(8,128)(2,1)S(1)} %add_convert_fusion.13), channel_id=1, source_target_pairs={{0,8},{8,0},{16,24},{24,16},{1,9},{9,1},{17,25},{25,17},{2,10},{10... | collective-permute-start | bytes 1056776 | tf_op jit(solution)/shard_map/ppermute | solution.py:492
  535.0 29.7 %all-to-all-start.2 = ((bf16[128,8,256]{2,0,1:T(8,128)(2,1)}), bf16[128,8,256]{2,0,1:T(8,128)(2,1)S(1)}, u32[]{:S(2)}, u32[]{:S(2)}) async-start(bf16[128,8,256]{2,0,1:T(8,128)(2,1)} %bitcast.159), calls=%async_computation.5 | async-start | bytes 1048576 | tf_op jit(solution)/shard_map/all_to_all | solution.py:876
  538.5 62.2 %reduce-scatter.15.cloned.1.call-start = ((), (), s32[]{:S(2)}) async-start(), calls=%async_computation.19 | async-start | bytes 4718592 | tf_op jit(solution)/shard_map/reduce_scatter | solution.py:720
  539.6 284.8 %reduce-scatter.13.cloned.1.call-start = ((), (), s32[]{:S(2)}) async-start(), calls=%async_computation.18 | async-start | bytes 4718592 | tf_op jit(solution)/shard_map/reduce_scatter | solution.py:720
  561.6 58.4 %collective-permute-start.16 = (bf16[688,512]{1,0:T(8,128)(2,1)}, bf16[688,512]{1,0:T(8,128)(2,1)}, u32[]{:S(2)}, u32[]{:S(2)}) collective-permute-start(bf16[688,512]{1,0:T(8,128)(2,1)} %pad_maximum_fusion.11.refs_1_), channel_id=1, source_target_pairs={{0,16},{8,24},{16,0},{24,8},{1,17},{9,25},{17,1},{25,9},{2,18},{10... | collective-permute-start | bytes 2113544 | tf_op jit(solution)/shard_map/ppermute | solution.py:492
  564.1 56.0 %collective-permute-start.15 = (bf16[688,512]{1,0:T(8,128)(2,1)}, bf16[688,512]{1,0:T(8,128)(2,1)}, u32[]{:S(2)}, u32[]{:S(2)}) collective-permute-start(bf16[688,512]{1,0:T(8,128)(2,1)} %pad_maximum_fusion.10.refs_0_), channel_id=1, source_target_pairs={{0,8},{8,0},{16,24},{24,16},{1,9},{9,1},{17,25},{25,17},{2,10},{10... | collective-permute-start | bytes 2113544 | tf_op jit(solution)/shard_map/ppermute | solution.py:492
  570.7 22.1 %collective-permute-start.13 = (bf16[2,688,256]{2,1,0:T(8,128)(2,1)}, bf16[2,688,256]{2,1,0:T(8,128)(2,1)}, u32[]{:S(2)}, u32[]{:S(2)}) collective-permute-start(bf16[2,688,256]{2,1,0:T(8,128)(2,1)} %constant_dynamic-slice_fusion.6), channel_id=1, source_target_pairs={{0,16},{8,24},{16,0},{24,8},{1,17},{9,25},{17,1},{25,9},{2,18},{10... | collective-permute-start | bytes 2113544 | tf_op jit(solution)/shard_map/ppermute | solution.py:492
  571.3 23.6 %collective-permute-start.14 = (bf16[2,688,256]{2,1,0:T(8,128)(2,1)}, bf16[2,688,256]{2,1,0:T(8,128)(2,1)}, u32[]{:S(2)}, u32[]{:S(2)}) collective-permute-start(bf16[2,688,256]{2,1,0:T(8,128)(2,1)} %constant_dynamic-slice_fusion.5), channel_id=1, source_target_pairs={{0,8},{8,0},{16,24},{24,16},{1,9},{9,1},{17,25},{25,17},{2,10},{10... | collective-permute-start | bytes 2113544 | tf_op jit(solution)/shard_map/ppermute | solution.py:492
  636.1 39.9 %collective-permute-start.19 = (bf16[1024,2048]{1,0:T(8,128)(2,1)}, bf16[1024,2048]{1,0:T(8,128)(2,1)}, u32[]{:S(2)}, u32[]{:S(2)}) collective-permute-start(bf16[1024,2048]{1,0:T(8,128)(2,1)} %get-tuple-element.183), channel_id=1, source_target_pairs={{0,1},{1,0},{2,3},{3,2},{4,5},{5,4},{6,7},{7,6},{8,9},{9,8},{10,11... | collective-permute-start | bytes 12582920 | tf_op jit(solution)/shard_map/ppermute | solution.py:492
  636.9 18.8 %all-to-all-start.3 = ((bf16[128,8,256]{2,0,1:T(8,128)(2,1)}), bf16[128,8,256]{2,0,1:T(8,128)(2,1)S(1)}, u32[]{:S(2)}, u32[]{:S(2)}) async-start(bf16[128,8,256]{2,0,1:T(8,128)(2,1)} %bitcast.158), calls=%async_computation.8 | async-start | bytes 1048576 | tf_op jit(solution)/shard_map/all_to_all | solution.py:876
  640.4 185.2 %reduce-scatter.17.cloned.1.call-start = ((), (), s32[]{:S(2)}) async-start(), calls=%async_computation.20 | async-start | bytes 4718592 | tf_op jit(solution)/shard_map/reduce_scatter | solution.py:720
  640.5 50.6 %collective-permute-start.22 = (bf16[2,688,512]{2,1,0:T(8,128)(2,1)}, bf16[2,688,512]{2,1,0:T(8,128)(2,1)}, u32[]{:S(2)}, u32[]{:S(2)}) collective-permute-start(bf16[2,688,512]{2,1,0:T(8,128)(2,1)} %pad_maximum_fusion.4.refs_1_), channel_id=1, source_target_pairs={{0,16},{8,24},{16,0},{24,8},{1,17},{9,25},{17,1},{25,9},{2,18},{10... | collective-permute-start | bytes 4227080 | tf_op jit(solution)/shard_map/ppermute | solution.py:492
  641.8 49.3 %collective-permute-start.21 = (bf16[2,688,512]{2,1,0:T(8,128)(2,1)}, bf16[2,688,512]{2,1,0:T(8,128)(2,1)}, u32[]{:S(2)}, u32[]{:S(2)}) collective-permute-start(bf16[2,688,512]{2,1,0:T(8,128)(2,1)} %pad_maximum_fusion.3.refs_0_), channel_id=1, source_target_pairs={{0,8},{8,0},{16,24},{24,16},{1,9},{9,1},{17,25},{25,17},{2,10},{10... | collective-permute-start | bytes 4227080 | tf_op jit(solution)/shard_map/ppermute | solution.py:492
  683.0 30.8 %collective-permute-start.27 = (bf16[1024,512]{1,0:T(8,128)(2,1)}, bf16[1024,512]{1,0:T(8,128)(2,1)}, u32[]{:S(2)}, u32[]{:S(2)}) collective-permute-start(bf16[1024,512]{1,0:T(8,128)(2,1)} %constant_dynamic-slice_fusion.4), channel_id=1, source_target_pairs={{0,8},{8,0},{16,24},{24,16},{1,9},{9,1},{17,25},{25,17},{2,10},{10... | collective-permute-start | bytes 3145736 | tf_op jit(solution)/shard_map/ppermute | solution.py:492
  684.9 30.7 %collective-permute-start.28 = (bf16[1024,512]{1,0:T(8,128)(2,1)}, bf16[1024,512]{1,0:T(8,128)(2,1)}, u32[]{:S(2)}, u32[]{:S(2)}) collective-permute-start(bf16[1024,512]{1,0:T(8,128)(2,1)} %constant_dynamic-slice_fusion.3), channel_id=1, source_target_pairs={{0,16},{8,24},{16,0},{24,8},{1,17},{9,25},{17,1},{25,9},{2,18},{10... | collective-permute-start | bytes 3145736 | tf_op jit(solution)/shard_map/ppermute | solution.py:492
  691.0 31.5 %collective-permute-start.26 = (f32[6,2048]{1,0:T(8,128)S(1)}, f32[6,2048]{1,0:T(8,128)S(1)}, u32[]{:S(2)}, u32[]{:S(2)}) collective-permute-start(f32[6,2048]{1,0:T(8,128)S(1)} %add.479), channel_id=1, source_target_pairs={{0,2},{1,3},{2,0},{3,1},{4,6},{5,7},{6,4},{7,5},{8,10},{9,11},{10,... | collective-permute-start | bytes 147464 | tf_op jit(solution)/shard_map/ppermute | solution.py:492
  704.0 21.5 %collective-permute-start.23 = (bf16[3,512,256]{2,1,0:T(8,128)(2,1)}, bf16[3,512,256]{2,1,0:T(8,128)(2,1)}, u32[]{:S(2)}, u32[]{:S(2)}) collective-permute-start(bf16[3,512,256]{2,1,0:T(8,128)(2,1)} %get-tuple-element.197), channel_id=1, source_target_pairs={{0,8},{8,0},{16,24},{24,16},{1,9},{9,1},{17,25},{25,17},{2,10},{10... | collective-permute-start | bytes 2359304 | tf_op jit(solution)/shard_map/ppermute | solution.py:596
  705.0 40.0 %collective-permute-start.24 = (bf16[3,512,256]{2,1,0:T(8,128)(2,1)}, bf16[3,512,256]{2,1,0:T(8,128)(2,1)}, u32[]{:S(2)}, u32[]{:S(2)}) collective-permute-start(bf16[3,512,256]{2,1,0:T(8,128)(2,1)} %get-tuple-element.198), channel_id=1, source_target_pairs={{0,16},{8,24},{16,0},{24,8},{1,17},{9,25},{17,1},{25,9},{2,18},{10... | collective-permute-start | bytes 2359304 | tf_op jit(solution)/shard_map/ppermute | solution.py:596
  713.8 31.2 %collective-permute-start.25 = (bf16[3,512,256]{2,1,0:T(8,128)(2,1)}, bf16[3,512,256]{2,1,0:T(8,128)(2,1)}, u32[]{:S(2)}, u32[]{:S(2)}) collective-permute-start(bf16[3,512,256]{2,1,0:T(8,128)(2,1)} %get-tuple-element.199), channel_id=1, source_target_pairs={{0,24},{8,16},{16,8},{24,0},{1,25},{9,17},{17,9},{25,1},{2,26},{10... | collective-permute-start | bytes 2359304 | tf_op jit(solution)/shard_map/ppermute | solution.py:596
  721.5 32.1 %collective-permute-start.34 = (bf16[1024,256]{1,0:T(8,128)(2,1)}, bf16[1024,256]{1,0:T(8,128)(2,1)S(1)}, u32[]{:S(2)}, u32[]{:S(2)}) collective-permute-start(bf16[1024,256]{1,0:T(8,128)(2,1)} %constant_dynamic-slice_fusion.1), channel_id=1, source_target_pairs={{0,8},{8,0},{16,24},{24,16},{1,9},{9,1},{17,25},{25,17},{2,10},{10... | collective-permute-start | bytes 1572872 | tf_op jit(solution)/shard_map/ppermute | solution.py:492
  722.5 50.4 %collective-permute-start.33 = (bf16[1024,256]{1,0:T(8,128)(2,1)}, bf16[1024,256]{1,0:T(8,128)(2,1)S(1)}, u32[]{:S(2)}, u32[]{:S(2)}) collective-permute-start(bf16[1024,256]{1,0:T(8,128)(2,1)} %constant_dynamic-slice_fusion.2), channel_id=1, source_target_pairs={{0,16},{8,24},{16,0},{24,8},{1,17},{9,25},{17,1},{25,9},{2,18},{10... | collective-permute-start | bytes 1572872 | tf_op jit(solution)/shard_map/ppermute | solution.py:492
  725.5 58.4 %collective-permute-start.32 = (f32[6,2048]{1,0:T(8,128)S(1)}, f32[6,2048]{1,0:T(8,128)S(1)}, u32[]{:S(2)}, u32[]{:S(2)}) collective-permute-start(f32[6,2048]{1,0:T(8,128)S(1)} %add.484), channel_id=1, source_target_pairs={{0,4},{1,5},{2,6},{3,7},{4,0},{5,1},{6,2},{7,3},{8,12},{9,13},{10,... | collective-permute-start | bytes 147464 | tf_op jit(solution)/shard_map/ppermute | solution.py:492
  747.0 38.2 %collective-permute-start.31 = (bf16[3,512,256]{2,1,0:T(8,128)(2,1)S(1)}, bf16[3,512,256]{2,1,0:T(8,128)(2,1)S(1)}, u32[]{:S(2)}, u32[]{:S(2)}) collective-permute-start(bf16[3,512,256]{2,1,0:T(8,128)(2,1)S(1)} %add_convert_fusion.5.refs_0_), channel_id=1, source_target_pairs={{0,24},{8,16},{16,8},{24,0},{1,25},{9,17},{17,9},{25,1},{2,26},{10... | collective-permute-start | bytes 2359304 | tf_op jit(solution)/shard_map/ppermute | solution.py:596
  749.0 39.3 %collective-permute-start.30 = (bf16[3,512,256]{2,1,0:T(8,128)(2,1)S(1)}, bf16[3,512,256]{2,1,0:T(8,128)(2,1)S(1)}, u32[]{:S(2)}, u32[]{:S(2)}) collective-permute-start(bf16[3,512,256]{2,1,0:T(8,128)(2,1)S(1)} %add_convert_fusion.5.refs_0_), channel_id=1, source_target_pairs={{0,16},{8,24},{16,0},{24,8},{1,17},{9,25},{17,1},{25,9},{2,18},{10... | collective-permute-start | bytes 2359304 | tf_op jit(solution)/shard_map/ppermute | solution.py:596
  753.5 35.9 %collective-permute-start.29 = (bf16[3,512,256]{2,1,0:T(8,128)(2,1)S(1)}, bf16[3,512,256]{2,1,0:T(8,128)(2,1)S(1)}, u32[]{:S(2)}, u32[]{:S(2)}) collective-permute-start(bf16[3,512,256]{2,1,0:T(8,128)(2,1)S(1)} %add_convert_fusion.5.refs_0_), channel_id=1, source_target_pairs={{0,8},{8,0},{16,24},{24,16},{1,9},{9,1},{17,25},{25,17},{2,10},{10... | collective-permute-start | bytes 2359304 | tf_op jit(solution)/shard_map/ppermute | solution.py:596
  773.3 20.5 %collective-permute-start.38 = (bf16[512,512]{1,0:T(8,128)(2,1)S(1)}, bf16[512,512]{1,0:T(8,128)(2,1)S(1)}, u32[]{:S(2)}, u32[]{:S(2)}) collective-permute-start(bf16[512,512]{1,0:T(8,128)(2,1)S(1)} %fusion.27), channel_id=1, source_target_pairs={{0,4},{1,5},{2,6},{3,7},{4,0},{5,1},{6,2},{7,3},{8,12},{9,13},{10,... | collective-permute-start | bytes 1572872 | tf_op jit(solution)/shard_map/ppermute | solution.py:492
  (129 other events, 1600.5 us)
Sparse Core Ops, SparseCore 0:
  10.2 31.7 all-gather.9
  44.2 46.6 all-gather.19
  93.1 57.0 all-gather.21
  154.1 56.4 all-gather.11
  212.7 45.8 all-gather.13
  261.3 48.7 reduce-scatter.6
  312.9 48.1 reduce-scatter.8
  363.3 45.2 all-gather.15
  410.8 45.8 all-gather.17
  459.4 48.6 reduce-scatter.10
  542.2 50.6 reduce-scatter.14
  595.0 50.0 reduce-scatter.12
  723.7 54.6 reduce-scatter.16

commit v4 on v3

--- a/solution.py
+++ b/solution.py
@@ -18,7 +18,7 @@
 GELU_ROOT = math.sqrt(2.0 / math.pi)
 GELU_CUBIC = 0.044715
 FACTOR = 1.0 / math.sqrt(HEAD_DIM)
-QUERY_TILE = 256
+QUERY_TILE = 512
 ROW_TILE = 256
 VMEM_LIMIT = 56 * 1024 * 1024
 LONG = pl.CostEstimate(flops=200_000_000_000, bytes_accessed=1024, transcendentals=0)
@@ -82,7 +82,7 @@
                 lse_ref[head, index] = top * FACTOR + jnp.log(total)
                 return carry
 
-            lax.fori_loop(0, length // QUERY_TILE, one_tile, 0)
+            lax.fori_loop(0, length // QUERY_TILE, one_tile, 0, unroll=True)
 
 
 def attend_forward(x, w, b, cosine, sine, lo, hi):
@@ -173,7 +173,7 @@
                 return query_bias + jnp.sum(query_grad, axis=0, keepdims=True)
 
             query_bias = lax.fori_loop(
-                0, length // QUERY_TILE, one_tile, jnp.zeros((1, HEAD_DIM), F32)
+                0, length // QUERY_TILE, one_tile, jnp.zeros((1, HEAD_DIM), F32), unroll=True
             )
             key_grad = rope_back(key_total[...] * FACTOR, cos_ref[...], sin_ref[...])
             value_grad = value_total[...]
@@ -931,7 +931,7 @@
     flows = [down_flow, glu_flow, small_flow, out_flow, qkv_flow]
     last = glu_flow.step(last).result
     while any(flow.result is None for flow in flows):
-        for flow in (out_flow, small_flow, qkv_flow, glu_flow, down_flow):
+        for flow in (out_flow, small_flow, qkv_flow, small_flow, glu_flow, down_flow):
             if flow.result is None:
                 flow.step(last)
                 if flow.result is None:

time: 842 us -> 836 us (level)
  Pallas kernels: 226 us -> 212 us
  waiting for transfers between devices: 381 us -> 392 us
    ppermute x41, waiting for transfers between devices: 89 us -> 97.8 us  [swap_bit(): return lax.ppermute(x, axis_name, [(i, i ^ 1 << bit) for i in range(size)])]
  transfers between devices with their start and end apart: 64 -> 64, of which waited for: 27 -> 28; matrix products, arithmetic and copies ran while one was open for 15% -> 15% of each run, Pallas kernels for 27% -> 26%
where the time goes in v4:
time: 836 us; the launch traced here: 827 us
  waiting for transfers between devices  392 us (47%)
  Pallas kernels  212 us (25%)
  other arithmetic  89.6 us (11%)
  starting transfers between devices  60.2 us (7%)
  local copies, waits for them, and re-layouts  42.1 us (5%)
  between operations  16.8 us (2%)
  matrix products  13.2 us (2%)
    all_gather x7, waiting for transfers between devices, gather_rows(): return lax.all_gather(x, 'tensor', axis=0, tiled=True)  130 us
    ppermute x41, waiting for transfers between devices, swap_bit(): return lax.ppermute(x, axis_name, [(i, i ^ 1 << bit) for i in range(size)])  97.8 us
    reduce_scatter x6, waiting for transfers between devices, scatter_rows(): return lax.psum_scatter(x, 'tensor', scatter_dimension=0, tiled=True)  76.8 us
    all_to_all x2, waiting for transfers between devices, per_device(): lax.all_to_all(context, 'tensor', split_axis=0, concat_axis=1, tiled=True)  53.3 us
    pallas_call x2, Pallas kernels, glu_backward(): pl.pallas_call(glu_backward_kernel, grid=(length // ROW_TILE,), in_specs=...  45.5 us
    ppermute x41, starting transfers between devices, swap_bit(): return lax.ppermute(x, axis_name, [(i, i ^ 1 << bit) for i in range(size)])  36.8 us
    pallas_call x2, Pallas kernels, glu_forward(): pl.pallas_call(glu_forward_kernel, grid=(length // ROW_TILE,), in_specs=[...  33.9 us
    pallas_call x2, Pallas kernels, attend_backward(): pl.pallas_call(attend_backward_kernel, grid=(length // ROW_TILE,), in_spe...  32.3 us
  transfers between devices with their start and end apart: 64, of which 28 were waited for; matrix products, arithmetic and copies ran while one was open for 15% of the time, Pallas kernels for 26%

profile of v4, /device:TPU:0, one launch (start us, length us, event | category | flops | bytes accessed | tf_op | source)
XLA Modules:
  0.0 826.6 jit_solution(14873844646458393714)
XLA Ops:
  12.2 29.8 %all-gather.10.cloned.1.call-done = bf16[2048,512]{1,0:T(8,128)(2,1)} async-done(((bf16[256,512]{1,0:T(8,128)(2,1)}), bf16[2048,512]{1,0:T(8,128)(2,1)}) %all-gather.10.cloned.1.call-update) | async-done | bytes 2097168 | tf_op jit(solution)/shard_map/all_gather | solution.py:717
  44.9 5.0 fusion.29
  51.4 6.1 collective-permute-done
  59.2 5.5 collective-permute-done.2
  68.7 17.4 %collective-permute-done.1 = bf16[2048,256]{1,0:T(8,128)(2,1)S(1)} collective-permute-done((bf16[2048,256]{1,0:T(8,128)(2,1)S(1)}, bf16[2048,256]{1,0:T(8,128)(2,1)S(1)}, u32[]{:S(2)}, u32[]{:S(2)}) %collective-permute-start.1) | collective-permute-done | bytes 1048608 | tf_op jit(solution)/shard_map/ppermute | solution.py:492
  91.5 13.7 %attend_forward.2 = (bf16[6,1024,128]{2,1,0:T(8,128)(2,1)}, bf16[1024,256]{1,0:T(8,128)(2,1)}, f32[2,2,1,512]{3,2,1,0:T(1,128)}) custom-call(bf16[1024,2048]{1,0:T(8,128)(2,1)} %bitcast.169, bf16[3,2048,256]{2,1,0:T(8,128)(2,1)} %bitcast.173, f32[3,1,256]{2,1,0:T(1,128)} %broadcast_in_dim.8.b_ref, f32[1024,128]{1,0:T(8,128)} %get-tuple-element.337.cos_ref, ...), custom_call_target="tpu_custom_call" | custom-call | flops 199999995904 | bytes 1024 | tf_op jit(solution)/shard_map/attend_forward/pallas_call | solution.py:94
  105.2 4.4 all-to-all-start
  110.6 2.9 pad_maximum_fusion.14
  114.1 25.4 %all-to-all-done = bf16[8,128,256]{2,1,0:T(8,128)(2,1)} async-done(((bf16[8,128,256]{2,1,0:T(8,128)(2,1)}), bf16[8,128,256]{2,1,0:T(8,128)(2,1)}, u32[]{:S(2)}, u32[]{:S(2)}) %all-to-all-start) | async-done | bytes 524320 | tf_op jit(solution)/shard_map/all_to_all | solution.py:787
  140.6 4.0 broadcast_select_fusion.1
  150.7 13.7 %attend_forward.3 = (bf16[6,1024,128]{2,1,0:T(8,128)(2,1)}, bf16[1024,256]{1,0:T(8,128)(2,1)}, f32[2,2,1,512]{3,2,1,0:T(1,128)}) custom-call(bf16[1024,2048]{1,0:T(8,128)(2,1)} %bitcast.171, bf16[3,2048,256]{2,1,0:T(8,128)(2,1)} %bitcast.174, f32[3,1,256]{2,1,0:T(1,128)} %broadcast_in_dim.8.b_ref, f32[1024,128]{1,0:T(8,128)} %get-tuple-element.339.cos_ref, ...), custom_call_target="tpu_custom_call" | custom-call | flops 199999995904 | bytes 1024 | tf_op jit(solution)/shard_map/attend_forward/pallas_call | solution.py:94
  164.5 3.6 all-to-all-start.1
  170.0 27.9 %all-to-all-done.1 = bf16[8,128,256]{2,1,0:T(8,128)(2,1)S(1)} async-done(((bf16[8,128,256]{2,1,0:T(8,128)(2,1)}), bf16[8,128,256]{2,1,0:T(8,128)(2,1)S(1)}, u32[]{:S(2)}, u32[]{:S(2)}) %all-to-all-start.1) | async-done | bytes 524320 | tf_op jit(solution)/shard_map/all_to_all | solution.py:787
  197.9 4.8 fusion.50
  205.8 2.8 all-gather.12.cloned.1.call-done.h_ref.refs_4_
  208.6 16.9 %glu_forward.2 = (bf16[688,1024]{1,0:T(8,128)(2,1)}, bf16[688,1024]{1,0:T(8,128)(2,1)}, bf16[688,1024]{1,0:T(8,128)(2,1)}, bf16[1024,2048]{1,0:T(8,128)(2,1)}) custom-call(s32[1]{0:T(128)} %bitcast.14.live_ref, bf16[1024,2048]{1,0:T(8,128)(2,1)} %all-gather.12.cloned.1.call-done.h_ref.refs_4_, bf16[688,2048]{1,0:T(8,128)(2,1)} %bitcast.217, ...), custom_call_target="tpu_custom_call" | custom-call | flops 199999995904 | bytes 1024 | tf_op jit(solution)/shard_map/glu_forward/pallas_call | solution.py:259
  225.5 30.9 %all-gather.14.cloned.1.call-done.h_ref.refs_5_ = bf16[1024,2048]{1,0:T(8,128)(2,1)} async-done(((bf16[128,2048]{1,0:T(8,128)(2,1)}), bf16[1024,2048]{1,0:T(8,128)(2,1)}) %all-gather.14.cloned.1.call-update) | async-done | bytes 4194320 | tf_op jit(solution)/shard_map/all_gather | solution.py:717
  256.4 17.0 %glu_forward.3 = (bf16[688,1024]{1,0:T(8,128)(2,1)}, bf16[688,1024]{1,0:T(8,128)(2,1)}, bf16[688,1024]{1,0:T(8,128)(2,1)}, bf16[1024,2048]{1,0:T(8,128)(2,1)}) custom-call(s32[1]{0:T(128)} %bitcast.14.live_ref, bf16[1024,2048]{1,0:T(8,128)(2,1)} %all-gather.14.cloned.1.call-done.h_ref.refs_5_, bf16[688,2048]{1,0:T(8,128)(2,1)} %bitcast.218, ...), custom_call_target="tpu_custom_call" | custom-call | flops 199999995904 | bytes 1024 | tf_op jit(solution)/shard_map/glu_forward/pallas_call | solution.py:259
  273.6 34.3 %reduce-scatter.7.cloned.1.call-done = bf16[128,2048]{1,0:T(8,128)(2,1)} async-done(((bf16[1024,2048]{1,0:T(8,128)(2,1)}), bf16[128,2048]{1,0:T(8,128)(2,1)}) %reduce-scatter.7.cloned.1.call-update) | async-done | bytes 524304 | tf_op jit(solution)/shard_map/reduce_scatter | solution.py:720
  316.5 42.5 %reduce-scatter.9.cloned.1.call-done = bf16[128,2048]{1,0:T(8,128)(2,1)} async-done(((bf16[1024,2048]{1,0:T(8,128)(2,1)}), bf16[128,2048]{1,0:T(8,128)(2,1)}) %reduce-scatter.9.cloned.1.call-update) | async-done | bytes 524304 | tf_op jit(solution)/shard_map/reduce_scatter | solution.py:720
  365.7 40.7 %all-gather.16.cloned.1.call-done.g_ref.refs_2_ = bf16[1024,2048]{1,0:T(8,128)(2,1)} async-done(((bf16[128,2048]{1,0:T(8,128)(2,1)}), bf16[1024,2048]{1,0:T(8,128)(2,1)}) %all-gather.16.cloned.1.call-update) | async-done | bytes 4194320 | tf_op jit(solution)/shard_map/all_gather | solution.py:717
  406.4 22.6 %glu_backward.2 = (bf16[688,1024]{1,0:T(8,128)(2,1)}, bf16[688,1024]{1,0:T(8,128)(2,1)}, f32[688,1]{1,0:T(8,128)}, f32[688,1]{1,0:T(8,128)}, bf16[1024,2048]{1,0:T(8,128)(2,1)}) custom-call(s32[1]{0:T(128)} %bitcast.14.live_ref, bf16[1024,2048]{1,0:T(8,128)(2,1)} %all-gather.16.cloned.1.call-done.g_ref.refs_2_, bf16[688,2048]{1,0:T(8,128)(2,1)} %bitcast.219, ...), custom_call_target="tpu_custom_call" | custom-call | flops 199999995904 | bytes 1024 | tf_op jit(solution)/shard_map/glu_backward/pallas_call | solution.py:322
  429.1 25.4 %all-gather.18.cloned.1.call-done.refs_3_.g_ref = bf16[1024,2048]{1,0:T(8,128)(2,1)} async-done(((bf16[128,2048]{1,0:T(8,128)(2,1)}), bf16[1024,2048]{1,0:T(8,128)(2,1)}) %all-gather.18.cloned.1.call-update) | async-done | bytes 4194320 | tf_op jit(solution)/shard_map/all_gather | solution.py:717
  454.5 11.5 %weight_grad.2 = (bf16[1,688,512]{2,1,0:T(8,128)(2,1)}, bf16[1,688,512]{2,1,0:T(8,128)(2,1)}, bf16[1,688,512]{2,1,0:T(8,128)(2,1)}, bf16[1,688,512]{2,1,0:T(8,128)(2,1)}) custom-call(s32[4]{0:T(128)} %pad_add_fusion.blocks_ref, bf16[688,1024]{1,0:T(8,128)(2,1)} %get-tuple-element.142.refs_0_, bf16[688,1024]{1,0:T(8,128)(2,1)} %get-tuple-element.143.refs_1_, ...), custom_call_target="tpu_custom_call" | custom-call | flops 199999995904 | bytes 1024 | tf_op jit(solution)/shard_map/weight_grad/pallas_call | solution.py:361
  469.0 22.9 %glu_backward.3 = (bf16[688,1024]{1,0:T(8,128)(2,1)}, bf16[688,1024]{1,0:T(8,128)(2,1)}, f32[688,1]{1,0:T(8,128)}, f32[688,1]{1,0:T(8,128)}, bf16[1024,2048]{1,0:T(8,128)(2,1)}) custom-call(s32[1]{0:T(128)} %bitcast.14.live_ref, bf16[1024,2048]{1,0:T(8,128)(2,1)} %all-gather.18.cloned.1.call-done.refs_3_.g_ref, bf16[688,2048]{1,0:T(8,128)(2,1)} %bitcast.220, ...), custom_call_target="tpu_custom_call" | custom-call | flops 199999995904 | bytes 1024 | tf_op jit(solution)/shard_map/glu_backward/pallas_call | solution.py:322
  498.3 19.2 %weight_grad.3 = (bf16[2,688,512]{2,1,0:T(8,128)(2,1)}, bf16[2,688,512]{2,1,0:T(8,128)(2,1)}, bf16[2,688,512]{2,1,0:T(8,128)(2,1)}, bf16[2,688,512]{2,1,0:T(8,128)(2,1)}) custom-call(s32[4]{0:T(128)} %pad_add_fusion.blocks_ref, bf16[688,1024]{1,0:T(8,128)(2,1)} %get-tuple-element.154.refs_0_, bf16[688,1024]{1,0:T(8,128)(2,1)} %get-tuple-element.155.refs_1_, ...), custom_call_target="tpu_custom_call" | custom-call | flops 199999995904 | bytes 1024 | tf_op jit(solution)/shard_map/weight_grad/pallas_call | solution.py:361
  529.0 3.1 convolution_convert_fusion.1
  532.9 3.5 all-to-all-start.2
  537.6 20.9 %collective-permute-done.11 = bf16[688,256]{1,0:T(8,128)(2,1)S(1)} collective-permute-done((bf16[688,256]{1,0:T(8,128)(2,1)S(1)}, bf16[688,256]{1,0:T(8,128)(2,1)S(1)}, u32[]{:S(2)}, u32[]{:S(2)}) %collective-permute-start.11) | collective-permute-done | bytes 352288 | tf_op jit(solution)/shard_map/ppermute | solution.py:492
  570.7 16.2 %attend_backward.2 = (bf16[3,1024,256]{2,1,0:T(8,128)(2,1)}, f32[3,1,256]{2,1,0:T(1,128)}, bf16[1024,2048]{1,0:T(8,128)(2,1)}) custom-call(bf16[6,1024,128]{2,1,0:T(8,128)(2,1)} %get-tuple-element.136.qkv_ref, bf16[1024,256]{1,0:T(8,128)(2,1)} %bitcast.183, f32[2,2,1,512]{3,2,1,0:T(1,128)} %get-tuple-element.170.lse_ref, s32[2,1,512]{2,1,0:T(1,128)} %bitcast.205, ...), custom_call_target="tpu_custom_call" | custom-call | flops 199999995904 | bytes 1024 | tf_op jit(solution)/shard_map/attend_backward/pallas_call | solution.py:199
  587.0 3.8 collective-permute-done.13
  604.1 3.8 convolution_convert_fusion
  607.9 4.4 collective-permute-done.17
  618.0 5.4 assemble.3
  623.4 10.6 %row_grad.1 = (bf16[1024,2048]{1,0:T(8,128)(2,1)}, bf16[1024,2048]{1,0:T(8,128)(2,1)}) custom-call(s32[2]{0:T(128)} %pad_add_fusion.1.sides_ref, bf16[256,2048]{1,0:T(8,128)(2,1)} %pad_maximum_fusion.8.left_ref, bf16[256,2048]{1,0:T(8,128)(2,1)} %pad_maximum_fusion.9.right_ref), custom_call_target="tpu_custom_call" | custom-call | flops 1024 | bytes 1024 | tf_op jit(solution)/shard_map/row_grad/pallas_call | solution.py:427
  634.8 3.5 all-to-all-start.3
  640.5 13.1 %all-to-all-done.3 = bf16[128,8,256]{2,0,1:T(8,128)(2,1)S(1)} async-done(((bf16[128,8,256]{2,0,1:T(8,128)(2,1)}), bf16[128,8,256]{2,0,1:T(8,128)(2,1)S(1)}, u32[]{:S(2)}, u32[]{:S(2)}) %all-to-all-start.3) | async-done | bytes 524320 | tf_op jit(solution)/shard_map/all_to_all | solution.py:876
  654.4 16.1 %attend_backward.3 = (bf16[3,1024,256]{2,1,0:T(8,128)(2,1)}, f32[3,1,256]{2,1,0:T(1,128)}, bf16[1024,2048]{1,0:T(8,128)(2,1)}) custom-call(bf16[6,1024,128]{2,1,0:T(8,128)(2,1)} %get-tuple-element.172.qkv_ref, bf16[1024,256]{1,0:T(8,128)(2,1)} %bitcast.177, f32[2,2,1,512]{3,2,1,0:T(1,128)} %get-tuple-element.185.lse_ref, s32[2,1,512]{2,1,0:T(1,128)} %bitcast.189, ...), custom_call_target="tpu_custom_call" | custom-call | flops 1024 | bytes 1024 | tf_op jit(solution)/shard_map/attend_backward/pallas_call | solution.py:199
  670.5 4.1 add_convert_fusion
  685.5 12.7 %slab_grad.1 = (bf16[3,512,256]{2,1,0:T(8,128)(2,1)}, bf16[3,512,256]{2,1,0:T(8,128)(2,1)}, bf16[3,512,256]{2,1,0:T(8,128)(2,1)}, bf16[3,512,256]{2,1,0:T(8,128)(2,1)}) custom-call(s32[4]{0:T(128)} %pad_add_fusion.3.blocks_ref.sources_ref, bf16[1024,2048]{1,0:T(8,128)(2,1)} %bitcast.170, bf16[1024,2048]{1,0:T(8,128)(2,1)} %bitcast.172, ...), custom_call_target="tpu_custom_call" | custom-call | flops 1024 | bytes 1024 | tf_op jit(solution)/shard_map/slab_grad/pallas_call | solution.py:396
  700.0 8.1 assemble.4
  721.1 18.4 %collective-permute-done.24 = bf16[3,512,256]{2,1,0:T(8,128)(2,1)} collective-permute-done((bf16[3,512,256]{2,1,0:T(8,128)(2,1)}, bf16[3,512,256]{2,1,0:T(8,128)(2,1)}, u32[]{:S(2)}, u32[]{:S(2)}) %collective-permute-start.24) | collective-permute-done | bytes 786464 | tf_op jit(solution)/shard_map/ppermute | solution.py:596
  742.7 5.6 collective-permute-done.32
  749.7 2.9 collective-permute-done.33
  756.1 10.5 %slice_bitcast_fusion = (f32[2048,688]{0,1:T(8,128)}, f32[2048,688]{0,1:T(8,128)}) fusion(f32[2,688,2048]{2,1,0:T(8,128)} %assemble.4), kind=kLoop, calls=%fused_computation.2 | loop fusion | bytes 22544384 | tf_op jit(solution)/shard_map/transpose | solution.py:953
  770.1 17.9 %collective-permute-done.41 = bf16[512,512]{1,0:T(8,128)(2,1)S(1)} collective-permute-done((bf16[512,512]{1,0:T(8,128)(2,1)S(1)}, bf16[512,512]{1,0:T(8,128)(2,1)S(1)}, u32[]{:S(2)}, u32[]{:S(2)}) %collective-permute-start.41) | collective-permute-done | bytes 524320 | tf_op jit(solution)/shard_map/ppermute | solution.py:492
  789.5 6.2 collective-permute-done.42
  806.2 5.7 assemble.5
  (500 shorter events, 162.2 us)
Async XLA Ops:
  7.2 34.8 %all-gather.10.cloned.1.call-start = ((), (), s32[]{:S(2)}) async-start(), calls=%async_computation.10 | async-start | bytes 2359296 | tf_op jit(solution)/shard_map/all_gather | solution.py:717
  9.7 81.8 %all-gather.20.cloned.1.call-start = ((), (), s32[]{:S(2)}) async-start(), calls=%async_computation.21 | async-start | bytes 4718592 | tf_op jit(solution)/shard_map/all_gather | solution.py:717
  10.8 139.9 %all-gather.22.cloned.1.call-start = ((), (), s32[]{:S(2)}) async-start(), calls=%async_computation.22 | async-start | bytes 4718592 | tf_op jit(solution)/shard_map/all_gather | solution.py:717
  57.7 28.5 %collective-permute-start.1 = (bf16[2048,256]{1,0:T(8,128)(2,1)S(1)}, bf16[2048,256]{1,0:T(8,128)(2,1)S(1)}, u32[]{:S(2)}, u32[]{:S(2)}) collective-permute-start(bf16[2048,256]{1,0:T(8,128)(2,1)S(1)} %pad_maximum_fusion.5), channel_id=1, source_target_pairs={{0,8},{8,0},{16,24},{24,16},{1,9},{9,1},{17,25},{25,17},{2,10},{10... | collective-permute-start | bytes 3145736 | tf_op jit(solution)/shard_map/ppermute | solution.py:492
  64.9 23.3 %collective-permute-start.3 = (bf16[2048,256]{1,0:T(8,128)(2,1)S(1)}, bf16[2048,256]{1,0:T(8,128)(2,1)S(1)}, u32[]{:S(2)}, u32[]{:S(2)}) collective-permute-start(bf16[2048,256]{1,0:T(8,128)(2,1)S(1)} %pad_maximum_fusion.6), channel_id=1, source_target_pairs={{0,16},{8,24},{16,0},{24,8},{1,17},{9,25},{17,1},{25,9},{2,18},{10... | collective-permute-start | bytes 3145736 | tf_op jit(solution)/shard_map/ppermute | solution.py:492
  91.4 49.2 %collective-permute-start.4 = (bf16[2048,1024]{1,0:T(8,128)(2,1)}, bf16[2048,1024]{1,0:T(8,128)(2,1)}, u32[]{:S(2)}, u32[]{:S(2)}) collective-permute-start(bf16[2048,1024]{1,0:T(8,128)(2,1)} %pad_maximum_fusion.1), channel_id=1, source_target_pairs={{0,1},{1,0},{2,3},{3,2},{4,5},{5,4},{6,7},{7,6},{8,9},{9,8},{10,11... | collective-permute-start | bytes 12582920 | tf_op jit(solution)/shard_map/ppermute | solution.py:492
  105.2 34.2 %all-to-all-start = ((bf16[8,128,256]{2,1,0:T(8,128)(2,1)}), bf16[8,128,256]{2,1,0:T(8,128)(2,1)}, u32[]{:S(2)}, u32[]{:S(2)}) async-start(bf16[8,128,256]{2,1,0:T(8,128)(2,1)} %bitcast.185), calls=%async_computation | async-start | bytes 1048576 | tf_op jit(solution)/shard_map/all_to_all | solution.py:787
  109.7 98.9 %all-gather.12.cloned.1.call-start = ((), (), s32[]{:S(2)}) async-start(), calls=%async_computation.11 | async-start | bytes 4718592 | tf_op jit(solution)/shard_map/all_gather | solution.py:717
  164.5 33.4 %all-to-all-start.1 = ((bf16[8,128,256]{2,1,0:T(8,128)(2,1)}), bf16[8,128,256]{2,1,0:T(8,128)(2,1)S(1)}, u32[]{:S(2)}, u32[]{:S(2)}) async-start(bf16[8,128,256]{2,1,0:T(8,128)(2,1)} %bitcast.186), calls=%async_computation.1 | async-start | bytes 1048576 | tf_op jit(solution)/shard_map/all_to_all | solution.py:787
  168.1 88.3 %all-gather.14.cloned.1.call-start = ((), (), s32[]{:S(2)}) async-start(), calls=%async_computation.13 | async-start | bytes 4718592 | tf_op jit(solution)/shard_map/all_gather | solution.py:717
  205.3 102.6 %reduce-scatter.7.cloned.1.call-start = ((), (), s32[]{:S(2)}) async-start(), calls=%async_computation.12 | async-start | bytes 4718592 | tf_op jit(solution)/shard_map/reduce_scatter | solution.py:720
  225.5 133.5 %reduce-scatter.9.cloned.1.call-start = ((), (), s32[]{:S(2)}) async-start(), calls=%async_computation.14 | async-start | bytes 4718592 | tf_op jit(solution)/shard_map/reduce_scatter | solution.py:720
  273.6 132.9 %all-gather.16.cloned.1.call-start = ((), (), s32[]{:S(2)}) async-start(), calls=%async_computation.15 | async-start | bytes 4718592 | tf_op jit(solution)/shard_map/all_gather | solution.py:717
  314.6 140.0 %all-gather.18.cloned.1.call-start = ((), (), s32[]{:S(2)}) async-start(), calls=%async_computation.17 | async-start | bytes 4718592 | tf_op jit(solution)/shard_map/all_gather | solution.py:717
  365.5 158.5 %reduce-scatter.11.cloned.1.call-start = ((), (), s32[]{:S(2)}) async-start(), calls=%async_computation.16 | async-start | bytes 4718592 | tf_op jit(solution)/shard_map/reduce_scatter | solution.py:720
  466.1 25.8 %collective-permute-start.5 = (bf16[688,512]{1,0:T(8,128)(2,1)}, bf16[688,512]{1,0:T(8,128)(2,1)}, u32[]{:S(2)}, u32[]{:S(2)}) collective-permute-start(bf16[688,512]{1,0:T(8,128)(2,1)} %bitcast.226), channel_id=1, source_target_pairs={{0,8},{8,0},{16,24},{24,16},{1,9},{9,1},{17,25},{25,17},{2,10},{10... | collective-permute-start | bytes 2113544 | tf_op jit(solution)/shard_map/ppermute | solution.py:492
  467.5 24.4 %collective-permute-start.6 = (bf16[688,512]{1,0:T(8,128)(2,1)}, bf16[688,512]{1,0:T(8,128)(2,1)}, u32[]{:S(2)}, u32[]{:S(2)}) collective-permute-start(bf16[688,512]{1,0:T(8,128)(2,1)} %bitcast.225), channel_id=1, source_target_pairs={{0,16},{8,24},{16,0},{24,8},{1,17},{9,25},{17,1},{25,9},{2,18},{10... | collective-permute-start | bytes 2113544 | tf_op jit(solution)/shard_map/ppermute | solution.py:492
  497.1 23.4 %collective-permute-start.7 = (bf16[688,256]{1,0:T(8,128)(2,1)}, bf16[688,256]{1,0:T(8,128)(2,1)}, u32[]{:S(2)}, u32[]{:S(2)}) collective-permute-start(bf16[688,256]{1,0:T(8,128)(2,1)} %constant_dynamic-slice_fusion.8), channel_id=1, source_target_pairs={{0,16},{8,24},{16,0},{24,8},{1,17},{9,25},{17,1},{25,9},{2,18},{10... | collective-permute-start | bytes 1056776 | tf_op jit(solution)/shard_map/ppermute | solution.py:492
  497.7 22.9 %collective-permute-start.8 = (bf16[688,256]{1,0:T(8,128)(2,1)}, bf16[688,256]{1,0:T(8,128)(2,1)}, u32[]{:S(2)}, u32[]{:S(2)}) collective-permute-start(bf16[688,256]{1,0:T(8,128)(2,1)} %constant_dynamic-slice_fusion.7), channel_id=1, source_target_pairs={{0,8},{8,0},{16,24},{24,16},{1,9},{9,1},{17,25},{25,17},{2,10},{10... | collective-permute-start | bytes 1056776 | tf_op jit(solution)/shard_map/ppermute | solution.py:492
  517.6 45.0 %collective-permute-start.9 = (bf16[2,688,512]{2,1,0:T(8,128)(2,1)}, bf16[2,688,512]{2,1,0:T(8,128)(2,1)}, u32[]{:S(2)}, u32[]{:S(2)}) collective-permute-start(bf16[2,688,512]{2,1,0:T(8,128)(2,1)} %get-tuple-element.158), channel_id=1, source_target_pairs={{0,8},{8,0},{16,24},{24,16},{1,9},{9,1},{17,25},{25,17},{2,10},{10... | collective-permute-start | bytes 4227080 | tf_op jit(solution)/shard_map/ppermute | solution.py:492
  519.0 43.6 %collective-permute-start.10 = (bf16[2,688,512]{2,1,0:T(8,128)(2,1)}, bf16[2,688,512]{2,1,0:T(8,128)(2,1)}, u32[]{:S(2)}, u32[]{:S(2)}) collective-permute-start(bf16[2,688,512]{2,1,0:T(8,128)(2,1)} %get-tuple-element.159), channel_id=1, source_target_pairs={{0,16},{8,24},{16,0},{24,8},{1,17},{9,25},{17,1},{25,9},{2,18},{10... | collective-permute-start | bytes 4227080 | tf_op jit(solution)/shard_map/ppermute | solution.py:492
  521.6 36.9 %collective-permute-start.11 = (bf16[688,256]{1,0:T(8,128)(2,1)S(1)}, bf16[688,256]{1,0:T(8,128)(2,1)S(1)}, u32[]{:S(2)}, u32[]{:S(2)}) collective-permute-start(bf16[688,256]{1,0:T(8,128)(2,1)S(1)} %add_convert_fusion.14), channel_id=1, source_target_pairs={{0,16},{8,24},{16,0},{24,8},{1,17},{9,25},{17,1},{25,9},{2,18},{10... | collective-permute-start | bytes 1056776 | tf_op jit(solution)/shard_map/ppermute | solution.py:492
  523.3 35.2 %collective-permute-start.12 = (bf16[688,256]{1,0:T(8,128)(2,1)S(1)}, bf16[688,256]{1,0:T(8,128)(2,1)S(1)}, u32[]{:S(2)}, u32[]{:S(2)}) collective-permute-start(bf16[688,256]{1,0:T(8,128)(2,1)S(1)} %add_convert_fusion.13), channel_id=1, source_target_pairs={{0,8},{8,0},{16,24},{24,16},{1,9},{9,1},{17,25},{25,17},{2,10},{10... | collective-permute-start | bytes 1056776 | tf_op jit(solution)/shard_map/ppermute | solution.py:492
  532.9 29.8 %all-to-all-start.2 = ((bf16[128,8,256]{2,0,1:T(8,128)(2,1)}), bf16[128,8,256]{2,0,1:T(8,128)(2,1)S(1)}, u32[]{:S(2)}, u32[]{:S(2)}) async-start(bf16[128,8,256]{2,0,1:T(8,128)(2,1)} %bitcast.159), calls=%async_computation.5 | async-start | bytes 1048576 | tf_op jit(solution)/shard_map/all_to_all | solution.py:876
  536.4 62.3 %reduce-scatter.15.cloned.1.call-start = ((), (), s32[]{:S(2)}) async-start(), calls=%async_computation.19 | async-start | bytes 4718592 | tf_op jit(solution)/shard_map/reduce_scatter | solution.py:720
  537.5 278.2 %reduce-scatter.13.cloned.1.call-start = ((), (), s32[]{:S(2)}) async-start(), calls=%async_computation.18 | async-start | bytes 4718592 | tf_op jit(solution)/shard_map/reduce_scatter | solution.py:720
  559.6 58.4 %collective-permute-start.16 = (bf16[688,512]{1,0:T(8,128)(2,1)}, bf16[688,512]{1,0:T(8,128)(2,1)}, u32[]{:S(2)}, u32[]{:S(2)}) collective-permute-start(bf16[688,512]{1,0:T(8,128)(2,1)} %pad_maximum_fusion.11.refs_1_), channel_id=1, source_target_pairs={{0,16},{8,24},{16,0},{24,8},{1,17},{9,25},{17,1},{25,9},{2,18},{10... | collective-permute-start | bytes 2113544 | tf_op jit(solution)/shard_map/ppermute | solution.py:492
  562.0 55.9 %collective-permute-start.15 = (bf16[688,512]{1,0:T(8,128)(2,1)}, bf16[688,512]{1,0:T(8,128)(2,1)}, u32[]{:S(2)}, u32[]{:S(2)}) collective-permute-start(bf16[688,512]{1,0:T(8,128)(2,1)} %pad_maximum_fusion.10.refs_0_), channel_id=1, source_target_pairs={{0,8},{8,0},{16,24},{24,16},{1,9},{9,1},{17,25},{25,17},{2,10},{10... | collective-permute-start | bytes 2113544 | tf_op jit(solution)/shard_map/ppermute | solution.py:492
  568.7 22.1 %collective-permute-start.13 = (bf16[2,688,256]{2,1,0:T(8,128)(2,1)}, bf16[2,688,256]{2,1,0:T(8,128)(2,1)}, u32[]{:S(2)}, u32[]{:S(2)}) collective-permute-start(bf16[2,688,256]{2,1,0:T(8,128)(2,1)} %constant_dynamic-slice_fusion.6), channel_id=1, source_target_pairs={{0,16},{8,24},{16,0},{24,8},{1,17},{9,25},{17,1},{25,9},{2,18},{10... | collective-permute-start | bytes 2113544 | tf_op jit(solution)/shard_map/ppermute | solution.py:492
  569.2 23.7 %collective-permute-start.14 = (bf16[2,688,256]{2,1,0:T(8,128)(2,1)}, bf16[2,688,256]{2,1,0:T(8,128)(2,1)}, u32[]{:S(2)}, u32[]{:S(2)}) collective-permute-start(bf16[2,688,256]{2,1,0:T(8,128)(2,1)} %constant_dynamic-slice_fusion.5), channel_id=1, source_target_pairs={{0,8},{8,0},{16,24},{24,16},{1,9},{9,1},{17,25},{25,17},{2,10},{10... | collective-permute-start | bytes 2113544 | tf_op jit(solution)/shard_map/ppermute | solution.py:492
  634.0 36.5 %collective-permute-start.19 = (bf16[1024,2048]{1,0:T(8,128)(2,1)}, bf16[1024,2048]{1,0:T(8,128)(2,1)}, u32[]{:S(2)}, u32[]{:S(2)}) collective-permute-start(bf16[1024,2048]{1,0:T(8,128)(2,1)} %get-tuple-element.183), channel_id=1, source_target_pairs={{0,1},{1,0},{2,3},{3,2},{4,5},{5,4},{6,7},{7,6},{8,9},{9,8},{10,11... | collective-permute-start | bytes 12582920 | tf_op jit(solution)/shard_map/ppermute | solution.py:492
  634.8 18.8 %all-to-all-start.3 = ((bf16[128,8,256]{2,0,1:T(8,128)(2,1)}), bf16[128,8,256]{2,0,1:T(8,128)(2,1)S(1)}, u32[]{:S(2)}, u32[]{:S(2)}) async-start(bf16[128,8,256]{2,0,1:T(8,128)(2,1)} %bitcast.158), calls=%async_computation.8 | async-start | bytes 1048576 | tf_op jit(solution)/shard_map/all_to_all | solution.py:876
  638.3 178.6 %reduce-scatter.17.cloned.1.call-start = ((), (), s32[]{:S(2)}) async-start(), calls=%async_computation.20 | async-start | bytes 4718592 | tf_op jit(solution)/shard_map/reduce_scatter | solution.py:720
  638.4 47.1 %collective-permute-start.22 = (bf16[2,688,512]{2,1,0:T(8,128)(2,1)}, bf16[2,688,512]{2,1,0:T(8,128)(2,1)}, u32[]{:S(2)}, u32[]{:S(2)}) collective-permute-start(bf16[2,688,512]{2,1,0:T(8,128)(2,1)} %pad_maximum_fusion.4.refs_1_), channel_id=1, source_target_pairs={{0,16},{8,24},{16,0},{24,8},{1,17},{9,25},{17,1},{25,9},{2,18},{10... | collective-permute-start | bytes 4227080 | tf_op jit(solution)/shard_map/ppermute | solution.py:492
  639.8 45.7 %collective-permute-start.21 = (bf16[2,688,512]{2,1,0:T(8,128)(2,1)}, bf16[2,688,512]{2,1,0:T(8,128)(2,1)}, u32[]{:S(2)}, u32[]{:S(2)}) collective-permute-start(bf16[2,688,512]{2,1,0:T(8,128)(2,1)} %pad_maximum_fusion.3.refs_0_), channel_id=1, source_target_pairs={{0,8},{8,0},{16,24},{24,16},{1,9},{9,1},{17,25},{25,17},{2,10},{10... | collective-permute-start | bytes 4227080 | tf_op jit(solution)/shard_map/ppermute | solution.py:492
  677.5 30.6 %collective-permute-start.27 = (bf16[1024,512]{1,0:T(8,128)(2,1)}, bf16[1024,512]{1,0:T(8,128)(2,1)}, u32[]{:S(2)}, u32[]{:S(2)}) collective-permute-start(bf16[1024,512]{1,0:T(8,128)(2,1)} %constant_dynamic-slice_fusion.4), channel_id=1, source_target_pairs={{0,8},{8,0},{16,24},{24,16},{1,9},{9,1},{17,25},{25,17},{2,10},{10... | collective-permute-start | bytes 3145736 | tf_op jit(solution)/shard_map/ppermute | solution.py:492
  679.3 30.5 %collective-permute-start.28 = (bf16[1024,512]{1,0:T(8,128)(2,1)}, bf16[1024,512]{1,0:T(8,128)(2,1)}, u32[]{:S(2)}, u32[]{:S(2)}) collective-permute-start(bf16[1024,512]{1,0:T(8,128)(2,1)} %constant_dynamic-slice_fusion.3), channel_id=1, source_target_pairs={{0,16},{8,24},{16,0},{24,8},{1,17},{9,25},{17,1},{25,9},{2,18},{10... | collective-permute-start | bytes 3145736 | tf_op jit(solution)/shard_map/ppermute | solution.py:492
  685.4 31.5 %collective-permute-start.26 = (f32[6,2048]{1,0:T(8,128)S(1)}, f32[6,2048]{1,0:T(8,128)S(1)}, u32[]{:S(2)}, u32[]{:S(2)}) collective-permute-start(f32[6,2048]{1,0:T(8,128)S(1)} %add.479), channel_id=1, source_target_pairs={{0,2},{1,3},{2,0},{3,1},{4,6},{5,7},{6,4},{7,5},{8,10},{9,11},{10,... | collective-permute-start | bytes 147464 | tf_op jit(solution)/shard_map/ppermute | solution.py:492
  698.2 22.1 %collective-permute-start.23 = (bf16[3,512,256]{2,1,0:T(8,128)(2,1)}, bf16[3,512,256]{2,1,0:T(8,128)(2,1)}, u32[]{:S(2)}, u32[]{:S(2)}) collective-permute-start(bf16[3,512,256]{2,1,0:T(8,128)(2,1)} %get-tuple-element.197), channel_id=1, source_target_pairs={{0,8},{8,0},{16,24},{24,16},{1,9},{9,1},{17,25},{25,17},{2,10},{10... | collective-permute-start | bytes 2359304 | tf_op jit(solution)/shard_map/ppermute | solution.py:596
  699.2 40.2 %collective-permute-start.24 = (bf16[3,512,256]{2,1,0:T(8,128)(2,1)}, bf16[3,512,256]{2,1,0:T(8,128)(2,1)}, u32[]{:S(2)}, u32[]{:S(2)}) collective-permute-start(bf16[3,512,256]{2,1,0:T(8,128)(2,1)} %get-tuple-element.198), channel_id=1, source_target_pairs={{0,16},{8,24},{16,0},{24,8},{1,17},{9,25},{17,1},{25,9},{2,18},{10... | collective-permute-start | bytes 2359304 | tf_op jit(solution)/shard_map/ppermute | solution.py:596
  708.1 32.6 %collective-permute-start.25 = (bf16[3,512,256]{2,1,0:T(8,128)(2,1)}, bf16[3,512,256]{2,1,0:T(8,128)(2,1)}, u32[]{:S(2)}, u32[]{:S(2)}) collective-permute-start(bf16[3,512,256]{2,1,0:T(8,128)(2,1)} %get-tuple-element.199), channel_id=1, source_target_pairs={{0,24},{8,16},{16,8},{24,0},{1,25},{9,17},{17,9},{25,1},{2,26},{10... | collective-permute-start | bytes 2359304 | tf_op jit(solution)/shard_map/ppermute | solution.py:596
  715.8 33.5 %collective-permute-start.37 = (bf16[1024,256]{1,0:T(8,128)(2,1)}, bf16[1024,256]{1,0:T(8,128)(2,1)S(1)}, u32[]{:S(2)}, u32[]{:S(2)}) collective-permute-start(bf16[1024,256]{1,0:T(8,128)(2,1)} %constant_dynamic-slice_fusion.1), channel_id=1, source_target_pairs={{0,8},{8,0},{16,24},{24,16},{1,9},{9,1},{17,25},{25,17},{2,10},{10... | collective-permute-start | bytes 1572872 | tf_op jit(solution)/shard_map/ppermute | solution.py:492
  716.9 32.4 %collective-permute-start.36 = (bf16[1024,256]{1,0:T(8,128)(2,1)}, bf16[1024,256]{1,0:T(8,128)(2,1)S(1)}, u32[]{:S(2)}, u32[]{:S(2)}) collective-permute-start(bf16[1024,256]{1,0:T(8,128)(2,1)} %constant_dynamic-slice_fusion.2), channel_id=1, source_target_pairs={{0,16},{8,24},{16,0},{24,8},{1,17},{9,25},{17,1},{25,9},{2,18},{10... | collective-permute-start | bytes 1572872 | tf_op jit(solution)/shard_map/ppermute | solution.py:492
  720.2 29.5 %collective-permute-start.34 = (f32[1376]{0:T(1024)S(1)}, f32[1376]{0:T(1024)S(1)}, u32[]{:S(2)}, u32[]{:S(2)}) collective-permute-start(f32[1376]{0:T(1024)S(1)} %pad_maximum_fusion.19), channel_id=1, source_target_pairs={{0,8},{8,0},{16,24},{24,16},{1,9},{9,1},{17,25},{25,17},{2,10},{10... | collective-permute-start | bytes 16520 | tf_op jit(solution)/shard_map/ppermute | solution.py:492
  749.6 38.4 %collective-permute-start.41 = (bf16[512,512]{1,0:T(8,128)(2,1)S(1)}, bf16[512,512]{1,0:T(8,128)(2,1)S(1)}, u32[]{:S(2)}, u32[]{:S(2)}) collective-permute-start(bf16[512,512]{1,0:T(8,128)(2,1)S(1)} %fusion.27), channel_id=1, source_target_pairs={{0,4},{1,5},{2,6},{3,7},{4,0},{5,1},{6,2},{7,3},{8,12},{9,13},{10,... | collective-permute-start | bytes 1572872 | tf_op jit(solution)/shard_map/ppermute | solution.py:492
  766.6 32.6 %collective-permute-start.31 = (bf16[3,512,256]{2,1,0:T(8,128)(2,1)S(1)}, bf16[3,512,256]{2,1,0:T(8,128)(2,1)S(1)}, u32[]{:S(2)}, u32[]{:S(2)}) collective-permute-start(bf16[3,512,256]{2,1,0:T(8,128)(2,1)S(1)} %add_convert_fusion.5.refs_0_), channel_id=1, source_target_pairs={{0,24},{8,16},{16,8},{24,0},{1,25},{9,17},{17,9},{25,1},{2,26},{10... | collective-permute-start | bytes 2359304 | tf_op jit(solution)/shard_map/ppermute | solution.py:596
  767.6 31.6 %collective-permute-start.30 = (bf16[3,512,256]{2,1,0:T(8,128)(2,1)S(1)}, bf16[3,512,256]{2,1,0:T(8,128)(2,1)S(1)}, u32[]{:S(2)}, u32[]{:S(2)}) collective-permute-start(bf16[3,512,256]{2,1,0:T(8,128)(2,1)S(1)} %add_convert_fusion.5.refs_0_), channel_id=1, source_target_pairs={{0,16},{8,24},{16,0},{24,8},{1,17},{9,25},{17,1},{25,9},{2,18},{10... | collective-permute-start | bytes 2359304 | tf_op jit(solution)/shard_map/ppermute | solution.py:596
  769.0 30.2 %collective-permute-start.29 = (bf16[3,512,256]{2,1,0:T(8,128)(2,1)S(1)}, bf16[3,512,256]{2,1,0:T(8,128)(2,1)S(1)}, u32[]{:S(2)}, u32[]{:S(2)}) collective-permute-start(bf16[3,512,256]{2,1,0:T(8,128)(2,1)S(1)} %add_convert_fusion.5.refs_0_), channel_id=1, source_target_pairs={{0,8},{8,0},{16,24},{24,16},{1,9},{9,1},{17,25},{25,17},{2,10},{10... | collective-permute-start | bytes 2359304 | tf_op jit(solution)/shard_map/ppermute | solution.py:596
  (135 other events, 1562.0 us)
Sparse Core Ops, SparseCore 0:
  10.2 31.7 all-gather.9
  44.2 46.6 all-gather.19
  93.1 56.9 all-gather.21
  151.5 56.9 all-gather.11
  210.6 45.7 all-gather.13
  259.1 48.7 reduce-scatter.6
  310.8 48.1 reduce-scatter.8
  361.1 45.2 all-gather.15
  408.6 45.8 all-gather.17
  457.2 48.6 reduce-scatter.10
  540.1 50.7 reduce-scatter.14
  593.0 49.9 reduce-scatter.12
  718.0 61.4 reduce-scatter.16

commit v5 on v4

--- a/solution.py
+++ b/solution.py
@@ -23,6 +23,7 @@
 VMEM_LIMIT = 56 * 1024 * 1024
 LONG = pl.CostEstimate(flops=200_000_000_000, bytes_accessed=1024, transcendentals=0)
 SHORT = pl.CostEstimate(flops=1024, bytes_accessed=1024, transcendentals=0)
+MIDDLE = pl.CostEstimate(flops=25_000_000_000, bytes_accessed=1024, transcendentals=0)
 BF16 = jnp.bfloat16
 F32 = jnp.float32
 
@@ -404,7 +405,7 @@
         ),
         out_shape=[jax.ShapeDtypeStruct((3, tile, columns), BF16)] * count,
         compiler_params=pltpu.CompilerParams(vmem_limit_bytes=VMEM_LIMIT),
-        cost_estimate=SHORT,
+        cost_estimate=LONG,
         name="slab_grad",
     )(blocks, *lefts, *rights)
 
@@ -853,13 +854,12 @@
     glu_blocks = weight_grad(
         [[after(gate, last), up] for gate, up in zip(gate_lows, up_lows)], hidden, blocks
     )
-    glu_flow = Flow(sum_stages(glu_blocks, batch_rank, orders, 2, SHORT)).step()
+    glu_flow = Flow(sum_stages(glu_blocks, batch_rank, orders, 2, LONG)).step()
     down_flow.step(glu_flow.sent)
     last = down_flow.sent
 
-    grads_one, attended_lows, lows, input_grads = [], [], [], []
+    grads_one, attended_lows, context_grads = [], [], []
     norm_gain_part = norm_shift_part = out_bias_part = 0.0
-    qkv_bias_part = 0.0
     for p in range(packs):
         normed_grad = (
             after(normed_sums[p], last).astype(F32) + scale_value * grads_two[p]
@@ -872,64 +872,66 @@
         grads_one.append(grad_one)
         attended_lows.append(attended_low)
         context_grad = dot_nt(attended_low, whole_out).astype(BF16)
+        context_grads.append(
+            lax.all_to_all(context_grad, "tensor", split_axis=1, concat_axis=0, tiled=True)
+        )
         last = context_grad
-        context_grad = lax.all_to_all(
-            context_grad, "tensor", split_axis=1, concat_axis=0, tiled=True
-        )
-        if p == packs - 1:
-            last = glu_flow.step(last).sent
-            last = down_flow.step(last).result
-            send, keep = row_grad(
-                after(jnp.concatenate(context_rows, axis=0), last),
-                jnp.concatenate(attended_lows, axis=0),
-                jnp.stack([1 - core, core]).astype(jnp.int32),
-                out_weight.shape[0],
-            )
-            out_flow = Flow(out_scatter_stages(send, keep)).step()
-            last = send
-            shared = jnp.stack(
-                [
-                    out_bias_part,
-                    norm_gain_part,
-                    norm_shift_part,
-                    down_bias_part,
-                    final_gain_part,
-                    final_shift_part,
-                ]
-            )
-            glu_bias = jnp.concatenate([gate_bias_part[:, 0], up_bias_part[:, 0]])
-            small_flow = Flow(
-                small_stages(
-                    shared,
-                    (glu_bias, lambda: qkv_bias_part[:, 0, :]),
-                    batch_size.bit_length() - 1,
-                    tensor_size.bit_length() - 1,
-                )
-            ).step(send)
-        else:
-            down_flow.step(last)
-            last = glu_flow.step(down_flow.sent, context_grad).sent
+        if p == 0:
+            last = [down_flow.step(last).sent, glu_flow.step(last).sent]
+    shared = jnp.stack(
+        [
+            out_bias_part,
+            norm_gain_part,
+            norm_shift_part,
+            down_bias_part,
+            final_gain_part,
+            final_shift_part,
+        ]
+    )
+    glu_bias = jnp.concatenate([gate_bias_part[:, 0], up_bias_part[:, 0]])
+
+    lows, input_grads = [], []
+    qkv_bias_part = 0.0
+    for p in range(packs):
         low, bias_sum, input_part = attend_backward(
-            qkvs[p], after(context_grad, last), log_sums[p], *ranges[p], *tables[p], qkv_slabs,
-            LONG if p < packs - 1 else SHORT,
-        )
-        last = low
+            qkvs[p], after(context_grads[p], last), log_sums[p], *ranges[p], *tables[p], qkv_slabs,
+            MIDDLE,
+        )
         lows.append(low)
         qkv_bias_part += bias_sum
         input_grads.append(
             scatter_rows(input_part).astype(F32) + scale_value * grads_one[p]
         )
-        if p == packs - 1:
-            last = [out_flow.step(low).sent, small_flow.step(low).sent, glu_flow.settle(low)]
-        else:
-            last = glu_flow.step(last).sent
+        last = glu_flow.step(low).sent
+        if p == 0:
+            last = [last, down_flow.settle(low)]
+    send, keep = row_grad(
+        after(jnp.concatenate(context_rows, axis=0), last),
+        jnp.concatenate(attended_lows, axis=0),
+        jnp.stack([1 - core, core]).astype(jnp.int32),
+        out_weight.shape[0],
+    )
+    out_flow = Flow(out_scatter_stages(send, keep)).step()
+    small_flow = Flow(
+        small_stages(
+            shared,
+            (glu_bias, lambda: qkv_bias_part[:, 0, :]),
+            batch_size.bit_length() - 1,
+            tensor_size.bit_length() - 1,
+        )
+    ).step(send)
+    last = out_flow.sent
     qkv_blocks = slab_grad(
         whole_tokens, [after(low, last) for low in lows], peer_blocks(batch_rank, batch_size)
     )
     qkv_flow = Flow(direct_sum_stages(qkv_blocks, batch_rank, batch_size, 1)).step()
     last = qkv_flow.sent
     flows = [down_flow, glu_flow, small_flow, out_flow, qkv_flow]
-    last = glu_flow.step(last).result
+    last = out_flow.step(last).sent
+    last = [last, glu_flow.step(last).result]
+    for flow in (qkv_flow, out_flow, small_flow):
+        last = flow.step(last).sent
+    last = [last, down_flow.step(last).result]
     while any(flow.result is None for flow in flows):
         for flow in (out_flow, small_flow, qkv_flow, small_flow, glu_flow, down_flow):
             if flow.result is None:

time: 836 us -> 857 us (1.025)
  starting transfers between devices: 60.2 us -> 69.6 us
    ppermute x41, waiting for transfers between devices: 97.8 us -> 117 us  [swap_bit(): return lax.ppermute(x, axis_name, [(i, i ^ 1 << bit) for i in range(size)])]
    all_to_all x2, waiting for transfers between devices: 13.1 us -> 0.01 us  [per_device(): lax.all_to_all(context_grad, 'tensor', split_axis=1, concat_axis=0, tiled...]
    unnamed x239 -> x219, local copies, waits for them, and re-layouts: 13.4 us -> 17.6 us
  transfers between devices with their start and end apart: 64 -> 64, of which waited for: 28 -> 22; matrix products, arithmetic and copies ran while one was open for 15% -> 16% of each run, Pallas kernels for 26% -> 25%
where the time goes in v5:
time: 857 us; the launch traced here: 848 us
  waiting for transfers between devices  396 us (46%)
  Pallas kernels  212 us (25%)
  other arithmetic  92.5 us (11%)
  starting transfers between devices  69.6 us (8%)
  local copies, waits for them, and re-layouts  48.5 us (6%)
  between operations  16.7 us (2%)
  matrix products  12.5 us (1%)
    all_gather x7, waiting for transfers between devices, gather_rows(): return lax.all_gather(x, 'tensor', axis=0, tiled=True)  131 us
    ppermute x41, waiting for transfers between devices, swap_bit(): return lax.ppermute(x, axis_name, [(i, i ^ 1 << bit) for i in range(size)])  117 us
    reduce_scatter x6, waiting for transfers between devices, scatter_rows(): return lax.psum_scatter(x, 'tensor', scatter_dimension=0, tiled=True)  74.9 us
    all_to_all x2, waiting for transfers between devices, per_device(): lax.all_to_all(context, 'tensor', split_axis=0, concat_axis=1, tiled=True)  52.9 us
    pallas_call x2, Pallas kernels, glu_backward(): pl.pallas_call(glu_backward_kernel, grid=(length // ROW_TILE,), in_specs=...  45.4 us
    ppermute x41, starting transfers between devices, swap_bit(): return lax.ppermute(x, axis_name, [(i, i ^ 1 << bit) for i in range(size)])  42.7 us
    pallas_call x2, Pallas kernels, glu_forward(): pl.pallas_call(glu_forward_kernel, grid=(length // ROW_TILE,), in_specs=[...  33.9 us
    pallas_call x2, Pallas kernels, attend_backward(): pl.pallas_call(attend_backward_kernel, grid=(length // ROW_TILE,), in_spe...  31.7 us
  transfers between devices with their start and end apart: 64, of which 22 were waited for; matrix products, arithmetic and copies ran while one was open for 16% of the time, Pallas kernels for 25%

profile of v5, /device:TPU:0, one launch (start us, length us, event | category | flops | bytes accessed | tf_op | source)
XLA Modules:
  0.0 848.0 jit_solution(13068214872070386921)
XLA Ops:
  12.2 29.8 %all-gather.10.cloned.1.call-done = bf16[2048,512]{1,0:T(8,128)(2,1)} async-done(((bf16[256,512]{1,0:T(8,128)(2,1)}), bf16[2048,512]{1,0:T(8,128)(2,1)}) %all-gather.10.cloned.1.call-update) | async-done | bytes 2097168 | tf_op jit(solution)/shard_map/all_gather | solution.py:718
  44.9 5.0 fusion.29
  51.3 6.1 collective-permute-done
  59.2 5.5 collective-permute-done.2
  68.7 17.4 %collective-permute-done.1 = bf16[2048,256]{1,0:T(8,128)(2,1)S(1)} collective-permute-done((bf16[2048,256]{1,0:T(8,128)(2,1)S(1)}, bf16[2048,256]{1,0:T(8,128)(2,1)S(1)}, u32[]{:S(2)}, u32[]{:S(2)}) %collective-permute-start.1) | collective-permute-done | bytes 1048608 | tf_op jit(solution)/shard_map/ppermute | solution.py:493
  88.6 2.7 pad_maximum_fusion.1
  91.5 13.7 %attend_forward.2 = (bf16[6,1024,128]{2,1,0:T(8,128)(2,1)}, bf16[1024,256]{1,0:T(8,128)(2,1)}, f32[2,2,1,512]{3,2,1,0:T(1,128)}) custom-call(bf16[1024,2048]{1,0:T(8,128)(2,1)} %bitcast.207, bf16[3,2048,256]{2,1,0:T(8,128)(2,1)} %bitcast.211, f32[3,1,256]{2,1,0:T(1,128)} %broadcast_in_dim.8.b_ref, f32[1024,128]{1,0:T(8,128)} %get-tuple-element.337.cos_ref, ...), custom_call_target="tpu_custom_call" | custom-call | flops 199999995904 | bytes 1024 | tf_op jit(solution)/shard_map/attend_forward/pallas_call | solution.py:95
  105.2 4.4 all-to-all-start
  110.6 2.9 pad_maximum_fusion.14
  114.0 25.4 %all-to-all-done = bf16[8,128,256]{2,1,0:T(8,128)(2,1)} async-done(((bf16[8,128,256]{2,1,0:T(8,128)(2,1)}), bf16[8,128,256]{2,1,0:T(8,128)(2,1)}, u32[]{:S(2)}, u32[]{:S(2)}) %all-to-all-start) | async-done | bytes 524320 | tf_op jit(solution)/shard_map/all_to_all | solution.py:788
  140.6 4.0 broadcast_select_fusion.1
  150.7 13.7 %attend_forward.3 = (bf16[6,1024,128]{2,1,0:T(8,128)(2,1)}, bf16[1024,256]{1,0:T(8,128)(2,1)}, f32[2,2,1,512]{3,2,1,0:T(1,128)}) custom-call(bf16[1024,2048]{1,0:T(8,128)(2,1)} %bitcast.209, bf16[3,2048,256]{2,1,0:T(8,128)(2,1)} %bitcast.212, f32[3,1,256]{2,1,0:T(1,128)} %broadcast_in_dim.8.b_ref, f32[1024,128]{1,0:T(8,128)} %get-tuple-element.339.cos_ref, ...), custom_call_target="tpu_custom_call" | custom-call | flops 199999995904 | bytes 1024 | tf_op jit(solution)/shard_map/attend_forward/pallas_call | solution.py:95
  164.4 3.6 all-to-all-start.1
  170.0 27.4 %all-to-all-done.1 = bf16[8,128,256]{2,1,0:T(8,128)(2,1)S(1)} async-done(((bf16[8,128,256]{2,1,0:T(8,128)(2,1)}), bf16[8,128,256]{2,1,0:T(8,128)(2,1)S(1)}, u32[]{:S(2)}, u32[]{:S(2)}) %all-to-all-start.1) | async-done | bytes 524320 | tf_op jit(solution)/shard_map/all_to_all | solution.py:788
  197.5 4.8 fusion.50
  205.3 4.2 all-gather.12.cloned.1.call-done.h_ref.refs_4_
  209.5 16.9 %glu_forward.2 = (bf16[688,1024]{1,0:T(8,128)(2,1)}, bf16[688,1024]{1,0:T(8,128)(2,1)}, bf16[688,1024]{1,0:T(8,128)(2,1)}, bf16[1024,2048]{1,0:T(8,128)(2,1)}) custom-call(s32[1]{0:T(128)} %bitcast.14.live_ref, bf16[1024,2048]{1,0:T(8,128)(2,1)} %all-gather.12.cloned.1.call-done.h_ref.refs_4_, bf16[688,2048]{1,0:T(8,128)(2,1)} %bitcast.215, ...), custom_call_target="tpu_custom_call" | custom-call | flops 199999995904 | bytes 1024 | tf_op jit(solution)/shard_map/glu_forward/pallas_call | solution.py:260
  226.4 30.9 %all-gather.14.cloned.1.call-done.h_ref.refs_5_ = bf16[1024,2048]{1,0:T(8,128)(2,1)} async-done(((bf16[128,2048]{1,0:T(8,128)(2,1)}), bf16[1024,2048]{1,0:T(8,128)(2,1)}) %all-gather.14.cloned.1.call-update) | async-done | bytes 4194320 | tf_op jit(solution)/shard_map/all_gather | solution.py:718
  257.4 17.0 %glu_forward.3 = (bf16[688,1024]{1,0:T(8,128)(2,1)}, bf16[688,1024]{1,0:T(8,128)(2,1)}, bf16[688,1024]{1,0:T(8,128)(2,1)}, bf16[1024,2048]{1,0:T(8,128)(2,1)}) custom-call(s32[1]{0:T(128)} %bitcast.14.live_ref, bf16[1024,2048]{1,0:T(8,128)(2,1)} %all-gather.14.cloned.1.call-done.h_ref.refs_5_, bf16[688,2048]{1,0:T(8,128)(2,1)} %bitcast.216, ...), custom_call_target="tpu_custom_call" | custom-call | flops 199999995904 | bytes 1024 | tf_op jit(solution)/shard_map/glu_forward/pallas_call | solution.py:260
  274.5 34.3 %reduce-scatter.7.cloned.1.call-done = bf16[128,2048]{1,0:T(8,128)(2,1)} async-done(((bf16[1024,2048]{1,0:T(8,128)(2,1)}), bf16[128,2048]{1,0:T(8,128)(2,1)}) %reduce-scatter.7.cloned.1.call-update) | async-done | bytes 524304 | tf_op jit(solution)/shard_map/reduce_scatter | solution.py:721
  319.3 40.6 %reduce-scatter.9.cloned.1.call-done = bf16[128,2048]{1,0:T(8,128)(2,1)} async-done(((bf16[1024,2048]{1,0:T(8,128)(2,1)}), bf16[128,2048]{1,0:T(8,128)(2,1)}) %reduce-scatter.9.cloned.1.call-update) | async-done | bytes 524304 | tf_op jit(solution)/shard_map/reduce_scatter | solution.py:721
  366.8 40.5 %all-gather.16.cloned.1.call-done.g_ref.refs_2_ = bf16[1024,2048]{1,0:T(8,128)(2,1)} async-done(((bf16[128,2048]{1,0:T(8,128)(2,1)}), bf16[1024,2048]{1,0:T(8,128)(2,1)}) %all-gather.16.cloned.1.call-update) | async-done | bytes 4194320 | tf_op jit(solution)/shard_map/all_gather | solution.py:718
  407.4 22.6 %glu_backward.2 = (bf16[688,1024]{1,0:T(8,128)(2,1)}, bf16[688,1024]{1,0:T(8,128)(2,1)}, f32[688,1]{1,0:T(8,128)}, f32[688,1]{1,0:T(8,128)}, bf16[1024,2048]{1,0:T(8,128)(2,1)}) custom-call(s32[1]{0:T(128)} %bitcast.14.live_ref, bf16[1024,2048]{1,0:T(8,128)(2,1)} %all-gather.16.cloned.1.call-done.g_ref.refs_2_, bf16[688,2048]{1,0:T(8,128)(2,1)} %bitcast.217, ...), custom_call_target="tpu_custom_call" | custom-call | flops 199999995904 | bytes 1024 | tf_op jit(solution)/shard_map/glu_backward/pallas_call | solution.py:323
  430.3 25.2 %all-gather.18.cloned.1.call-done.refs_3_.g_ref = bf16[1024,2048]{1,0:T(8,128)(2,1)} async-done(((bf16[128,2048]{1,0:T(8,128)(2,1)}), bf16[1024,2048]{1,0:T(8,128)(2,1)}) %all-gather.18.cloned.1.call-update) | async-done | bytes 4194320 | tf_op jit(solution)/shard_map/all_gather | solution.py:718
  455.5 11.5 %weight_grad.2 = (bf16[1,688,512]{2,1,0:T(8,128)(2,1)}, bf16[1,688,512]{2,1,0:T(8,128)(2,1)}, bf16[1,688,512]{2,1,0:T(8,128)(2,1)}, bf16[1,688,512]{2,1,0:T(8,128)(2,1)}) custom-call(s32[4]{0:T(128)} %pad_add_fusion.blocks_ref, bf16[688,1024]{1,0:T(8,128)(2,1)} %get-tuple-element.142.refs_0_, bf16[688,1024]{1,0:T(8,128)(2,1)} %get-tuple-element.143.refs_1_, ...), custom_call_target="tpu_custom_call" | custom-call | flops 199999995904 | bytes 1024 | tf_op jit(solution)/shard_map/weight_grad/pallas_call | solution.py:362
  469.9 22.8 %glu_backward.3 = (bf16[688,1024]{1,0:T(8,128)(2,1)}, bf16[688,1024]{1,0:T(8,128)(2,1)}, f32[688,1]{1,0:T(8,128)}, f32[688,1]{1,0:T(8,128)}, bf16[1024,2048]{1,0:T(8,128)(2,1)}) custom-call(s32[1]{0:T(128)} %bitcast.14.live_ref, bf16[1024,2048]{1,0:T(8,128)(2,1)} %all-gather.18.cloned.1.call-done.refs_3_.g_ref, bf16[688,2048]{1,0:T(8,128)(2,1)} %bitcast.218, ...), custom_call_target="tpu_custom_call" | custom-call | flops 199999995904 | bytes 1024 | tf_op jit(solution)/shard_map/glu_backward/pallas_call | solution.py:323
  501.4 19.3 %weight_grad.3 = (bf16[2,688,512]{2,1,0:T(8,128)(2,1)}, bf16[2,688,512]{2,1,0:T(8,128)(2,1)}, bf16[2,688,512]{2,1,0:T(8,128)(2,1)}, bf16[2,688,512]{2,1,0:T(8,128)(2,1)}) custom-call(s32[4]{0:T(128)} %pad_add_fusion.blocks_ref, bf16[688,1024]{1,0:T(8,128)(2,1)} %get-tuple-element.154.refs_0_, bf16[688,1024]{1,0:T(8,128)(2,1)} %get-tuple-element.155.refs_1_, ...), custom_call_target="tpu_custom_call" | custom-call | flops 199999995904 | bytes 1024 | tf_op jit(solution)/shard_map/weight_grad/pallas_call | solution.py:362
  531.7 3.1 convolution_convert_fusion.1
  534.7 27.0 %collective-permute-done.9 = bf16[688,256]{1,0:T(8,128)(2,1)} collective-permute-done((bf16[688,256]{1,0:T(8,128)(2,1)S(1)}, bf16[688,256]{1,0:T(8,128)(2,1)}, u32[]{:S(2)}, u32[]{:S(2)}) %collective-permute-start.9) | collective-permute-done | bytes 352288 | tf_op jit(solution)/shard_map/ppermute | solution.py:493
  562.6 4.5 all-to-all-start.2
  587.2 3.1 convolution_convert_fusion
  591.1 5.1 all-to-all-start.3
  596.2 15.8 %attend_backward.2 = (bf16[3,1024,256]{2,1,0:T(8,128)(2,1)}, f32[3,1,256]{2,1,0:T(1,128)}, bf16[1024,2048]{1,0:T(8,128)(2,1)}) custom-call(bf16[6,1024,128]{2,1,0:T(8,128)(2,1)} %get-tuple-element.136.qkv_ref, bf16[1024,256]{1,0:T(8,128)(2,1)} %bitcast.42.grad_ref, f32[2,2,1,512]{3,2,1,0:T(1,128)} %get-tuple-element.172.lse_ref, s32[2,1,512]{2,1,0:T(1,128)} %bitcast.195, ...), custom_call_target="tpu_custom_call" | custom-call | flops 24999999488 | bytes 1024 | tf_op jit(solution)/shard_map/attend_backward/pallas_call | solution.py:200
  620.8 15.9 %attend_backward.3 = (bf16[3,1024,256]{2,1,0:T(8,128)(2,1)}, f32[3,1,256]{2,1,0:T(1,128)}, bf16[1024,2048]{1,0:T(8,128)(2,1)}) custom-call(bf16[6,1024,128]{2,1,0:T(8,128)(2,1)} %get-tuple-element.174.qkv_ref, bf16[1024,256]{1,0:T(8,128)(2,1)} %bitcast.45.grad_ref, f32[2,2,1,512]{3,2,1,0:T(1,128)} %get-tuple-element.181.lse_ref, s32[2,1,512]{2,1,0:T(1,128)} %bitcast.191, ...), custom_call_target="tpu_custom_call" | custom-call | flops 24999999488 | bytes 1024 | tf_op jit(solution)/shard_map/attend_backward/pallas_call | solution.py:200
  643.2 10.6 %row_grad.1 = (bf16[1024,2048]{1,0:T(8,128)(2,1)}, bf16[1024,2048]{1,0:T(8,128)(2,1)}) custom-call(s32[2]{0:T(128)} %pad_add_fusion.2.sides_ref, bf16[256,2048]{1,0:T(8,128)(2,1)} %pad_maximum_fusion.8.left_ref, bf16[256,2048]{1,0:T(8,128)(2,1)} %pad_maximum_fusion.9.right_ref), custom_call_target="tpu_custom_call" | custom-call | flops 1024 | bytes 1024 | tf_op jit(solution)/shard_map/row_grad/pallas_call | solution.py:428
  653.8 12.8 %slab_grad.1 = (bf16[3,512,256]{2,1,0:T(8,128)(2,1)}, bf16[3,512,256]{2,1,0:T(8,128)(2,1)}, bf16[3,512,256]{2,1,0:T(8,128)(2,1)}, bf16[3,512,256]{2,1,0:T(8,128)(2,1)}) custom-call(s32[4]{0:T(128)} %pad_add_fusion.1.blocks_ref.sources_ref, bf16[1024,2048]{1,0:T(8,128)(2,1)} %bitcast.208, bf16[1024,2048]{1,0:T(8,128)(2,1)} %bitcast.210, ...), custom_call_target="tpu_custom_call" | custom-call | flops 199999995904 | bytes 1024 | tf_op jit(solution)/shard_map/slab_grad/pallas_call | solution.py:397
  671.4 5.4 add_convert_fusion
  683.0 8.3 assemble.3
  692.8 17.8 %collective-permute-done.21 = bf16[3,512,256]{2,1,0:T(8,128)(2,1)} collective-permute-done((bf16[3,512,256]{2,1,0:T(8,128)(2,1)}, bf16[3,512,256]{2,1,0:T(8,128)(2,1)}, u32[]{:S(2)}, u32[]{:S(2)}) %collective-permute-start.21) | collective-permute-done | bytes 786464 | tf_op jit(solution)/shard_map/ppermute | solution.py:597
  710.6 2.9 add_convert_fusion.5.refs_0_
  716.4 15.7 %collective-permute-done.29 = bf16[1024,512]{1,0:T(8,128)(2,1)} collective-permute-done((bf16[1024,512]{1,0:T(8,128)(2,1)}, bf16[1024,512]{1,0:T(8,128)(2,1)}, u32[]{:S(2)}, u32[]{:S(2)}) %collective-permute-start.29) | collective-permute-done | bytes 1048608 | tf_op jit(solution)/shard_map/ppermute | solution.py:493
  741.4 5.4 assemble.4
  746.8 28.9 %collective-permute-done.33 = bf16[1024,256]{1,0:T(8,128)(2,1)} collective-permute-done((bf16[1024,256]{1,0:T(8,128)(2,1)}, bf16[1024,256]{1,0:T(8,128)(2,1)}, u32[]{:S(2)}, u32[]{:S(2)}) %collective-permute-start.33) | collective-permute-done | bytes 524320 | tf_op jit(solution)/shard_map/ppermute | solution.py:493
  779.8 2.5 collective-permute-start.38
  783.0 10.5 %slice_bitcast_fusion = (f32[2048,688]{0,1:T(8,128)}, f32[2048,688]{0,1:T(8,128)}) fusion(f32[2,688,2048]{2,1,0:T(8,128)} %assemble.3), kind=kLoop, calls=%fused_computation.2 | loop fusion | bytes 22544384 | tf_op jit(solution)/shard_map/transpose | solution.py:955
  795.6 10.8 %collective-permute-done.34 = f32[6,2048]{1,0:T(8,128)S(1)} collective-permute-done((f32[6,2048]{1,0:T(8,128)S(1)}, f32[6,2048]{1,0:T(8,128)S(1)}, u32[]{:S(2)}, u32[]{:S(2)}) %collective-permute-start.34) | collective-permute-done | bytes 49184 | tf_op jit(solution)/shard_map/ppermute | solution.py:493
  808.3 2.5 collective-permute-done.35
  819.8 5.7 assemble.5
  (480 shorter events, 164.7 us)
Async XLA Ops:
  7.2 34.8 %all-gather.10.cloned.1.call-start = ((), (), s32[]{:S(2)}) async-start(), calls=%async_computation.10 | async-start | bytes 2359296 | tf_op jit(solution)/shard_map/all_gather | solution.py:718
  9.7 81.8 %all-gather.20.cloned.1.call-start = ((), (), s32[]{:S(2)}) async-start(), calls=%async_computation.21 | async-start | bytes 4718592 | tf_op jit(solution)/shard_map/all_gather | solution.py:718
  10.8 139.9 %all-gather.22.cloned.1.call-start = ((), (), s32[]{:S(2)}) async-start(), calls=%async_computation.22 | async-start | bytes 4718592 | tf_op jit(solution)/shard_map/all_gather | solution.py:718
  57.7 28.5 %collective-permute-start.1 = (bf16[2048,256]{1,0:T(8,128)(2,1)S(1)}, bf16[2048,256]{1,0:T(8,128)(2,1)S(1)}, u32[]{:S(2)}, u32[]{:S(2)}) collective-permute-start(bf16[2048,256]{1,0:T(8,128)(2,1)S(1)} %pad_maximum_fusion.5), channel_id=1, source_target_pairs={{0,8},{8,0},{16,24},{24,16},{1,9},{9,1},{17,25},{25,17},{2,10},{10... | collective-permute-start | bytes 3145736 | tf_op jit(solution)/shard_map/ppermute | solution.py:493
  64.9 23.3 %collective-permute-start.3 = (bf16[2048,256]{1,0:T(8,128)(2,1)S(1)}, bf16[2048,256]{1,0:T(8,128)(2,1)S(1)}, u32[]{:S(2)}, u32[]{:S(2)}) collective-permute-start(bf16[2048,256]{1,0:T(8,128)(2,1)S(1)} %pad_maximum_fusion.6), channel_id=1, source_target_pairs={{0,16},{8,24},{16,0},{24,8},{1,17},{9,25},{17,1},{25,9},{2,18},{10... | collective-permute-start | bytes 3145736 | tf_op jit(solution)/shard_map/ppermute | solution.py:493
  91.4 49.2 %collective-permute-start.4 = (bf16[2048,1024]{1,0:T(8,128)(2,1)}, bf16[2048,1024]{1,0:T(8,128)(2,1)}, u32[]{:S(2)}, u32[]{:S(2)}) collective-permute-start(bf16[2048,1024]{1,0:T(8,128)(2,1)} %pad_maximum_fusion.1), channel_id=1, source_target_pairs={{0,1},{1,0},{2,3},{3,2},{4,5},{5,4},{6,7},{7,6},{8,9},{9,8},{10,11... | collective-permute-start | bytes 12582920 | tf_op jit(solution)/shard_map/ppermute | solution.py:493
  105.2 34.2 %all-to-all-start = ((bf16[8,128,256]{2,1,0:T(8,128)(2,1)}), bf16[8,128,256]{2,1,0:T(8,128)(2,1)}, u32[]{:S(2)}, u32[]{:S(2)}) async-start(bf16[8,128,256]{2,1,0:T(8,128)(2,1)} %bitcast.174), calls=%async_computation | async-start | bytes 1048576 | tf_op jit(solution)/shard_map/all_to_all | solution.py:788
  109.6 99.8 %all-gather.12.cloned.1.call-start = ((), (), s32[]{:S(2)}) async-start(), calls=%async_computation.11 | async-start | bytes 4718592 | tf_op jit(solution)/shard_map/all_gather | solution.py:718
  164.4 32.9 %all-to-all-start.1 = ((bf16[8,128,256]{2,1,0:T(8,128)(2,1)}), bf16[8,128,256]{2,1,0:T(8,128)(2,1)S(1)}, u32[]{:S(2)}, u32[]{:S(2)}) async-start(bf16[8,128,256]{2,1,0:T(8,128)(2,1)} %bitcast.175), calls=%async_computation.1 | async-start | bytes 1048576 | tf_op jit(solution)/shard_map/all_to_all | solution.py:788
  168.1 89.3 %all-gather.14.cloned.1.call-start = ((), (), s32[]{:S(2)}) async-start(), calls=%async_computation.13 | async-start | bytes 4718592 | tf_op jit(solution)/shard_map/all_gather | solution.py:718
  204.9 104.0 %reduce-scatter.7.cloned.1.call-start = ((), (), s32[]{:S(2)}) async-start(), calls=%async_computation.12 | async-start | bytes 4718592 | tf_op jit(solution)/shard_map/reduce_scatter | solution.py:721
  226.4 133.5 %reduce-scatter.9.cloned.1.call-start = ((), (), s32[]{:S(2)}) async-start(), calls=%async_computation.14 | async-start | bytes 4718592 | tf_op jit(solution)/shard_map/reduce_scatter | solution.py:721
  274.5 132.9 %all-gather.16.cloned.1.call-start = ((), (), s32[]{:S(2)}) async-start(), calls=%async_computation.15 | async-start | bytes 4718592 | tf_op jit(solution)/shard_map/all_gather | solution.py:718
  313.7 141.7 %all-gather.18.cloned.1.call-start = ((), (), s32[]{:S(2)}) async-start(), calls=%async_computation.17 | async-start | bytes 4718592 | tf_op jit(solution)/shard_map/all_gather | solution.py:718
  365.7 161.4 %reduce-scatter.11.cloned.1.call-start = ((), (), s32[]{:S(2)}) async-start(), calls=%async_computation.16 | async-start | bytes 4718592 | tf_op jit(solution)/shard_map/reduce_scatter | solution.py:721
  430.1 151.9 %reduce-scatter.13.cloned.1.call-start = ((), (), s32[]{:S(2)}) async-start(), calls=%async_computation.18 | async-start | bytes 4718592 | tf_op jit(solution)/shard_map/reduce_scatter | solution.py:721
  467.0 27.9 %collective-permute-start.5 = (bf16[688,512]{1,0:T(8,128)(2,1)}, bf16[688,512]{1,0:T(8,128)(2,1)}, u32[]{:S(2)}, u32[]{:S(2)}) collective-permute-start(bf16[688,512]{1,0:T(8,128)(2,1)} %bitcast.224), channel_id=1, source_target_pairs={{0,8},{8,0},{16,24},{24,16},{1,9},{9,1},{17,25},{25,17},{2,10},{10... | collective-permute-start | bytes 2113544 | tf_op jit(solution)/shard_map/ppermute | solution.py:493
  468.4 26.4 %collective-permute-start.6 = (bf16[688,512]{1,0:T(8,128)(2,1)}, bf16[688,512]{1,0:T(8,128)(2,1)}, u32[]{:S(2)}, u32[]{:S(2)}) collective-permute-start(bf16[688,512]{1,0:T(8,128)(2,1)} %bitcast.223), channel_id=1, source_target_pairs={{0,16},{8,24},{16,0},{24,8},{1,17},{9,25},{17,1},{25,9},{2,18},{10... | collective-permute-start | bytes 2113544 | tf_op jit(solution)/shard_map/ppermute | solution.py:493
  500.2 23.4 %collective-permute-start.7 = (bf16[688,256]{1,0:T(8,128)(2,1)}, bf16[688,256]{1,0:T(8,128)(2,1)}, u32[]{:S(2)}, u32[]{:S(2)}) collective-permute-start(bf16[688,256]{1,0:T(8,128)(2,1)} %constant_dynamic-slice_fusion.8), channel_id=1, source_target_pairs={{0,16},{8,24},{16,0},{24,8},{1,17},{9,25},{17,1},{25,9},{2,18},{10... | collective-permute-start | bytes 1056776 | tf_op jit(solution)/shard_map/ppermute | solution.py:493
  500.8 22.9 %collective-permute-start.8 = (bf16[688,256]{1,0:T(8,128)(2,1)}, bf16[688,256]{1,0:T(8,128)(2,1)}, u32[]{:S(2)}, u32[]{:S(2)}) collective-permute-start(bf16[688,256]{1,0:T(8,128)(2,1)} %constant_dynamic-slice_fusion.7), channel_id=1, source_target_pairs={{0,8},{8,0},{16,24},{24,16},{1,9},{9,1},{17,25},{25,17},{2,10},{10... | collective-permute-start | bytes 1056776 | tf_op jit(solution)/shard_map/ppermute | solution.py:493
  520.7 52.6 %collective-permute-start.11 = (bf16[2,688,512]{2,1,0:T(8,128)(2,1)}, bf16[2,688,512]{2,1,0:T(8,128)(2,1)}, u32[]{:S(2)}, u32[]{:S(2)}) collective-permute-start(bf16[2,688,512]{2,1,0:T(8,128)(2,1)} %get-tuple-element.158), channel_id=1, source_target_pairs={{0,8},{8,0},{16,24},{24,16},{1,9},{9,1},{17,25},{25,17},{2,10},{10... | collective-permute-start | bytes 4227080 | tf_op jit(solution)/shard_map/ppermute | solution.py:493
  522.2 51.1 %collective-permute-start.12 = (bf16[2,688,512]{2,1,0:T(8,128)(2,1)}, bf16[2,688,512]{2,1,0:T(8,128)(2,1)}, u32[]{:S(2)}, u32[]{:S(2)}) collective-permute-start(bf16[2,688,512]{2,1,0:T(8,128)(2,1)} %get-tuple-element.159), channel_id=1, source_target_pairs={{0,16},{8,24},{16,0},{24,8},{1,17},{9,25},{17,1},{25,9},{2,18},{10... | collective-permute-start | bytes 4227080 | tf_op jit(solution)/shard_map/ppermute | solution.py:493
  524.8 37.0 %collective-permute-start.9 = (bf16[688,256]{1,0:T(8,128)(2,1)S(1)}, bf16[688,256]{1,0:T(8,128)(2,1)}, u32[]{:S(2)}, u32[]{:S(2)}) collective-permute-start(bf16[688,256]{1,0:T(8,128)(2,1)S(1)} %add_convert_fusion.14), channel_id=1, source_target_pairs={{0,16},{8,24},{16,0},{24,8},{1,17},{9,25},{17,1},{25,9},{2,18},{10... | collective-permute-start | bytes 1056776 | tf_op jit(solution)/shard_map/ppermute | solution.py:493
  526.4 35.3 %collective-permute-start.10 = (bf16[688,256]{1,0:T(8,128)(2,1)S(1)}, bf16[688,256]{1,0:T(8,128)(2,1)}, u32[]{:S(2)}, u32[]{:S(2)}) collective-permute-start(bf16[688,256]{1,0:T(8,128)(2,1)S(1)} %add_convert_fusion.13), channel_id=1, source_target_pairs={{0,8},{8,0},{16,24},{24,16},{1,9},{9,1},{17,25},{25,17},{2,10},{10... | collective-permute-start | bytes 1056776 | tf_op jit(solution)/shard_map/ppermute | solution.py:493
  562.6 27.7 %all-to-all-start.2 = ((bf16[128,8,256]{2,0,1:T(8,128)(2,1)}), bf16[128,8,256]{2,0,1:T(8,128)(2,1)}, u32[]{:S(2)}, u32[]{:S(2)}) async-start(bf16[128,8,256]{2,0,1:T(8,128)(2,1)} %bitcast.159), calls=%async_computation.5 | async-start | bytes 1048576 | tf_op jit(solution)/shard_map/all_to_all | solution.py:876
  569.3 42.7 %collective-permute-start.16 = (bf16[688,512]{1,0:T(8,128)(2,1)}, bf16[688,512]{1,0:T(8,128)(2,1)}, u32[]{:S(2)}, u32[]{:S(2)}) collective-permute-start(bf16[688,512]{1,0:T(8,128)(2,1)} %pad_maximum_fusion.11.refs_1_), channel_id=1, source_target_pairs={{0,16},{8,24},{16,0},{24,8},{1,17},{9,25},{17,1},{25,9},{2,18},{10... | collective-permute-start | bytes 2113544 | tf_op jit(solution)/shard_map/ppermute | solution.py:493
  572.7 39.3 %collective-permute-start.15 = (bf16[688,512]{1,0:T(8,128)(2,1)}, bf16[688,512]{1,0:T(8,128)(2,1)}, u32[]{:S(2)}, u32[]{:S(2)}) collective-permute-start(bf16[688,512]{1,0:T(8,128)(2,1)} %pad_maximum_fusion.10.refs_0_), channel_id=1, source_target_pairs={{0,8},{8,0},{16,24},{24,16},{1,9},{9,1},{17,25},{25,17},{2,10},{10... | collective-permute-start | bytes 2113544 | tf_op jit(solution)/shard_map/ppermute | solution.py:493
  576.0 35.9 %collective-permute-start.13 = (bf16[2,688,256]{2,1,0:T(8,128)(2,1)}, bf16[2,688,256]{2,1,0:T(8,128)(2,1)}, u32[]{:S(2)}, u32[]{:S(2)}) collective-permute-start(bf16[2,688,256]{2,1,0:T(8,128)(2,1)} %constant_dynamic-slice_fusion.6), channel_id=1, source_target_pairs={{0,16},{8,24},{16,0},{24,8},{1,17},{9,25},{17,1},{25,9},{2,18},{10... | collective-permute-start | bytes 2113544 | tf_op jit(solution)/shard_map/ppermute | solution.py:493
  580.5 31.5 %collective-permute-start.14 = (bf16[2,688,256]{2,1,0:T(8,128)(2,1)}, bf16[2,688,256]{2,1,0:T(8,128)(2,1)}, u32[]{:S(2)}, u32[]{:S(2)}) collective-permute-start(bf16[2,688,256]{2,1,0:T(8,128)(2,1)} %constant_dynamic-slice_fusion.5), channel_id=1, source_target_pairs={{0,8},{8,0},{16,24},{24,16},{1,9},{9,1},{17,25},{25,17},{2,10},{10... | collective-permute-start | bytes 2113544 | tf_op jit(solution)/shard_map/ppermute | solution.py:493
  591.1 29.7 %all-to-all-start.3 = ((bf16[128,8,256]{2,0,1:T(8,128)(2,1)}), bf16[128,8,256]{2,0,1:T(8,128)(2,1)}, u32[]{:S(2)}, u32[]{:S(2)}) async-start(bf16[128,8,256]{2,0,1:T(8,128)(2,1)} %bitcast.158), calls=%async_computation.8 | async-start | bytes 1048576 | tf_op jit(solution)/shard_map/all_to_all | solution.py:876
  596.2 240.9 %reduce-scatter.15.cloned.1.call-start = ((), (), s32[]{:S(2)}) async-start(), calls=%async_computation.19 | async-start | bytes 4718592 | tf_op jit(solution)/shard_map/reduce_scatter | solution.py:721
  612.0 226.2 %reduce-scatter.17.cloned.1.call-start = ((), (), s32[]{:S(2)}) async-start(), calls=%async_computation.20 | async-start | bytes 4718592 | tf_op jit(solution)/shard_map/reduce_scatter | solution.py:721
  613.5 23.2 %collective-permute-start.17 = (bf16[2,688,256]{2,1,0:T(8,128)(2,1)S(1)}, bf16[2,688,256]{2,1,0:T(8,128)(2,1)S(1)}, u32[]{:S(2)}, u32[]{:S(2)}) collective-permute-start(bf16[2,688,256]{2,1,0:T(8,128)(2,1)S(1)} %add_convert_fusion.7), channel_id=1, source_target_pairs={{0,16},{8,24},{16,0},{24,8},{1,17},{9,25},{17,1},{25,9},{2,18},{10... | collective-permute-start | bytes 2113544 | tf_op jit(solution)/shard_map/ppermute | solution.py:493
  640.1 40.7 %collective-permute-start.24 = (bf16[2,688,512]{2,1,0:T(8,128)(2,1)}, bf16[2,688,512]{2,1,0:T(8,128)(2,1)}, u32[]{:S(2)}, u32[]{:S(2)}) collective-permute-start(bf16[2,688,512]{2,1,0:T(8,128)(2,1)} %pad_maximum_fusion.4.refs_1_), channel_id=1, source_target_pairs={{0,16},{8,24},{16,0},{24,8},{1,17},{9,25},{17,1},{25,9},{2,18},{10... | collective-permute-start | bytes 4227080 | tf_op jit(solution)/shard_map/ppermute | solution.py:493
  641.8 39.7 %collective-permute-start.23 = (bf16[2,688,512]{2,1,0:T(8,128)(2,1)}, bf16[2,688,512]{2,1,0:T(8,128)(2,1)}, u32[]{:S(2)}, u32[]{:S(2)}) collective-permute-start(bf16[2,688,512]{2,1,0:T(8,128)(2,1)} %pad_maximum_fusion.3.refs_0_), channel_id=1, source_target_pairs={{0,8},{8,0},{16,24},{24,16},{1,9},{9,1},{17,25},{25,17},{2,10},{10... | collective-permute-start | bytes 4227080 | tf_op jit(solution)/shard_map/ppermute | solution.py:493
  667.8 24.9 %collective-permute-start.19 = (bf16[3,512,256]{2,1,0:T(8,128)(2,1)}, bf16[3,512,256]{2,1,0:T(8,128)(2,1)}, u32[]{:S(2)}, u32[]{:S(2)}) collective-permute-start(bf16[3,512,256]{2,1,0:T(8,128)(2,1)} %get-tuple-element.191), channel_id=1, source_target_pairs={{0,8},{8,0},{16,24},{24,16},{1,9},{9,1},{17,25},{25,17},{2,10},{10... | collective-permute-start | bytes 2359304 | tf_op jit(solution)/shard_map/ppermute | solution.py:597
  668.4 24.3 %collective-permute-start.20 = (bf16[3,512,256]{2,1,0:T(8,128)(2,1)}, bf16[3,512,256]{2,1,0:T(8,128)(2,1)}, u32[]{:S(2)}, u32[]{:S(2)}) collective-permute-start(bf16[3,512,256]{2,1,0:T(8,128)(2,1)} %get-tuple-element.192), channel_id=1, source_target_pairs={{0,16},{8,24},{16,0},{24,8},{1,17},{9,25},{17,1},{25,9},{2,18},{10... | collective-permute-start | bytes 2359304 | tf_op jit(solution)/shard_map/ppermute | solution.py:597
  670.0 40.6 %collective-permute-start.21 = (bf16[3,512,256]{2,1,0:T(8,128)(2,1)}, bf16[3,512,256]{2,1,0:T(8,128)(2,1)}, u32[]{:S(2)}, u32[]{:S(2)}) collective-permute-start(bf16[3,512,256]{2,1,0:T(8,128)(2,1)} %get-tuple-element.193), channel_id=1, source_target_pairs={{0,24},{8,16},{16,8},{24,0},{1,25},{9,17},{17,9},{25,1},{2,26},{10... | collective-permute-start | bytes 2359304 | tf_op jit(solution)/shard_map/ppermute | solution.py:597
  680.8 51.3 %collective-permute-start.29 = (bf16[1024,512]{1,0:T(8,128)(2,1)}, bf16[1024,512]{1,0:T(8,128)(2,1)}, u32[]{:S(2)}, u32[]{:S(2)}) collective-permute-start(bf16[1024,512]{1,0:T(8,128)(2,1)} %constant_dynamic-slice_fusion.4), channel_id=1, source_target_pairs={{0,8},{8,0},{16,24},{24,16},{1,9},{9,1},{17,25},{25,17},{2,10},{10... | collective-permute-start | bytes 3145736 | tf_op jit(solution)/shard_map/ppermute | solution.py:493
  681.4 52.1 %collective-permute-start.30 = (bf16[1024,512]{1,0:T(8,128)(2,1)}, bf16[1024,512]{1,0:T(8,128)(2,1)}, u32[]{:S(2)}, u32[]{:S(2)}) collective-permute-start(bf16[1024,512]{1,0:T(8,128)(2,1)} %constant_dynamic-slice_fusion.3), channel_id=1, source_target_pairs={{0,16},{8,24},{16,0},{24,8},{1,17},{9,25},{17,1},{25,9},{2,18},{10... | collective-permute-start | bytes 3145736 | tf_op jit(solution)/shard_map/ppermute | solution.py:493
  692.8 46.5 %collective-permute-start.28 = (f32[6,2048]{1,0:T(8,128)S(1)}, f32[6,2048]{1,0:T(8,128)S(1)}, u32[]{:S(2)}, u32[]{:S(2)}) collective-permute-start(f32[6,2048]{1,0:T(8,128)S(1)} %copy-done.67), channel_id=1, source_target_pairs={{0,1},{1,0},{2,3},{3,2},{4,5},{5,4},{6,7},{7,6},{8,9},{9,8},{10,11... | collective-permute-start | bytes 147464 | tf_op jit(solution)/shard_map/ppermute | solution.py:493
  713.5 80.0 %collective-permute-start.27 = (bf16[3,512,256]{2,1,0:T(8,128)(2,1)}, bf16[3,512,256]{2,1,0:T(8,128)(2,1)}, u32[]{:S(2)}, u32[]{:S(2)}) collective-permute-start(bf16[3,512,256]{2,1,0:T(8,128)(2,1)} %add_convert_fusion.5.refs_0_), channel_id=1, source_target_pairs={{0,24},{8,16},{16,8},{24,0},{1,25},{9,17},{17,9},{25,1},{2,26},{10... | collective-permute-start | bytes 2359304 | tf_op jit(solution)/shard_map/ppermute | solution.py:597
  714.9 80.1 %collective-permute-start.26 = (bf16[3,512,256]{2,1,0:T(8,128)(2,1)}, bf16[3,512,256]{2,1,0:T(8,128)(2,1)}, u32[]{:S(2)}, u32[]{:S(2)}) collective-permute-start(bf16[3,512,256]{2,1,0:T(8,128)(2,1)} %add_convert_fusion.5.refs_0_), channel_id=1, source_target_pairs={{0,16},{8,24},{16,0},{24,8},{1,17},{9,25},{17,1},{25,9},{2,18},{10... | collective-permute-start | bytes 2359304 | tf_op jit(solution)/shard_map/ppermute | solution.py:597
  732.1 63.5 %collective-permute-start.25 = (bf16[3,512,256]{2,1,0:T(8,128)(2,1)}, bf16[3,512,256]{2,1,0:T(8,128)(2,1)}, u32[]{:S(2)}, u32[]{:S(2)}) collective-permute-start(bf16[3,512,256]{2,1,0:T(8,128)(2,1)} %add_convert_fusion.5.refs_0_), channel_id=1, source_target_pairs={{0,8},{8,0},{16,24},{24,16},{1,9},{9,1},{17,25},{25,17},{2,10},{10... | collective-permute-start | bytes 2359304 | tf_op jit(solution)/shard_map/ppermute | solution.py:597
  738.7 37.0 %collective-permute-start.33 = (bf16[1024,256]{1,0:T(8,128)(2,1)}, bf16[1024,256]{1,0:T(8,128)(2,1)}, u32[]{:S(2)}, u32[]{:S(2)}) collective-permute-start(bf16[1024,256]{1,0:T(8,128)(2,1)} %constant_dynamic-slice_fusion.1), channel_id=1, source_target_pairs={{0,8},{8,0},{16,24},{24,16},{1,9},{9,1},{17,25},{25,17},{2,10},{10... | collective-permute-start | bytes 1572872 | tf_op jit(solution)/shard_map/ppermute | solution.py:493
  739.3 38.1 %collective-permute-start.32 = (bf16[1024,256]{1,0:T(8,128)(2,1)}, bf16[1024,256]{1,0:T(8,128)(2,1)}, u32[]{:S(2)}, u32[]{:S(2)}) collective-permute-start(bf16[1024,256]{1,0:T(8,128)(2,1)} %constant_dynamic-slice_fusion.2), channel_id=1, source_target_pairs={{0,16},{8,24},{16,0},{24,8},{1,17},{9,25},{17,1},{25,9},{2,18},{10... | collective-permute-start | bytes 1572872 | tf_op jit(solution)/shard_map/ppermute | solution.py:493
  779.8 28.2 %collective-permute-start.38 = (bf16[512,512]{1,0:T(8,128)(2,1)S(1)}, bf16[512,512]{1,0:T(8,128)(2,1)S(1)}, u32[]{:S(2)}, u32[]{:S(2)}) collective-permute-start(bf16[512,512]{1,0:T(8,128)(2,1)S(1)} %fusion.27), channel_id=1, source_target_pairs={{0,4},{1,5},{2,6},{3,7},{4,0},{5,1},{6,2},{7,3},{8,12},{9,13},{10,... | collective-permute-start | bytes 1572872 | tf_op jit(solution)/shard_map/ppermute | solution.py:493
  782.3 24.2 %collective-permute-start.34 = (f32[6,2048]{1,0:T(8,128)S(1)}, f32[6,2048]{1,0:T(8,128)S(1)}, u32[]{:S(2)}, u32[]{:S(2)}) collective-permute-start(f32[6,2048]{1,0:T(8,128)S(1)} %add.490), channel_id=1, source_target_pairs={{0,4},{1,5},{2,6},{3,7},{4,0},{5,1},{6,2},{7,3},{8,12},{9,13},{10,... | collective-permute-start | bytes 147464 | tf_op jit(solution)/shard_map/ppermute | solution.py:493
  (125 other events, 1548.2 us)
Sparse Core Ops, SparseCore 0:
  10.2 31.7 all-gather.9
  44.2 46.6 all-gather.19
  93.1 57.0 all-gather.21
  152.2 57.1 all-gather.11
  211.5 45.8 all-gather.13
  260.1 48.7 reduce-scatter.6
  311.7 48.1 reduce-scatter.8
  362.1 45.2 all-gather.15
  409.6 45.8 all-gather.17
  458.2 48.6 reduce-scatter.10
  509.7 48.1 reduce-scatter.12
  612.2 50.4 reduce-scatter.14
  670.1 50.5 reduce-scatter.16
